TPU v7x, 512 devices: a whole 4x4x16 slice. The times are simulated.
512 devices in a mesh: outer: 16 (over x, y), tp: 32 (over z, core).
Axes of the slice: x: 4, y: 4, z: 16, core: 2. Of those that a mesh axis runs over, the one named last changes fastest.
Arguments:
- activations: bfloat16 [4096, 4096], P('outer', 'tp'), may hold values from -6 to 6
- grads_out: bfloat16 [4096, 16384], P('outer', 'tp'), may hold values from -0.375 to 0.375
- feedback: bfloat16 [65536, 16384], P('outer', 'tp'), may hold values from -12 to 12
- start_right: float32 [16384, 64], P('tp'), may hold values from -0.046875 to 0.046875
Outputs:
- decompressed: bfloat16 [4096, 16384], P('outer', 'tp')
- right_factor: float32 [16384, 64], P('tp')
All inputs are finite; a program needn't handle non-finite values.
Results may differ from a plain program's by a relative error of at most 0.001.
Values may be sent and summed in bfloat16 or wider, within the bound.
No kernel may reach another device: no remote copies, remote signals or barrier semaphores. Data moves between devices by JAX's collectives and lax.ppermute only.
A program may use at most 64 MiB of HBM per device.

v0:
```python
import jax
import jax.numpy as jnp
from jax import lax
from jax.sharding import PartitionSpec as P


def orthonormal(matrix, gram_matrix):
    factor = jnp.linalg.cholesky(gram_matrix)
    return jax.scipy.linalg.solve_triangular(factor, matrix.T, lower=True).T


def inner_first(left_side, right_side):
    return lax.dot_general(
        left_side,
        right_side,
        (((0,), (0,)), ((), ())),
        precision=lax.Precision.HIGHEST,
        preferred_element_type=jnp.float32,
    )


def per_device(activations, grads_out, feedback, start_right):
    shifted = lax.dot_general(
        lax.all_gather(activations, "tp", axis=1, tiled=True),
        grads_out,
        (((0,), (0,)), ((), ())),
        preferred_element_type=jnp.float32,
    ) + feedback.astype(jnp.float32)
    partial_left = jnp.dot(shifted, start_right, precision=lax.Precision.HIGHEST)
    left = lax.psum(partial_left, ("outer", "tp"))
    gram_matrix = jnp.dot(left.T, left, precision=lax.Precision.HIGHEST)
    basis = orthonormal(left, gram_matrix)
    right_part = inner_first(shifted, basis)
    right_factor = lax.psum(right_part, "outer")
    slab_rows = basis.shape[0] // lax.axis_size("outer")
    slab = lax.dynamic_slice_in_dim(basis, lax.axis_index("outer") * slab_rows, slab_rows, 0)
    decompressed = jnp.dot(slab, right_factor.T, precision=lax.Precision.HIGHEST).astype(
        jnp.bfloat16
    )
    return (decompressed, right_factor)


def solution(mesh):
    in_specs = (P("outer", "tp"), P("outer", "tp"), P("outer", "tp"), P("tp", None))
    out_specs = (P("outer", "tp"), P("tp", None))
    return jax.shard_map(
        per_device, mesh=mesh, in_specs=in_specs, out_specs=out_specs, check_vma=False
    )
```

profile of v0, /device:TPU:6, one launch (start us, length us, event | category | flops | bytes accessed | tf_op | source)
XLA Modules:
  0.0 713.9 jit_solution(3668332356312263636)
XLA Ops:
  7.2 0.0 copy-start
  7.2 0.0 all-gather.2.cloned.1.call-start
  7.2 0.7 all-gather.2.cloned.1.call-update
  7.9 0.0 copy-start.2
  7.9 0.0 all-reduce.3.cloned.1.call-start
  8.0 80.1 %all-gather.2.cloned.1.call-done = bf16[256,4096]{1,0:T(8,128)(2,1)} async-done(((bf16[256,128]{1,0:T(8,128)(2,1)}), bf16[256,4096]{1,0:T(8,128)(2,1)}) %all-gather.2.cloned.1.call-update) | async-done | bytes 2097168 | tf_op jit(solution)/shard_map/all_gather | solution.py:24
  88.1 0.0 copy-done
  88.1 4.1 convert_add_fusion
  92.2 0.0 copy-start.1
  92.2 3.2 copy-done.1
  95.4 0.0 copy-done.2
  95.4 9.2 %fusion.6 = f32[4096,64]{0,1:T(8,128)} fusion(f32[4096,512]{1,0:T(8,128)S(1)} %convert_add_fusion, f32[512,64]{0,1:T(8,128)S(1)} %copy-done.2), kind=kOutput, calls=%fused_computation.14 | convolution fusion | flops 1610612736 | bytes 9568256 | tf_op jit(solution)/shard_map/dot_general | solution.py:29
  104.7 0.0 all-reduce.3.cloned.1.call-update
  104.7 0.2 all-reduce.5.cloned.1.call-start
  104.9 462.5 %all-reduce.3.cloned.1.call-done = f32[4096,64]{0,1:T(8,128)} async-done(((f32[4096,64]{0,1:T(8,128)}), f32[4096,64]{0,1:T(8,128)}) %all-reduce.3.cloned.1.call-update) | async-done | bytes 1048592 | tf_op jit(solution)/shard_map/psum | solution.py:30
  567.4 2.7 fusion.7
  570.1 0.1 copy.6
  570.2 5.8 cholesky.16
  576.1 0.6 compare_reduce_fusion
  576.7 0.7 fusion.1
  577.4 4.9 custom-call.7
  582.3 2.3 fusion.2
  584.6 8.5 %fusion.8 = f32[512,64]{0,1:T(8,128)} fusion(f32[4096,512]{1,0:T(8,128)} %copy-done.1, f32[64,4096]{1,0:T(8,128)S(1)} %fusion.2), kind=kOutput, calls=%fused_computation.16 | convolution fusion | flops 1610612736 | bytes 9568256 | tf_op jit(solution)/shard_map/dot_general | solution.py:13
  593.0 0.0 all-reduce.5.cloned.1.call-update
  593.1 110.5 %all-reduce.5.cloned.1.call-done = f32[512,64]{0,1:T(8,128)} async-done(((f32[512,64]{0,1:T(8,128)}), f32[512,64]{0,1:T(8,128)}) %all-reduce.5.cloned.1.call-update) | async-done | bytes 131088 | tf_op jit(solution)/shard_map/psum | solution.py:34
  703.6 2.2 convolution_convert_fusion
  705.8 1.6 copy.9
  (2 shorter events, 0.0 us)
Async XLA Ops:
  7.2 80.9 %copy-start = (bf16[256,512]{1,0:T(8,128)(2,1)S(1)}, bf16[256,512]{1,0:T(8,128)(2,1)}, u32[]{:S(2)}) copy-start(bf16[256,512]{1,0:T(8,128)(2,1)} %param.5) | copy-start | bytes 786436
  7.2 80.9 %all-gather.2.cloned.1.call-start = ((), (), s32[]{:S(2)}) async-start(), calls=%async_computation | async-start | bytes 2162688 | tf_op jit(solution)/shard_map/all_gather | solution.py:24
  7.9 87.5 %copy-start.2 = (f32[512,64]{0,1:T(8,128)S(1)}, f32[512,64]{0,1:T(8,128)}, u32[]{:S(2)}) copy-start(f32[512,64]{0,1:T(8,128)} %param.7) | copy-start | bytes 393220
  7.9 559.5 %all-reduce.3.cloned.1.call-start = ((), (), s32[]{:S(2)}) async-start(), calls=%async_computation.1 | async-start | bytes 2097152 | tf_op jit(solution)/shard_map/psum | solution.py:30
  92.2 3.2 copy-start.1
  104.7 598.9 %all-reduce.5.cloned.1.call-start = ((), (), s32[]{:S(2)}) async-start(), calls=%async_computation.2 | async-start | bytes 262144 | tf_op jit(solution)/shard_map/psum | solution.py:34
Sparse Core Ops, SparseCore 0:
  10.1 77.9 all-gather.1
  104.8 462.5 all-reduce.2
  593.2 110.3 all-reduce.4
where the time goes:
time: 714 us
  waiting for transfers between devices  654 us (92%)
  matrix products  29 us (4%)
  between operations  13.8 us (2%)
  other arithmetic  12.1 us (2%)
    psum x1, waiting for transfers between devices, per_device(): left = lax.psum(partial_left, ('outer', 'tp'))  462 us
    psum x1, waiting for transfers between devices, per_device(): right_factor = lax.psum(right_part, 'outer')  111 us
    all_gather x1, waiting for transfers between devices, per_device(): lax.all_gather(activations, 'tp', axis=1, tiled=True)  80.1 us
  transfers between devices with their start and end apart: 3, of which 3 were waited for; matrix products, arithmetic and copies ran while one was open for 0% of the time, Pallas kernels for 0%

commit v1 on v0

v1 whole, which is shorter than its diff:
```python
import jax
import jax.numpy as jnp
from jax import lax
from jax.experimental import pallas as pl
from jax.experimental.pallas import tpu as pltpu
from jax.sharding import Mesh
from jax.sharding import PartitionSpec as P

F32 = jnp.float32
BF16 = jnp.bfloat16
LANES = 128
XYC = ("x", "y", "c")
XY = ("x", "y")
FAST = dict(preferred_element_type=F32)
FULL = dict(preferred_element_type=F32, precision=lax.Precision.HIGHEST)


def nn(a, b, kind=FAST):
    return lax.dot_general(a, b, (((1,), (0,)), ((), ())), **kind)


def nt(a, b, kind=FAST):
    return lax.dot_general(a, b, (((1,), (1,)), ((), ())), **kind)


def tn(a, b, kind=FAST):
    return lax.dot_general(a, b, (((0,), (0,)), ((), ())), **kind)


def pieces(value):
    high = value.astype(BF16)
    rest = value - high.astype(F32)
    middle = rest.astype(BF16)
    low = (rest - middle.astype(F32)).astype(BF16)
    return jnp.concatenate([high, middle, low], axis=0)


def folded(stacked):
    third = stacked.shape[0] // 3
    return stacked[:third] + (stacked[third : 2 * third] + stacked[2 * third :])


def cost(flops, count):
    return pl.CostEstimate(flops=flops, bytes_accessed=count, transcendentals=0)


def project(start_right, grads):
    width, rank = start_right.shape
    tokens = grads.shape[0]

    def kernel(start_ref, grads_ref, split_ref, out_ref):
        split = pieces(start_ref[...].T)
        split_ref[...] = split
        result = folded(nt(split, grads_ref[...]))
        half = tokens // 2
        out_ref[0] = result[:, :half]
        out_ref[1] = result[:, half:]

    return pl.pallas_call(
        kernel,
        out_shape=(
            jax.ShapeDtypeStruct((3 * rank, width), BF16),
            jax.ShapeDtypeStruct((2, rank, tokens // 2), F32),
        ),
        cost_estimate=cost(6 * rank * width * tokens, 2 * grads.size + 8 * start_right.size),
        name="project",
    )(start_right, grads)


def feedback_left(split, feedback, group):
    rows, width = feedback.shape
    rank = split.shape[0] // 3

    def kernel(split_ref, feed_ref, out_ref):
        result = folded(nt(split_ref[...], feed_ref[...]))
        for i in range(group):
            out_ref[i] = result[:, i * LANES : (i + 1) * LANES]

    return pl.pallas_call(
        kernel,
        grid=(rows // (group * LANES),),
        in_specs=[
            pl.BlockSpec(split.shape, lambda i: (0, 0)),
            pl.BlockSpec((group * LANES, width), lambda i: (i, 0)),
        ],
        out_specs=pl.BlockSpec((group, rank, LANES), lambda i: (i, 0, 0)),
        out_shape=jax.ShapeDtypeStruct((rows // LANES, rank, LANES), F32),
        cost_estimate=cost(6 * rank * width * rows, 2 * feedback.size + 4 * rows * rank),
        name="feedback_left",
    )(split, feedback)


def add_activations(place, shares, columns, partial):
    ways, rank, tokens = shares.shape

    def kernel(place_ref, shares_ref, columns_ref, partial_ref, out_ref):
        total = shares_ref[0]
        for i in range(1, ways):
            total = total + shares_ref[i]
        out_ref[0] = partial_ref[0] + folded(nn(pieces(total), columns_ref[0]))

    block = pl.BlockSpec((1, rank, LANES), lambda i, place: (2 * place[0] + i, 0, 0))
    return pl.pallas_call(
        kernel,
        grid_spec=pltpu.PrefetchScalarGridSpec(
            num_scalar_prefetch=1,
            grid=(2,),
            in_specs=[
                pl.BlockSpec(shares.shape, lambda i, place: (0, 0, 0)),
                pl.BlockSpec((1, tokens, LANES), lambda i, place: (i, 0, 0)),
                block,
            ],
            out_specs=block,
        ),
        out_shape=jax.ShapeDtypeStruct(partial.shape, F32),
        input_output_aliases={3: 0},
        cost_estimate=cost(12 * rank * tokens * LANES, 4 * shares.size),
        name="add_activations",
    )(place, shares, columns, partial)


def summed_copies(shares, copies):
    ways, rows, lanes = shares.shape

    def kernel(shares_ref, out_ref):
        total = shares_ref[0]
        for i in range(1, ways):
            total = total + shares_ref[i]
        for i in range(copies):
            out_ref[i] = total

    return pl.pallas_call(
        kernel,
        out_shape=jax.ShapeDtypeStruct((copies, rows, lanes), F32),
        cost_estimate=cost(shares.size, 4 * shares.size),
        name="summed_copies",
    )(shares)


def right_products(left, feedback, activations, grads, group, parts):
    blocks, rank, _ = left.shape
    rows, width = feedback.shape
    tokens = grads.shape[0]
    steps = blocks // group
    split_rows = rank * width // (256 * parts)
    across = width // 256

    def kernel(left_ref, feed_ref, act_ref, grads_ref, out_ref, gram_ref, right, inner, gram):
        step = pl.program_id(0)

        @pl.when(step == 0)
        def _():
            right[...] = jnp.zeros_like(right)
            inner[...] = jnp.zeros_like(inner)
            gram[...] = jnp.zeros_like(gram)

        split = pieces(jnp.concatenate([left_ref[i] for i in range(group)], axis=1))
        cols = jnp.concatenate([act_ref[i] for i in range(group)], axis=1)
        right[...] += nn(split, feed_ref[...])
        inner[...] += nt(split, cols)
        gram[...] += nt(split, split)

        @pl.when(step == steps - 1)
        def _():
            total = folded(right[...] + nn(pieces(folded(inner[...])), grads_ref[...]))
            for i in range(parts):
                down, over = i // across, i % across
                out_ref[i] = total[
                    down * split_rows : (down + 1) * split_rows, over * 256 : (over + 1) * 256
                ]
            square = folded(gram[...])
            gram_ref[...] = (
                square[:, :rank] + square[:, rank : 2 * rank] + square[:, 2 * rank :]
            )

    return pl.pallas_call(
        kernel,
        grid=(steps,),
        in_specs=[
            pl.BlockSpec((group, rank, LANES), lambda i: (i, 0, 0)),
            pl.BlockSpec((group * LANES, width), lambda i: (i, 0)),
            pl.BlockSpec((group, tokens, LANES), lambda i: (i, 0, 0)),
            pl.BlockSpec(grads.shape, lambda i: (0, 0)),
        ],
        out_specs=[
            pl.BlockSpec((parts, split_rows, 256), lambda i: (0, 0, 0)),
            pl.BlockSpec((rank, rank), lambda i: (0, 0)),
        ],
        out_shape=(
            jax.ShapeDtypeStruct((parts, split_rows, 256), F32),
            jax.ShapeDtypeStruct((rank, rank), F32),
        ),
        scratch_shapes=[
            pltpu.VMEM((3 * rank, width), F32),
            pltpu.VMEM((3 * rank, tokens), F32),
            pltpu.VMEM((3 * rank, 3 * rank), F32),
        ],
        cost_estimate=cost(
            6 * rank * rows * (width + tokens + 3 * rank), 2 * feedback.size + 2 * activations.size
        ),
        name="right_products",
    )(left, feedback, activations, grads)


def inverse_factor(gram):
    rank = gram.shape[0]

    def kernel(gram_ref, out_ref):
        row = lax.broadcasted_iota(jnp.int32, (rank, rank), 0)
        col = lax.broadcasted_iota(jnp.int32, (rank, rank), 1)
        work = jnp.concatenate([gram_ref[...], (row == col).astype(F32)], axis=1)
        index = lax.broadcasted_iota(jnp.int32, (rank, 1), 0)
        for k in range(rank):
            low = k // 8 * 8
            pivot_row = work[k : k + 1]
            scale = 1.0 / work[k : k + 1, k : k + 1]
            part = work[low:]
            factor = jnp.where(index[low:] > k, part[:, k : k + 1] * scale, 0.0)
            part = part - factor * pivot_row
            work = part if low == 0 else jnp.concatenate([work[:low], part], axis=0)
        diagonal = jnp.sum(jnp.where(row == col, work[:, :rank], 0.0), axis=1, keepdims=True)
        out_ref[...] = work[:, rank:] / jnp.sqrt(diagonal)

    return pl.pallas_call(
        kernel,
        out_shape=jax.ShapeDtypeStruct((rank, rank), F32),
        cost_estimate=cost(2 * rank * rank * rank * 8, 8 * rank * rank),
        name="inverse_factor",
    )(gram)


def finish(place, inverse, left, gathered, width, slab):
    rank = inverse.shape[0]
    parts = gathered.shape[0]
    across = width // 256
    blocks = slab // LANES

    def kernel(place_ref, inverse_ref, left_ref, gathered_ref, dec_ref, right_ref):
        across_rows = [
            jnp.concatenate([gathered_ref[i + j] for j in range(across)], axis=1)
            for i in range(0, parts, across)
        ]
        right = nn(inverse_ref[...], jnp.concatenate(across_rows, axis=0), FULL)
        right_ref[...] = right.T
        rows = jnp.concatenate([left_ref[i] for i in range(blocks)], axis=1)
        basis = nn(inverse_ref[...], rows, FULL)
        dec_ref[...] = tn(basis, right, FULL).astype(BF16)

    return pl.pallas_call(
        kernel,
        grid_spec=pltpu.PrefetchScalarGridSpec(
            num_scalar_prefetch=1,
            grid=(1,),
            in_specs=[
                pl.BlockSpec(inverse.shape, lambda i, place: (0, 0)),
                pl.BlockSpec((blocks, rank, LANES), lambda i, place: (place[0], 0, 0)),
                pl.BlockSpec(gathered.shape, lambda i, place: (0, 0, 0)),
            ],
            out_specs=[
                pl.BlockSpec((slab, width), lambda i, place: (0, 0)),
                pl.BlockSpec((width, rank), lambda i, place: (0, 0)),
            ],
        ),
        out_shape=(
            jax.ShapeDtypeStruct((slab, width), BF16),
            jax.ShapeDtypeStruct((width, rank), F32),
        ),
        cost_estimate=cost(12 * rank * slab * width, 4 * gathered.size),
        name="finish",
    )(place, inverse, left, gathered)


def exchange(value, axes):
    return lax.all_to_all(value, axes, 0, 0, tiled=True)


def index_of(axes):
    return lax.axis_index(axes).astype(jnp.int32).reshape(1)


def per_device(activations, grads_out, feedback, start_right):
    tokens, lanes = activations.shape
    width = grads_out.shape[1]
    z_far, z_near = lax.axis_size("zh"), lax.axis_size("zl")
    groups = lax.axis_size(XYC)
    outer = lax.axis_size(XY)
    gathered = lax.all_gather(activations, ("zh", "zl", "c"), axis=0)
    columns = exchange(activations.reshape(2, tokens // 2, lanes), "c")

    split, inner = project(start_right, grads_out)
    inner = summed_copies(exchange(inner, "c"), z_near)
    inner = summed_copies(exchange(inner, "zl"), z_far)
    inner = exchange(inner, "zh")

    partial = feedback_left(split, feedback, 4)
    partial = add_activations(index_of(("zh", "zl")), inner, columns, partial)

    left = summed_copies(exchange(partial, XYC), z_near)
    left = summed_copies(exchange(left, "zl"), z_far)
    left = summed_copies(exchange(left, "zh"), groups)
    left = exchange(left, XYC)

    right, gram = right_products(left, feedback, gathered, grads_out, 4, outer)
    inverse = inverse_factor(gram)
    right = summed_copies(exchange(right, XY), outer)
    right = exchange(right, XY)
    return finish(index_of(XY), inverse, left, right, width, feedback.shape[0] // outer)


def solution(mesh):
    outer, tp = mesh.shape["outer"], mesh.shape["tp"]
    across = 4 if outer == 16 else 2
    near = 4 if tp == 32 else 2
    names = ("x", "y", "zh", "zl", "c")
    shape = (outer // across, across, tp // (2 * near), near, 2)
    split_mesh = Mesh(mesh.devices.reshape(shape), names)
    z = ("zh", "zl", "c")
    return jax.shard_map(
        per_device,
        mesh=split_mesh,
        in_specs=(P(XY, z), P(XY, z), P(XY, z), P(z, None)),
        out_specs=(P(XY, z), P(z, None)),
        check_vma=False,
    )
```

time: 714 us -> 196 us (0.27)
  waiting for transfers between devices: 654 us -> 9.79 us
  blocking collectives: 0 us -> 103 us
  Pallas kernels: 0 us -> 38.7 us
  matrix products: 29 us -> 0 us
  starting transfers between devices: 0.3 us -> 22.3 us
  other arithmetic: 12.1 us -> 0 us
    psum x2 -> x0, waiting for transfers between devices: 573 us -> none  [the longest x1 462 us: per_device(): left = lax.psum(partial_left, ('outer', 'tp'))]
    all_to_all x0 -> x7, blocking collectives: none -> 103 us  [exchange(): return lax.all_to_all(value, axes, 0, 0, tiled=True)]
    all_gather x1, waiting for transfers between devices: 80.1 us -> 0.01 us  [per_device(): gathered = lax.all_gather(activations, ('zh', 'zl', 'c'), axis=0)]
    pallas_call x0 -> x12, Pallas kernels: none -> 38.7 us  [the longest x6 10.2 us: summed_copies(): pl.pallas_call(kernel, out_shape=jax.ShapeDtypeStruct((copies, rows, lane...]
    dot_general x5 -> x0, matrix products: 26.7 us -> none  [the longest x1 9.21 us: per_device(): jnp.dot(shifted, start_right, precision=lax.Precision.HIGHEST)]
    all_to_all x0 -> x3, starting transfers between devices: none -> 22.3 us  [exchange(): return lax.all_to_all(value, axes, 0, 0, tiled=True)]
    another operation x5 -> x0, other arithmetic: 12.1 us -> none  [the longest x3 6.52 us: orthonormal(): factor = jnp.linalg.cholesky(gram_matrix)]
    all_to_all x0 -> x3, waiting for transfers between devices: none -> 9.11 us  [exchange(): return lax.all_to_all(value, axes, 0, 0, tiled=True)]
  transfers between devices with their start and end apart: 3 -> 4, of which waited for: 3 -> 1; matrix products, arithmetic and copies ran while one was open for 0% -> 1% of each run, Pallas kernels for 0% -> 14%
where the time goes in v1:
time: 196 us; the launch traced here: 193 us
  blocking collectives  103 us (53%)
  Pallas kernels  38.7 us (20%)
  starting transfers between devices  22.3 us (11%)
  between operations  14 us (7%)
  waiting for transfers between devices  9.79 us (5%)
  local copies, waits for them, and re-layouts  4.77 us (2%)
    all_to_all x7, blocking collectives, exchange(): return lax.all_to_all(value, axes, 0, 0, tiled=True)  103 us
    all_to_all x3, starting transfers between devices, exchange(): return lax.all_to_all(value, axes, 0, 0, tiled=True)  22.3 us
    pallas_call x6, Pallas kernels, summed_copies(): pl.pallas_call(kernel, out_shape=jax.ShapeDtypeStruct((copies, rows, lane...  10.2 us
    all_to_all x3, waiting for transfers between devices, exchange(): return lax.all_to_all(value, axes, 0, 0, tiled=True)  9.11 us
    pallas_call x1, Pallas kernels, right_products(): pl.pallas_call(kernel, grid=(steps,), in_specs=[pl.BlockSpec((group, rank...  8.13 us
    pallas_call x1, Pallas kernels, feedback_left(): pl.pallas_call(kernel, grid=(rows // (group * LANES),), in_specs=[pl.Bloc...  7.05 us
    pallas_call x1, Pallas kernels, inverse_factor(): pl.pallas_call(kernel, out_shape=jax.ShapeDtypeStruct((rank, rank), F32),...  6.83 us
  transfers between devices with their start and end apart: 4, of which 1 were waited for; matrix products, arithmetic and copies ran while one was open for 1% of the time, Pallas kernels for 14%

profile of v1, /device:TPU:6, one launch (start us, length us, event | category | flops | bytes accessed | tf_op | source)
XLA Modules:
  0.0 192.6 jit_solution(17431707800419258892)
XLA Ops:
  7.2 0.0 all-gather.3.cloned.1.call-start
  7.2 0.7 all-gather.3.cloned.1.call-update
  7.9 1.7 copy.7.start_ref
  9.6 1.9 %project.1 = (bf16[192,512]{1,0:T(8,128)(2,1)}, f32[2,64,128]{2,1,0:T(8,128)}) custom-call(f32[512,64]{1,0:T(8,128)} %copy.7.start_ref, bf16[256,512]{1,0:T(8,128)(2,1)} %grads_ref.3), custom_call_target="tpu_custom_call" | custom-call | flops 50331648 | bytes 524288 | tf_op jit(solution)/shard_map/project/pallas_call | solution.py:59
  11.6 5.4 %all_to_all.50.shares_ref = f32[2,64,128]{2,1,0:T(8,128)} all-to-all(f32[2,64,128]{2,1,0:T(8,128)} %get-tuple-element.6), channel_id=1, replica_groups=mesh['x'=4,'y'=4,'zh'=4,'zl'=4,'c'=2] {'c'}, dimensions={0} | all-to-all | bytes 131072 | tf_op jit(solution)/shard_map/all_to_all | solution.py:274
  17.0 1.5 summed_copies.6
  18.5 12.2 %all_to_all.51.shares_ref = f32[4,64,128]{2,1,0:T(8,128)} all-to-all(f32[4,64,128]{2,1,0:T(8,128)} %summed_copies.6), channel_id=1, replica_groups=mesh['x'=4,'y'=4,'zh'=4,'zl'=4,'c'=2] {'zl'}, dimensions={0} | all-to-all | bytes 262144 | tf_op jit(solution)/shard_map/all_to_all | solution.py:274
  30.8 3.3 %all-to-all-start.3 = ((bf16[2,128,128]{2,1,0:T(8,128)(2,1)}), bf16[2,128,128]{2,1,0:T(8,128)(2,1)S(1)}, u32[]{:S(2)}, u32[]{:S(2)}) async-start(bf16[2,128,128]{2,1,0:T(8,128)(2,1)} %bitcast.5), calls=%async_computation.3 | async-start | bytes 131072 | tf_op jit(solution)/shard_map/all_to_all | solution.py:274
  34.1 1.6 summed_copies.7
  35.6 0.0 all-to-all-done.3.columns_ref
  35.6 13.3 %all-to-all-start.2 = ((f32[4,64,128]{2,1,0:T(8,128)}), f32[4,64,128]{2,1,0:T(8,128)S(1)}, u32[]{:S(2)}, u32[]{:S(2)}) async-start(f32[4,64,128]{2,1,0:T(8,128)} %summed_copies.7), calls=%async_computation.2 | async-start | bytes 262144 | tf_op jit(solution)/shard_map/all_to_all | solution.py:274
  48.9 7.1 %feedback_left.1.partial_ref = f32[32,64,128]{2,1,0:T(8,128)} custom-call(bf16[192,512]{1,0:T(8,128)(2,1)} %get-tuple-element.7.split_ref, bf16[4096,512]{1,0:T(8,128)(2,1)} %feed_ref.3), custom_call_target="tpu_custom_call" | custom-call | flops 805306368 | bytes 5242880 | tf_op jit(solution)/shard_map/feedback_left/pallas_call | solution.py:79
  56.0 9.1 %all-to-all-done.2.shares_ref = f32[4,64,128]{2,1,0:T(8,128)S(1)} async-done(((f32[4,64,128]{2,1,0:T(8,128)}), f32[4,64,128]{2,1,0:T(8,128)S(1)}, u32[]{:S(2)}, u32[]{:S(2)}) %all-to-all-start.2) | async-done | bytes 131104 | tf_op jit(solution)/shard_map/all_to_all | solution.py:274
  65.1 0.0 copy-done.2
  65.1 0.7 copy-done.1
  65.7 1.8 add_activations.1
  67.6 23.5 %all_to_all.52.shares_ref = f32[32,64,128]{2,1,0:T(8,128)} all-to-all(f32[32,64,128]{2,1,0:T(8,128)} %add_activations.1), channel_id=1, replica_groups=mesh['x'=4,'y'=4,'zh'=4,'zl'=4,'c'=2] {'x','y','c'}, dimensions={0} | all-to-all | bytes 2097152 | tf_op jit(solution)/shard_map/all_to_all | solution.py:274
  91.0 1.9 %summed_copies.8 = f32[4,64,128]{2,1,0:T(8,128)} custom-call(f32[32,64,128]{2,1,0:T(8,128)} %all_to_all.52.shares_ref), custom_call_target="tpu_custom_call" | custom-call | flops 262144 | bytes 1048576 | tf_op jit(solution)/shard_map/summed_copies/pallas_call | solution.py:132
  93.0 10.2 %all_to_all.53.shares_ref = f32[4,64,128]{2,1,0:T(8,128)} all-to-all(f32[4,64,128]{2,1,0:T(8,128)} %summed_copies.8), channel_id=1, replica_groups=mesh['x'=4,'y'=4,'zh'=4,'zl'=4,'c'=2] {'zl'}, dimensions={0} | all-to-all | bytes 262144 | tf_op jit(solution)/shard_map/all_to_all | solution.py:274
  103.2 1.6 summed_copies.9
  104.8 18.6 %all_to_all.54.shares_ref = f32[4,64,128]{2,1,0:T(8,128)} all-to-all(f32[4,64,128]{2,1,0:T(8,128)} %summed_copies.9), channel_id=1, replica_groups=mesh['x'=4,'y'=4,'zh'=4,'zl'=4,'c'=2] {'zh'}, dimensions={0} | all-to-all | bytes 262144 | tf_op jit(solution)/shard_map/all_to_all | solution.py:274
  123.4 2.0 %summed_copies.10 = f32[32,64,128]{2,1,0:T(8,128)} custom-call(f32[4,64,128]{2,1,0:T(8,128)} %all_to_all.54.shares_ref), custom_call_target="tpu_custom_call" | custom-call | flops 32768 | bytes 131072 | tf_op jit(solution)/shard_map/summed_copies/pallas_call | solution.py:132
  125.4 21.4 %all_to_all.55.left_ref = f32[32,64,128]{2,1,0:T(8,128)} all-to-all(f32[32,64,128]{2,1,0:T(8,128)} %summed_copies.10), channel_id=1, replica_groups=mesh['x'=4,'y'=4,'zh'=4,'zl'=4,'c'=2] {'x','y','c'}, dimensions={0} | all-to-all | bytes 2097152 | tf_op jit(solution)/shard_map/all_to_all | solution.py:274
  146.8 8.1 %right_products.1 = (f32[16,8,256]{2,1,0:T(8,128)}, f32[64,64]{1,0:T(8,128)}) custom-call(f32[32,64,128]{2,1,0:T(8,128)} %all_to_all.55.left_ref, bf16[4096,512]{1,0:T(8,128)(2,1)} %feed_ref.3, bf16[32,256,128]{2,1,0:T(8,128)(2,1)} %bitcast.4, bf16[256,512]{1,0:T(8,128)(2,1)} %grads_ref.3), custom_call_target="tpu_custom_call" | custom-call | flops 1509949440 | bytes 6291456 | tf_op jit(solution)/shard_map/right_products/pallas_call | solution.py:176
  155.0 11.7 %all_to_all.56.shares_ref = f32[16,8,256]{2,1,0:T(8,128)} all-to-all(f32[16,8,256]{2,1,0:T(8,128)} %get-tuple-element.9), channel_id=1, replica_groups=mesh['x'=4,'y'=4,'zh'=4,'zl'=4,'c'=2] {'x','y'}, dimensions={0} | all-to-all | bytes 262144 | tf_op jit(solution)/shard_map/all_to_all | solution.py:274
  166.6 1.6 summed_copies.11
  168.2 5.7 %all-to-all-start.9 = ((f32[16,8,256]{2,1,0:T(8,128)}), f32[16,8,256]{2,1,0:T(8,128)S(1)}, u32[]{:S(2)}, u32[]{:S(2)}) async-start(f32[16,8,256]{2,1,0:T(8,128)} %summed_copies.11), calls=%async_computation.9 | async-start | bytes 262144 | tf_op jit(solution)/shard_map/all_to_all | solution.py:274
  173.9 6.8 %inverse_factor.1.inverse_ref = f32[64,64]{1,0:T(8,128)} custom-call(f32[64,64]{1,0:T(8,128)} %get-tuple-element.8.gram_ref), custom_call_target="tpu_custom_call" | custom-call | flops 4194304 | bytes 32768 | tf_op jit(solution)/shard_map/inverse_factor/pallas_call | solution.py:224
  180.7 0.0 all-to-all-done.9.gathered_ref
  180.7 0.7 copy-done
  181.4 2.7 %finish.1 = (bf16[256,512]{1,0:T(8,128)(2,1)}, f32[512,64]{1,0:T(8,128)}) custom-call(s32[1]{0:T(128)} %bitcast.place_ref, f32[64,64]{1,0:T(8,128)} %inverse_factor.1.inverse_ref, f32[32,64,128]{2,1,0:T(8,128)} %all_to_all.55.left_ref, f32[16,8,256]{2,1,0:T(8,128)} %copy-done), custom_call_target="tpu_custom_call" | custom-call | flops 100663296 | bytes 131072 | tf_op jit(solution)/shard_map/finish/pallas_call | solution.py:249
  184.0 1.7 copy.8
  (4 shorter events, 0.0 us)
Async XLA Ops:
  7.2 139.7 %all-gather.3.cloned.1.call-start = ((), (), s32[]{:S(2)}) async-start(), calls=%async_computation.10 | async-start | bytes 2162688 | tf_op jit(solution)/shard_map/all_gather | solution.py:287
  30.8 4.9 %all-to-all-start.3 = ((bf16[2,128,128]{2,1,0:T(8,128)(2,1)}), bf16[2,128,128]{2,1,0:T(8,128)(2,1)S(1)}, u32[]{:S(2)}, u32[]{:S(2)}) async-start(bf16[2,128,128]{2,1,0:T(8,128)(2,1)} %bitcast.5), calls=%async_computation.3 | async-start | bytes 131072 | tf_op jit(solution)/shard_map/all_to_all | solution.py:274
  35.6 29.4 %copy-start.2 = (bf16[2,128,128]{2,1,0:T(8,128)(2,1)}, bf16[2,128,128]{2,1,0:T(8,128)(2,1)S(1)}, u32[]{:S(2)}) copy-start(bf16[2,128,128]{2,1,0:T(8,128)(2,1)S(1)} %all-to-all-done.3.columns_ref) | copy-start | bytes 196612
  35.6 29.4 %all-to-all-start.2 = ((f32[4,64,128]{2,1,0:T(8,128)}), f32[4,64,128]{2,1,0:T(8,128)S(1)}, u32[]{:S(2)}, u32[]{:S(2)}) async-start(f32[4,64,128]{2,1,0:T(8,128)} %summed_copies.7), calls=%async_computation.2 | async-start | bytes 262144 | tf_op jit(solution)/shard_map/all_to_all | solution.py:274
  65.1 0.7 copy-start.1
  168.2 12.5 %all-to-all-start.9 = ((f32[16,8,256]{2,1,0:T(8,128)}), f32[16,8,256]{2,1,0:T(8,128)S(1)}, u32[]{:S(2)}, u32[]{:S(2)}) async-start(f32[16,8,256]{2,1,0:T(8,128)} %summed_copies.11), calls=%async_computation.9 | async-start | bytes 262144 | tf_op jit(solution)/shard_map/all_to_all | solution.py:274
  180.7 0.7 copy-start
Sparse Core Ops, SparseCore 0:
  10.1 78.7 all-gather.2

commit v2 on v1

v2 whole, which is shorter than its diff:
```python
import jax
import jax.numpy as jnp
from jax import lax
from jax.experimental import pallas as pl
from jax.experimental.pallas import tpu as pltpu
from jax.sharding import Mesh
from jax.sharding import PartitionSpec as P

F32 = jnp.float32
BF16 = jnp.bfloat16
LANES = 128
XY = ("x", "y")
FAST = dict(preferred_element_type=F32)
FULL = dict(preferred_element_type=F32, precision=lax.Precision.HIGHEST)


def nn(a, b, kind=FAST):
    return lax.dot_general(a, b, (((1,), (0,)), ((), ())), **kind)


def nt(a, b, kind=FAST):
    return lax.dot_general(a, b, (((1,), (1,)), ((), ())), **kind)


def tn(a, b, kind=FAST):
    return lax.dot_general(a, b, (((0,), (0,)), ((), ())), **kind)


def pieces(value):
    high = value.astype(BF16)
    rest = value - high.astype(F32)
    middle = rest.astype(BF16)
    low = (rest - middle.astype(F32)).astype(BF16)
    return jnp.concatenate([high, middle, low], axis=0)


def folded(stacked):
    third = stacked.shape[0] // 3
    return stacked[:third] + (stacked[third : 2 * third] + stacked[2 * third :])


PARAMS = pltpu.CompilerParams(vmem_limit_bytes=16 * 1024 * 1024)


def cost(flops, count):
    return pl.CostEstimate(flops=flops, bytes_accessed=count, transcendentals=0)


def project(start_right, grads, copies):
    rank, width = start_right.shape
    tokens = grads.shape[0]

    def kernel(start_ref, grads_ref, split_ref, out_ref):
        split = pieces(start_ref[...])
        split_ref[...] = split
        result = folded(nt(split, grads_ref[...]))
        for i in range(copies):
            out_ref[i] = result

    return pl.pallas_call(
        kernel,
        out_shape=(
            jax.ShapeDtypeStruct((3 * rank, width), BF16),
            jax.ShapeDtypeStruct((copies, rank, tokens), F32),
        ),
        cost_estimate=cost(6 * rank * width * tokens, 2 * grads.size + 8 * start_right.size),
        compiler_params=PARAMS,
        name="project",
    )(start_right, grads)


def feedback_left(half, split, feedback, pairs):
    rows, width = feedback.shape
    rank = split.shape[0] // 3

    def kernel(half_ref, split_ref, feed_ref, own_ref, other_ref):
        result = folded(nt(split_ref[...], feed_ref[...]))
        odd = half_ref[0] == 1
        for i in range(pairs):
            even_rows = result[:, 2 * i * LANES : (2 * i + 1) * LANES]
            odd_rows = result[:, (2 * i + 1) * LANES : (2 * i + 2) * LANES]
            own_ref[i] = jnp.where(odd, odd_rows, even_rows)
            other_ref[i] = jnp.where(odd, even_rows, odd_rows)

    block = pl.BlockSpec((pairs, rank, LANES), lambda i, half: (i, 0, 0))
    shape = jax.ShapeDtypeStruct((rows // (2 * LANES), rank, LANES), F32)
    return pl.pallas_call(
        kernel,
        grid_spec=pltpu.PrefetchScalarGridSpec(
            num_scalar_prefetch=1,
            grid=(rows // (2 * pairs * LANES),),
            in_specs=[
                pl.BlockSpec(split.shape, lambda i, half: (0, 0)),
                pl.BlockSpec((2 * pairs * LANES, width), lambda i, half: (i, 0)),
            ],
            out_specs=[block, block],
        ),
        out_shape=(shape, shape),
        cost_estimate=cost(6 * rank * width * rows, 2 * feedback.size + 4 * rows * rank),
        compiler_params=PARAMS,
        name="feedback_left",
    )(half, split, feedback)


def block_at(place_ref, step, far_size, near_size):
    far = lax.rem(place_ref[0] + step, far_size)
    return far * near_size + place_ref[1]


def whole_specs(count):
    scalar = pl.BlockSpec(memory_space=pltpu.SMEM)
    return [scalar] + [pl.BlockSpec(memory_space=pltpu.VMEM)] * count


def add_activations(place, shares, columns, own, other):
    ways, rank, tokens = shares.shape
    far_size, blocks = len(columns), own.shape[0]

    def kernel(place_ref, shares_ref, own_ref, other_ref, *refs):
        column_refs, out_ref = refs[:-1], refs[-1]
        for i in range(blocks):
            out_ref[i] = own_ref[i] + other_ref[i]
        total = shares_ref[0]
        for i in range(1, ways):
            total = total + shares_ref[i]
        across = jnp.concatenate([ref[...] for ref in column_refs], axis=1)
        extra = folded(nn(pieces(total), across))
        for i in range(far_size):
            block = block_at(place_ref, i, far_size, blocks // far_size)
            out_ref[block] = out_ref[block] + extra[:, i * LANES : (i + 1) * LANES]

    return pl.pallas_call(
        kernel,
        in_specs=whole_specs(3 + far_size),
        out_shape=jax.ShapeDtypeStruct(own.shape, F32),
        cost_estimate=cost(24 * rank * tokens * LANES, 12 * own.size),
        compiler_params=PARAMS,
        name="add_activations",
    )(place, shares, own, other, *columns)


def summed_copies(shares, copies):
    ways, rows, lanes = shares.shape

    def kernel(shares_ref, out_ref):
        total = shares_ref[0]
        for i in range(1, ways):
            total = total + shares_ref[i]
        for i in range(copies):
            out_ref[i] = total

    return pl.pallas_call(
        kernel,
        out_shape=jax.ShapeDtypeStruct((copies, rows, lanes), F32),
        cost_estimate=cost(shares.size, 4 * shares.size),
        compiler_params=PARAMS,
        name="summed_copies",
    )(shares)


def inner_products(place, left, columns, copies):
    blocks, rank, _ = left.shape
    far_size, tokens = len(columns), columns[0].shape[0]

    def kernel(place_ref, left_ref, *refs):
        column_refs, out_ref = refs[:-1], refs[-1]
        rows = [left_ref[block_at(place_ref, i, far_size, blocks // far_size)] for i in range(far_size)]
        across = jnp.concatenate([ref[...] for ref in column_refs], axis=1)
        result = folded(nt(pieces(jnp.concatenate(rows, axis=1)), across))
        for i in range(copies):
            out_ref[i] = result

    return pl.pallas_call(
        kernel,
        in_specs=whole_specs(1 + far_size),
        out_shape=jax.ShapeDtypeStruct((copies, rank, tokens), F32),
        cost_estimate=cost(6 * rank * tokens * far_size * LANES, 8 * columns[0].size),
        compiler_params=PARAMS,
        name="inner_products",
    )(place, left, *columns)


def feedback_right(half, left, feedback, group, before):
    blocks, rank, _ = left.shape
    rows, width = feedback.shape
    steps = blocks // group
    first = before is None

    def kernel(half_ref, left_ref, *refs):
        feeds, refs = refs[:group], refs[group:]
        old, (out_ref, gram_ref, right, gram) = refs[:-4], refs[-4:]
        step = pl.program_id(0)

        @pl.when(step == 0)
        def _():
            right[...] = jnp.zeros_like(right)
            gram[...] = jnp.zeros_like(gram)

        split = pieces(jnp.concatenate([left_ref[i] for i in range(group)], axis=1))
        right[...] += folded(nn(split, jnp.concatenate([feed[...] for feed in feeds], axis=0)))
        gram[...] += nt(split, split)

        @pl.when(step == steps - 1)
        def _():
            square = folded(gram[...])
            square = square[:, :rank] + square[:, rank : 2 * rank] + square[:, 2 * rank :]
            total = right[...]
            out_ref[...] = total if first else total + old[0][...]
            gram_ref[...] = square if first else square + old[1][...]

    whole = [
        pl.BlockSpec((rank, width), lambda i, half: (0, 0)),
        pl.BlockSpec((rank, rank), lambda i, half: (0, 0)),
    ]
    return pl.pallas_call(
        kernel,
        grid_spec=pltpu.PrefetchScalarGridSpec(
            num_scalar_prefetch=1,
            grid=(steps,),
            in_specs=[
                pl.BlockSpec((group, rank, LANES), lambda i, half: (i, 0, 0)),
            ]
            + [
                pl.BlockSpec((LANES, width), lambda i, half, j=j: (2 * (group * i + j) + half[0], 0))
                for j in range(group)
            ]
            + ([] if first else whole),
            out_specs=whole,
            scratch_shapes=[
                pltpu.VMEM((rank, width), F32),
                pltpu.VMEM((3 * rank, 3 * rank), F32),
            ],
        ),
        out_shape=(
            jax.ShapeDtypeStruct((rank, width), F32),
            jax.ShapeDtypeStruct((rank, rank), F32),
        ),
        cost_estimate=cost(3 * rank * rows * (width + 3 * rank), feedback.size),
        compiler_params=PARAMS,
        name="feedback_right",
    )(half, left, *([feedback] * group), *(before or ()))


def add_grads(shares, grads, partial, parts):
    ways, rank, tokens = shares.shape
    width = grads.shape[1]
    split_rows = rank * width // (256 * parts)
    across = width // 256

    def kernel(shares_ref, grads_ref, partial_ref, out_ref):
        inner = shares_ref[0]
        for i in range(1, ways):
            inner = inner + shares_ref[i]
        total = partial_ref[...] + folded(nn(pieces(inner), grads_ref[...]))
        for i in range(parts):
            down, over = i // across * split_rows, i % across * 256
            out_ref[i] = total[down : down + split_rows, over : over + 256]

    return pl.pallas_call(
        kernel,
        out_shape=jax.ShapeDtypeStruct((parts, split_rows, 256), F32),
        cost_estimate=cost(6 * rank * tokens * width, 4 * shares.size + 2 * grads.size),
        compiler_params=PARAMS,
        name="add_grads",
    )(shares, grads, partial)


def inverse_factor(gram):
    rank = gram.shape[0]

    def kernel(gram_ref, out_ref):
        row = lax.broadcasted_iota(jnp.int32, (rank, rank), 0)
        col = lax.broadcasted_iota(jnp.int32, (rank, rank), 1)
        work = jnp.concatenate([gram_ref[...], (row == col).astype(F32)], axis=1)
        index = lax.broadcasted_iota(jnp.int32, (rank, 1), 0)
        for k in range(rank):
            low = k // 8 * 8
            pivot_row = work[k : k + 1]
            scale = 1.0 / work[k : k + 1, k : k + 1]
            part = work[low:]
            factor = jnp.where(index[low:] > k, part[:, k : k + 1] * scale, 0.0)
            part = part - factor * pivot_row
            work = part if low == 0 else jnp.concatenate([work[:low], part], axis=0)
        diagonal = jnp.sum(jnp.where(row == col, work[:, :rank], 0.0), axis=1, keepdims=True)
        out_ref[...] = work[:, rank:] / jnp.sqrt(diagonal)

    return pl.pallas_call(
        kernel,
        out_shape=jax.ShapeDtypeStruct((rank, rank), F32),
        cost_estimate=cost(2 * rank * rank * rank * 8, 8 * rank * rank),
        compiler_params=PARAMS,
        name="inverse_factor",
    )(gram)


def finish(place, half, inverse, own, other, gathered, width):
    rank = inverse.shape[0]
    parts = gathered.shape[0]
    across = width // 256
    slab = 2 * LANES

    def kernel(place_ref, half_ref, inverse_ref, own_ref, other_ref, gathered_ref, dec_ref, right_ref):
        across_rows = [
            jnp.concatenate([gathered_ref[i + j] for j in range(across)], axis=1)
            for i in range(0, parts, across)
        ]
        right = nn(inverse_ref[...], jnp.concatenate(across_rows, axis=0), FULL)
        right_ref[...] = right
        odd = half_ref[0] == 1
        even_rows = jnp.where(odd, other_ref[0], own_ref[0])
        odd_rows = jnp.where(odd, own_ref[0], other_ref[0])
        basis = nn(inverse_ref[...], jnp.concatenate([even_rows, odd_rows], axis=1), FULL)
        dec_ref[...] = tn(basis, right, FULL).astype(BF16)

    block = pl.BlockSpec((1, rank, LANES), lambda i, place, half: (place[0], 0, 0))
    return pl.pallas_call(
        kernel,
        grid_spec=pltpu.PrefetchScalarGridSpec(
            num_scalar_prefetch=2,
            grid=(1,),
            in_specs=[
                pl.BlockSpec(inverse.shape, lambda i, place, half: (0, 0)),
                block,
                block,
                pl.BlockSpec(gathered.shape, lambda i, place, half: (0, 0, 0)),
            ],
            out_specs=[
                pl.BlockSpec((slab, width), lambda i, place, half: (0, 0)),
                pl.BlockSpec((rank, width), lambda i, place, half: (0, 0)),
            ],
        ),
        out_shape=(
            jax.ShapeDtypeStruct((slab, width), BF16),
            jax.ShapeDtypeStruct((rank, width), F32),
        ),
        cost_estimate=cost(12 * rank * slab * width, 4 * gathered.size),
        compiler_params=PARAMS,
        name="finish",
    )(place, half, inverse, own, other, gathered)


def exchange(value, axes):
    return lax.all_to_all(value, axes, 0, 0, tiled=True)


def index_of(axes):
    return lax.axis_index(axes).astype(jnp.int32).reshape(1)


def per_device(activations, grads_out, feedback, start_right):
    width = grads_out.shape[1]
    far, near = lax.axis_size("zh"), lax.axis_size("zl")
    outer = lax.axis_size(XY)
    place, half = jnp.concatenate([index_of("zh"), index_of("zl")]), index_of("c")

    columns = [activations] + [
        lax.ppermute(activations, "zh", [((i + j) % far, i) for i in range(far)])
        for j in range(1, far)
    ]
    split, inner = project(start_right.T, grads_out, 2 * near)
    inner = exchange(inner, ("zl", "c"))
    own, other = feedback_left(half, split, feedback, 2)
    other = lax.ppermute(other, "c", [(0, 1), (1, 0)])
    left = add_activations(place, inner, columns, own, other)

    left = summed_copies(exchange(left, XY), near)
    left = summed_copies(exchange(left, "zl"), far)
    left = summed_copies(exchange(left, "zh"), outer)
    own = exchange(left, XY)
    other = lax.ppermute(own, "c", [(0, 1), (1, 0)])

    inner = exchange(inner_products(place, own, columns, 2 * near), ("zl", "c"))
    right = feedback_right(half, own, feedback, 4, None)
    right, gram = feedback_right(1 - half, other, feedback, 4, right)
    inverse = inverse_factor(gram)
    right = add_grads(inner, grads_out, right, outer)
    right = summed_copies(exchange(right, XY), outer)
    right = exchange(right, XY)
    decompressed, right = finish(index_of(XY), half, inverse, own, other, right, width)
    return decompressed, right.T


def solution(mesh):
    outer, tp = mesh.shape["outer"], mesh.shape["tp"]
    across = 4 if outer == 16 else 2
    near = 4 if tp == 32 else 2
    names = ("x", "y", "zh", "zl", "c")
    shape = (outer // across, across, tp // (2 * near), near, 2)
    split_mesh = Mesh(mesh.devices.reshape(shape), names)
    z = ("zh", "zl", "c")
    return jax.shard_map(
        per_device,
        mesh=split_mesh,
        in_specs=(P(XY, z), P(XY, z), P(XY, z), P(z, None)),
        out_specs=(P(XY, z), P(z, None)),
        check_vma=False,
    )
```

time: 196 us -> 158 us (0.81)
  blocking collectives: 103 us -> 77.2 us
  Pallas kernels: 38.7 us -> 17.2 us
  starting transfers between devices: 22.3 us -> 42.8 us
  between operations: 14 us -> 0.78 us
  local copies, waits for them, and re-layouts: 4.77 us -> 6.9 us
    ppermute x0 -> x5, starting transfers between devices: none -> 27.8 us  [the longest x3 23 us: per_device(): lax.ppermute(activations, 'zh', [((i + j) % far, i) for i in range(far)])]
    all_to_all x7 -> x5, blocking collectives: 103 us -> 77.2 us  [exchange(): return lax.all_to_all(value, axes, 0, 0, tiled=True)]
    pallas_call x6 -> x4, Pallas kernels: 10.2 us -> 0.77 us  [summed_copies(): pl.pallas_call(kernel, out_shape=jax.ShapeDtypeStruct((copies, rows, lane...]
    pallas_call x3 -> x6, Pallas kernels: 17 us -> 8.24 us  [the longest x2 2.98 us: feedback_right(): pl.pallas_call(kernel, grid_spec=pltpu.PrefetchScalarGridSpec(num_scalar_...]
    all_to_all x3, starting transfers between devices: 22.3 us -> 15 us  [exchange(): return lax.all_to_all(value, axes, 0, 0, tiled=True)]
    ppermute x0 -> x5, waiting for transfers between devices: none -> 4.09 us  [the longest x3 4.09 us: per_device(): lax.ppermute(activations, 'zh', [((i + j) % far, i) for i in range(far)])]
    unnamed x7 -> x14, local copies, waits for them, and re-layouts: 3.05 us -> 6.9 us
  transfers between devices with their start and end apart: 4 -> 8, of which waited for: 1 -> 4; matrix products, arithmetic and copies ran while one was open for 1% -> 0% of each run, Pallas kernels for 14% -> 7%
where the time goes in v2:
time: 158 us; the launch traced here: 157 us
  blocking collectives  77.2 us (49%)
  starting transfers between devices  42.8 us (27%)
  Pallas kernels  17.2 us (11%)
  waiting for transfers between devices  11.6 us (7%)
  local copies, waits for them, and re-layouts  6.9 us (4%)
    all_to_all x5, blocking collectives, exchange(): return lax.all_to_all(value, axes, 0, 0, tiled=True)  77.2 us
    ppermute x3, starting transfers between devices, per_device(): lax.ppermute(activations, 'zh', [((i + j) % far, i) for i in range(far)])  23 us
    all_to_all x3, starting transfers between devices, exchange(): return lax.all_to_all(value, axes, 0, 0, tiled=True)  15 us
    all_to_all x3, waiting for transfers between devices, exchange(): return lax.all_to_all(value, axes, 0, 0, tiled=True)  7.48 us
    unnamed x14, local copies, waits for them, and re-layouts  6.9 us
    pallas_call x1, Pallas kernels, inverse_factor(): pl.pallas_call(kernel, out_shape=jax.ShapeDtypeStruct((rank, rank), F32),...  5.46 us
    ppermute x3, waiting for transfers between devices, per_device(): lax.ppermute(activations, 'zh', [((i + j) % far, i) for i in range(far)])  4.09 us
  transfers between devices with their start and end apart: 8, of which 4 were waited for; matrix products, arithmetic and copies ran while one was open for 0% of the time, Pallas kernels for 7%

profile of v2, /device:TPU:6, one launch (start us, length us, event | category | flops | bytes accessed | tf_op | source)
XLA Modules:
  0.0 156.5 jit_solution(7686984945639357840)
XLA Ops:
  0.6 0.9 copy-done.3
  1.6 0.9 copy-done.6
  2.5 1.1 project.1
  3.6 5.9 %all-to-all-start = ((f32[8,64,256]{2,1,0:T(8,128)}), f32[8,64,256]{2,1,0:T(8,128)S(1)}, u32[]{:S(2)}, u32[]{:S(2)}) async-start(f32[8,64,256]{2,1,0:T(8,128)} %get-tuple-element.12), calls=%async_computation | async-start | bytes 1048576 | tf_op jit(solution)/shard_map/all_to_all | solution.py:343
  9.5 2.2 %copy-done = bf16[4096,512]{1,0:T(8,128)(2,1)S(1)} copy-done((bf16[4096,512]{1,0:T(8,128)(2,1)S(1)}, bf16[4096,512]{1,0:T(8,128)(2,1)}, u32[]{:S(2)}) %copy-start) | copy-done | bytes 4194328
  11.6 2.7 %feedback_left.1 = (f32[16,64,128]{2,1,0:T(8,128)S(1)}, f32[16,64,128]{2,1,0:T(8,128)S(1)}) custom-call(s32[1]{0:T(128)} %bitcast.1.half_ref, bf16[192,512]{1,0:T(8,128)(2,1)S(1)} %get-tuple-element.13.split_ref, bf16[4096,512]{1,0:T(8,128)(2,1)S(1)} %copy-done), custom_call_target="tpu_custom_call" | custom-call | flops 805306368 | bytes 5242880 | tf_op jit(solution)/shard_map/feedback_left/pallas_call | solution.py:87
  14.3 2.4 %collective-permute-start = (f32[16,64,128]{2,1,0:T(8,128)S(1)}, f32[16,64,128]{2,1,0:T(8,128)S(1)}, u32[]{:S(2)}, u32[]{:S(2)}) collective-permute-start(f32[16,64,128]{2,1,0:T(8,128)S(1)} %get-tuple-element.15), channel_id=1, source_target_pairs={{0,1},{1,0},{2,3},{3,2},{4,5},{5,4},{6,7},{7,6},{8,9},{9,8},{10,11... | collective-permute-start | bytes 1572872 | tf_op jit(solution)/shard_map/ppermute | solution.py:363
  16.8 10.2 %collective-permute-start.1 = (bf16[256,128]{1,0:T(8,128)(2,1)S(1)}, bf16[256,128]{1,0:T(8,128)(2,1)S(1)}, u32[]{:S(2)}, u32[]{:S(2)}) collective-permute-start(bf16[256,128]{1,0:T(8,128)(2,1)S(1)} %copy-done.5), channel_id=1, source_target_pairs={{8,0},{16,8},{24,16},{0,24},{9,1},{17,9},{25,17},{1,25},{10,2},{18... | collective-permute-start | bytes 196616 | tf_op jit(solution)/shard_map/ppermute | solution.py:357
  27.0 6.1 %collective-permute-start.2 = (bf16[256,128]{1,0:T(8,128)(2,1)S(1)}, bf16[256,128]{1,0:T(8,128)(2,1)S(1)}, u32[]{:S(2)}, u32[]{:S(2)}) collective-permute-start(bf16[256,128]{1,0:T(8,128)(2,1)S(1)} %copy-done.5), channel_id=1, source_target_pairs={{16,0},{24,8},{0,16},{8,24},{17,1},{25,9},{1,17},{9,25},{18,2},{26... | collective-permute-start | bytes 196616 | tf_op jit(solution)/shard_map/ppermute | solution.py:357
  33.2 6.6 %collective-permute-start.3 = (bf16[256,128]{1,0:T(8,128)(2,1)S(1)}, bf16[256,128]{1,0:T(8,128)(2,1)S(1)}, u32[]{:S(2)}, u32[]{:S(2)}) collective-permute-start(bf16[256,128]{1,0:T(8,128)(2,1)S(1)} %copy-done.5), channel_id=1, source_target_pairs={{24,0},{0,8},{8,16},{16,24},{25,1},{1,9},{9,17},{17,25},{26,2},{2,... | collective-permute-start | bytes 196616 | tf_op jit(solution)/shard_map/ppermute | solution.py:357
  39.8 2.3 %collective-permute-done.2.refs_2_ = bf16[256,128]{1,0:T(8,128)(2,1)S(1)} collective-permute-done((bf16[256,128]{1,0:T(8,128)(2,1)S(1)}, bf16[256,128]{1,0:T(8,128)(2,1)S(1)}, u32[]{:S(2)}, u32[]{:S(2)}) %collective-permute-start.2) | collective-permute-done | bytes 65568 | tf_op jit(solution)/shard_map/ppermute | solution.py:357
  42.1 1.8 %collective-permute-done.3.refs_3_ = bf16[256,128]{1,0:T(8,128)(2,1)S(1)} collective-permute-done((bf16[256,128]{1,0:T(8,128)(2,1)S(1)}, bf16[256,128]{1,0:T(8,128)(2,1)S(1)}, u32[]{:S(2)}, u32[]{:S(2)}) %collective-permute-start.3) | collective-permute-done | bytes 65568 | tf_op jit(solution)/shard_map/ppermute | solution.py:357
  43.9 0.8 add_activations.1
  44.7 16.2 %all_to_all.40.shares_ref = f32[16,64,128]{2,1,0:T(8,128)S(1)} all-to-all(f32[16,64,128]{2,1,0:T(8,128)S(1)} %add_activations.1), channel_id=1, replica_groups=mesh['x'=4,'y'=4,'zh'=4,'zl'=4,'c'=2] {'x','y'}, dimensions={0} | all-to-all | bytes 1048576 | tf_op jit(solution)/shard_map/all_to_all | solution.py:343
  60.9 14.7 %all_to_all.41.shares_ref = f32[4,64,128]{2,1,0:T(8,128)S(1)} all-to-all(f32[4,64,128]{2,1,0:T(8,128)S(1)} %summed_copies.4), channel_id=1, replica_groups=mesh['x'=4,'y'=4,'zh'=4,'zl'=4,'c'=2] {'zl'}, dimensions={0} | all-to-all | bytes 262144 | tf_op jit(solution)/shard_map/all_to_all | solution.py:343
  75.6 21.8 %all_to_all.42.shares_ref = f32[4,64,128]{2,1,0:T(8,128)S(1)} all-to-all(f32[4,64,128]{2,1,0:T(8,128)S(1)} %summed_copies.5), channel_id=1, replica_groups=mesh['x'=4,'y'=4,'zh'=4,'zl'=4,'c'=2] {'zh'}, dimensions={0} | all-to-all | bytes 262144 | tf_op jit(solution)/shard_map/all_to_all | solution.py:343
  97.5 13.4 %all_to_all.43.left_ref.own_ref = f32[16,64,128]{2,1,0:T(8,128)S(1)} all-to-all(f32[16,64,128]{2,1,0:T(8,128)S(1)} %summed_copies.6), channel_id=1, replica_groups=mesh['x'=4,'y'=4,'zh'=4,'zl'=4,'c'=2] {'x','y'}, dimensions={0} | all-to-all | bytes 1048576 | tf_op jit(solution)/shard_map/all_to_all | solution.py:343
  110.9 1.6 %inner_products.1 = f32[8,64,256]{2,1,0:T(8,128)} custom-call(s32[2]{0:T(128)S(1)} %pad_add_fusion.place_ref, f32[16,64,128]{2,1,0:T(8,128)S(1)} %all_to_all.43.left_ref.own_ref, bf16[256,128]{1,0:T(8,128)(2,1)S(1)} %copy-done.5, bf16[256,128]{1,0:T(8,128)(2,1)S(1)} %collective-permute-done.1.refs_1_, bf16[256,128]{1,0:T(8,128)(2,1)S(1)} %collective-permute-done.2.refs_2_, ...), custom_call_target="tpu_custom_call" | custom-call | flops 50331648 | bytes 262144 | tf_op jit(solution)/shard_map/inner_products/pallas_call | solution.py:173
  112.5 3.5 %all-to-all-start.5 = ((f32[8,64,256]{2,1,0:T(8,128)}), f32[8,64,256]{2,1,0:T(8,128)S(1)}, u32[]{:S(2)}, u32[]{:S(2)}) async-start(f32[8,64,256]{2,1,0:T(8,128)} %inner_products.1), calls=%async_computation.5 | async-start | bytes 1048576 | tf_op jit(solution)/shard_map/all_to_all | solution.py:343
  116.0 2.4 %collective-permute-start.4 = (f32[16,64,128]{2,1,0:T(8,128)S(1)}, f32[16,64,128]{2,1,0:T(8,128)S(1)}, u32[]{:S(2)}, u32[]{:S(2)}) collective-permute-start(f32[16,64,128]{2,1,0:T(8,128)S(1)} %all_to_all.43.left_ref.own_ref), channel_id=1, source_target_pairs={{0,1},{1,0},{2,3},{3,2},{4,5},{5,4},{6,7},{7,6},{8,9},{9,8},{10,11... | collective-permute-start | bytes 1572872 | tf_op jit(solution)/shard_map/ppermute | solution.py:370
  118.4 2.2 %copy-done.1 = bf16[4096,512]{1,0:T(8,128)(2,1)S(1)} copy-done((bf16[4096,512]{1,0:T(8,128)(2,1)S(1)}, bf16[4096,512]{1,0:T(8,128)(2,1)}, u32[]{:S(2)}) %copy-start.1) | copy-done | bytes 4194328
  120.6 1.5 feedback_right.2
  122.1 0.7 copy-done.2
  122.8 1.5 feedback_right.3
  124.3 7.1 %all-to-all-done.5.shares_ref = f32[8,64,256]{2,1,0:T(8,128)S(1)} async-done(((f32[8,64,256]{2,1,0:T(8,128)}), f32[8,64,256]{2,1,0:T(8,128)S(1)}, u32[]{:S(2)}, u32[]{:S(2)}) %all-to-all-start.5) | async-done | bytes 524320 | tf_op jit(solution)/shard_map/all_to_all | solution.py:343
  131.4 0.2 add_grads.1
  131.6 11.2 %all_to_all.44.shares_ref = f32[16,8,256]{2,1,0:T(8,128)S(1)} all-to-all(f32[16,8,256]{2,1,0:T(8,128)S(1)} %add_grads.1), channel_id=1, replica_groups=mesh['x'=4,'y'=4,'zh'=4,'zl'=4,'c'=2] {'x','y'}, dimensions={0} | all-to-all | bytes 262144 | tf_op jit(solution)/shard_map/all_to_all | solution.py:343
  142.7 0.7 summed_copies.7
  143.4 5.6 %all-to-all-start.7 = ((f32[16,8,256]{2,1,0:T(8,128)}), f32[16,8,256]{2,1,0:T(8,128)S(1)}, u32[]{:S(2)}, u32[]{:S(2)}) async-start(f32[16,8,256]{2,1,0:T(8,128)} %summed_copies.7), calls=%async_computation.7 | async-start | bytes 262144 | tf_op jit(solution)/shard_map/all_to_all | solution.py:343
  149.0 5.5 %inverse_factor.1.inverse_ref = f32[64,64]{1,0:T(8,128)S(1)} custom-call(f32[64,64]{1,0:T(8,128)S(1)} %get-tuple-element.18.gram_ref), custom_call_target="tpu_custom_call" | custom-call | flops 4194304 | bytes 32768 | tf_op jit(solution)/shard_map/inverse_factor/pallas_call | solution.py:287
  154.4 0.4 all-to-all-done.7.gathered_ref
  154.9 1.7 %finish.1 = (bf16[256,512]{1,0:T(8,128)(2,1)}, f32[64,512]{1,0:T(8,128)}) custom-call(s32[1]{0:T(128)} %bitcast.place_ref, s32[1]{0:T(128)} %bitcast.1.half_ref, f32[64,64]{1,0:T(8,128)S(1)} %inverse_factor.1.inverse_ref, f32[16,64,128]{2,1,0:T(8,128)S(1)} %all_to_all.43.left_ref.own_ref, f32[16,64,128]{2,1,0:T(8,128)S(1)} %collective-permute-done.4.left_ref.other_ref, ...), custom_call_target="tpu_custom_call" | custom-call | flops 100663296 | bytes 131072 | tf_op jit(solution)/shard_map/finish/pallas_call | solution.py:316
  (17 shorter events, 0.2 us)
Async XLA Ops:
  0.6 1.0 copy-start.3
  1.6 0.9 copy-start.6
  2.5 14.3 %copy-start.5 = (bf16[256,128]{1,0:T(8,128)(2,1)S(1)}, bf16[256,128]{1,0:T(8,128)(2,1)}, u32[]{:S(2)}) copy-start(bf16[256,128]{1,0:T(8,128)(2,1)} %refs_0_.7) | copy-start | bytes 196612
  3.6 40.4 %all-to-all-start = ((f32[8,64,256]{2,1,0:T(8,128)}), f32[8,64,256]{2,1,0:T(8,128)S(1)}, u32[]{:S(2)}, u32[]{:S(2)}) async-start(f32[8,64,256]{2,1,0:T(8,128)} %get-tuple-element.12), calls=%async_computation | async-start | bytes 1048576 | tf_op jit(solution)/shard_map/all_to_all | solution.py:343
  9.5 2.2 %copy-start = (bf16[4096,512]{1,0:T(8,128)(2,1)S(1)}, bf16[4096,512]{1,0:T(8,128)(2,1)}, u32[]{:S(2)}) copy-start(bf16[4096,512]{1,0:T(8,128)(2,1)} %refs_3_.3) | copy-start | bytes 12582916
  14.3 29.6 %collective-permute-start = (f32[16,64,128]{2,1,0:T(8,128)S(1)}, f32[16,64,128]{2,1,0:T(8,128)S(1)}, u32[]{:S(2)}, u32[]{:S(2)}) collective-permute-start(f32[16,64,128]{2,1,0:T(8,128)S(1)} %get-tuple-element.15), channel_id=1, source_target_pairs={{0,1},{1,0},{2,3},{3,2},{4,5},{5,4},{6,7},{7,6},{8,9},{9,8},{10,11... | collective-permute-start | bytes 1572872 | tf_op jit(solution)/shard_map/ppermute | solution.py:363
  16.8 23.1 %collective-permute-start.1 = (bf16[256,128]{1,0:T(8,128)(2,1)S(1)}, bf16[256,128]{1,0:T(8,128)(2,1)S(1)}, u32[]{:S(2)}, u32[]{:S(2)}) collective-permute-start(bf16[256,128]{1,0:T(8,128)(2,1)S(1)} %copy-done.5), channel_id=1, source_target_pairs={{8,0},{16,8},{24,16},{0,24},{9,1},{17,9},{25,17},{1,25},{10,2},{18... | collective-permute-start | bytes 196616 | tf_op jit(solution)/shard_map/ppermute | solution.py:357
  27.0 15.1 %collective-permute-start.2 = (bf16[256,128]{1,0:T(8,128)(2,1)S(1)}, bf16[256,128]{1,0:T(8,128)(2,1)S(1)}, u32[]{:S(2)}, u32[]{:S(2)}) collective-permute-start(bf16[256,128]{1,0:T(8,128)(2,1)S(1)} %copy-done.5), channel_id=1, source_target_pairs={{16,0},{24,8},{0,16},{8,24},{17,1},{25,9},{1,17},{9,25},{18,2},{26... | collective-permute-start | bytes 196616 | tf_op jit(solution)/shard_map/ppermute | solution.py:357
  33.2 10.8 %collective-permute-start.3 = (bf16[256,128]{1,0:T(8,128)(2,1)S(1)}, bf16[256,128]{1,0:T(8,128)(2,1)S(1)}, u32[]{:S(2)}, u32[]{:S(2)}) collective-permute-start(bf16[256,128]{1,0:T(8,128)(2,1)S(1)} %copy-done.5), channel_id=1, source_target_pairs={{24,0},{0,8},{8,16},{16,24},{25,1},{1,9},{9,17},{17,25},{26,2},{2,... | collective-permute-start | bytes 196616 | tf_op jit(solution)/shard_map/ppermute | solution.py:357
  112.5 18.9 %all-to-all-start.5 = ((f32[8,64,256]{2,1,0:T(8,128)}), f32[8,64,256]{2,1,0:T(8,128)S(1)}, u32[]{:S(2)}, u32[]{:S(2)}) async-start(f32[8,64,256]{2,1,0:T(8,128)} %inner_products.1), calls=%async_computation.5 | async-start | bytes 1048576 | tf_op jit(solution)/shard_map/all_to_all | solution.py:343
  116.0 6.1 %collective-permute-start.4 = (f32[16,64,128]{2,1,0:T(8,128)S(1)}, f32[16,64,128]{2,1,0:T(8,128)S(1)}, u32[]{:S(2)}, u32[]{:S(2)}) collective-permute-start(f32[16,64,128]{2,1,0:T(8,128)S(1)} %all_to_all.43.left_ref.own_ref), channel_id=1, source_target_pairs={{0,1},{1,0},{2,3},{3,2},{4,5},{5,4},{6,7},{7,6},{8,9},{9,8},{10,11... | collective-permute-start | bytes 1572872 | tf_op jit(solution)/shard_map/ppermute | solution.py:370
  118.4 2.2 %copy-start.1 = (bf16[4096,512]{1,0:T(8,128)(2,1)S(1)}, bf16[4096,512]{1,0:T(8,128)(2,1)}, u32[]{:S(2)}) copy-start(bf16[4096,512]{1,0:T(8,128)(2,1)} %refs_3_.3) | copy-start | bytes 12582916
  120.6 2.2 %copy-start.2 = (bf16[4096,512]{1,0:T(8,128)(2,1)S(1)}, bf16[4096,512]{1,0:T(8,128)(2,1)}, u32[]{:S(2)}) copy-start(bf16[4096,512]{1,0:T(8,128)(2,1)} %refs_3_.3) | copy-start | bytes 12582916
  122.8 8.6 %copy-start.4 = (bf16[256,512]{1,0:T(8,128)(2,1)S(1)}, bf16[256,512]{1,0:T(8,128)(2,1)}, u32[]{:S(2)}) copy-start(bf16[256,512]{1,0:T(8,128)(2,1)} %grads_ref.3) | copy-start | bytes 786436
  143.4 11.4 %all-to-all-start.7 = ((f32[16,8,256]{2,1,0:T(8,128)}), f32[16,8,256]{2,1,0:T(8,128)S(1)}, u32[]{:S(2)}, u32[]{:S(2)}) async-start(f32[16,8,256]{2,1,0:T(8,128)} %summed_copies.7), calls=%async_computation.7 | async-start | bytes 262144 | tf_op jit(solution)/shard_map/all_to_all | solution.py:343

commit v3 on v2

v3 whole, which is shorter than its diff:
```python
import jax
import jax.numpy as jnp
from jax import lax
from jax.experimental import pallas as pl
from jax.experimental.pallas import tpu as pltpu
from jax.sharding import Mesh
from jax.sharding import PartitionSpec as P

F32 = jnp.float32
BF16 = jnp.bfloat16
LANES = 128
XY = ("x", "y")
FAST = dict(preferred_element_type=F32)
FULL = dict(preferred_element_type=F32, precision=lax.Precision.HIGHEST)


def nn(a, b, kind=FAST):
    return lax.dot_general(a, b, (((1,), (0,)), ((), ())), **kind)


def nt(a, b, kind=FAST):
    return lax.dot_general(a, b, (((1,), (1,)), ((), ())), **kind)


def tn(a, b, kind=FAST):
    return lax.dot_general(a, b, (((0,), (0,)), ((), ())), **kind)


def pieces(value):
    high = value.astype(BF16)
    rest = value - high.astype(F32)
    middle = rest.astype(BF16)
    low = (rest - middle.astype(F32)).astype(BF16)
    return jnp.concatenate([high, middle, low], axis=0)


def folded(stacked):
    third = stacked.shape[0] // 3
    return stacked[:third] + (stacked[third : 2 * third] + stacked[2 * third :])


PARAMS = pltpu.CompilerParams(vmem_limit_bytes=16 * 1024 * 1024)


def cost(flops, count):
    return pl.CostEstimate(flops=flops, bytes_accessed=count, transcendentals=0)


def kept_and_given(odd, value):
    half = value.shape[0] // 2
    first, second = value[:half], value[half:]
    return jnp.where(odd, second, first), jnp.where(odd, first, second)


def joined(odd, own, other):
    return jnp.concatenate([jnp.where(odd, other, own), jnp.where(odd, own, other)], axis=0)


def whole_specs(count):
    scalar = pl.BlockSpec(memory_space=pltpu.SMEM)
    return [scalar] + [pl.BlockSpec(memory_space=pltpu.VMEM)] * count


def added_copies(one, two, copies):
    def kernel(one_ref, two_ref, out_ref):
        total = one_ref[...] + two_ref[...]
        for i in range(copies):
            out_ref[i] = total

    return pl.pallas_call(
        kernel,
        out_shape=jax.ShapeDtypeStruct((copies,) + one.shape, F32),
        cost_estimate=cost(one.size, 4 * one.size * (2 + copies)),
        compiler_params=PARAMS,
        name="added_copies",
    )(one, two)


def fetched(feed_ref, held, sems):
    rows = held.shape[0] // sems.shape[0]
    copies = []
    for i in range(sems.shape[0]):
        part = pl.ds(i * rows, rows)
        copies.append(pltpu.make_async_copy(feed_ref.at[part], held.at[part], sems.at[i]))
        copies[-1].start()
    return copies


def left_products(half, start_right, grads, feedback, chunks):
    rows, width = feedback.shape
    rank, tokens = start_right.shape[0], grads.shape[0]
    pairs = rows // (2 * LANES * chunks)

    def kernel(half_ref, start_ref, grads_ref, feed_ref, *refs):
        keep_ref, give_ref, own_ref, other_ref, held, sems, start, held_grads, few = refs
        first = [
            pltpu.make_async_copy(start_ref, start, few.at[0]),
            pltpu.make_async_copy(grads_ref, held_grads, few.at[1]),
        ]
        for copy in first:
            copy.start()
        copies = fetched(feed_ref, held, sems)
        odd = half_ref[0] == 1
        first[0].wait()
        split = pieces(start[...])
        first[1].wait()
        keep_ref[...], give_ref[...] = kept_and_given(odd, folded(nt(split, held_grads[...])))
        for k in range(chunks):
            copies[k].wait()
            part = held[k * (rows // chunks) : (k + 1) * (rows // chunks)]
            result = folded(nt(split, part))
            for i in range(pairs):
                even_rows = result[:, 2 * i * LANES : (2 * i + 1) * LANES]
                odd_rows = result[:, (2 * i + 1) * LANES : (2 * i + 2) * LANES]
                own_ref[k * pairs + i] = jnp.where(odd, odd_rows, even_rows)
                other_ref[k * pairs + i] = jnp.where(odd, even_rows, odd_rows)

    small = jax.ShapeDtypeStruct((rank // 2, tokens), F32)
    large = jax.ShapeDtypeStruct((rows // (2 * LANES), rank, LANES), F32)
    return pl.pallas_call(
        kernel,
        in_specs=whole_specs(0) + [pl.BlockSpec(memory_space=pltpu.HBM)] * 3,
        out_shape=(small, small, large, large),
        scratch_shapes=[
            pltpu.VMEM(feedback.shape, BF16),
            pltpu.SemaphoreType.DMA((chunks,)),
            pltpu.VMEM(start_right.shape, F32),
            pltpu.VMEM(grads.shape, BF16),
            pltpu.SemaphoreType.DMA((2,)),
        ],
        cost_estimate=cost(6 * rank * width * rows, 2 * feedback.size + 4 * rows * rank),
        compiler_params=PARAMS,
        name="left_products",
    )(half, start_right, grads, feedback)


def add_activations(place, inner, columns, own, other):
    near_size, tokens = len(columns), columns[0].shape[0]
    blocks, rank, _ = own.shape

    def kernel(place_ref, inner_ref, inner_other_ref, own_ref, other_ref, *refs):
        column_refs, out_ref = refs[:-1], refs[-1]
        for i in range(blocks):
            out_ref[i] = own_ref[i] + other_ref[i]
        total = joined(place_ref[2] == 1, inner_ref[...], inner_other_ref[...])
        across = jnp.concatenate([ref[...] for ref in column_refs], axis=1)
        extra = folded(nn(pieces(total), across))
        for i in range(near_size):
            block = place_ref[0] * near_size + lax.rem(place_ref[1] + i, near_size)
            out_ref[block] = out_ref[block] + extra[:, i * LANES : (i + 1) * LANES]

    return pl.pallas_call(
        kernel,
        in_specs=whole_specs(4 + near_size),
        out_shape=jax.ShapeDtypeStruct(own.shape, F32),
        cost_estimate=cost(24 * rank * tokens * LANES, 12 * own.size),
        compiler_params=PARAMS,
        name="add_activations",
    )(place, *inner, own, other, *columns)


def summed_copies(shares, copies):
    ways, rows, lanes = shares.shape

    def kernel(shares_ref, out_ref):
        total = shares_ref[0]
        for i in range(1, ways):
            total = total + shares_ref[i]
        for i in range(copies):
            out_ref[i] = total

    return pl.pallas_call(
        kernel,
        out_shape=jax.ShapeDtypeStruct((copies, rows, lanes), F32),
        cost_estimate=cost(shares.size, 4 * shares.size),
        compiler_params=PARAMS,
        name="summed_copies",
    )(shares)


def right_products(half, own, other, gathered, feedback, grads, chunks, parts):
    blocks, rank, _ = own.shape
    rows, width = feedback.shape
    tokens = grads.shape[0]
    pairs = blocks // chunks
    split_rows = rank * width // (256 * parts)
    across = width // 256

    def kernel(
        half_ref, own_ref, other_ref, grads_ref, act_ref, feed_ref, out_ref, gram_ref, held, sems, act, act_sems
    ):
        act_copies = fetched(act_ref, act, act_sems)
        copies = fetched(feed_ref, held, sems)
        odd = half_ref[0] == 1
        right = jnp.zeros((rank, width), F32)
        inner = jnp.zeros((rank, tokens), F32)
        square = jnp.zeros((rank, 3 * rank), F32)
        for k in range(chunks):
            row_blocks = []
            for i in range(k * pairs, (k + 1) * pairs):
                row_blocks.append(jnp.where(odd, other_ref[i], own_ref[i]))
                row_blocks.append(jnp.where(odd, own_ref[i], other_ref[i]))
            split = pieces(jnp.concatenate(row_blocks, axis=1))
            square = square + folded(nt(split, split))
            act_copies[k].wait()
            columns = [act[i] for i in range(2 * k * pairs, 2 * (k + 1) * pairs)]
            inner = inner + folded(nt(split, jnp.concatenate(columns, axis=1)))
            copies[k].wait()
            part = held[k * (rows // chunks) : (k + 1) * (rows // chunks)]
            right = right + folded(nn(split, part))
        right = right + folded(nn(pieces(inner), grads_ref[...]))
        for i in range(parts):
            down, over = i // across * split_rows, i % across * 256
            out_ref[i] = right[down : down + split_rows, over : over + 256]
        gram_ref[...] = square[:, :rank] + square[:, rank : 2 * rank] + square[:, 2 * rank :]

    return pl.pallas_call(
        kernel,
        in_specs=whole_specs(3) + [pl.BlockSpec(memory_space=pltpu.HBM)] * 2,
        out_shape=(
            jax.ShapeDtypeStruct((parts, split_rows, 256), F32),
            jax.ShapeDtypeStruct((rank, rank), F32),
        ),
        scratch_shapes=[
            pltpu.VMEM(feedback.shape, BF16),
            pltpu.SemaphoreType.DMA((chunks,)),
            pltpu.VMEM(gathered.shape, BF16),
            pltpu.SemaphoreType.DMA((chunks,)),
        ],
        cost_estimate=cost(6 * rank * rows * (width + 3 * rank), 2 * feedback.size),
        compiler_params=PARAMS,
        name="right_products",
    )(half, own, other, grads, gathered, feedback)


def inverse_factor(gram):
    rank = gram.shape[0]

    def kernel(gram_ref, out_ref):
        row = lax.broadcasted_iota(jnp.int32, (rank, rank), 0)
        col = lax.broadcasted_iota(jnp.int32, (rank, rank), 1)
        work = jnp.concatenate([gram_ref[...], (row == col).astype(F32)], axis=1)
        index = lax.broadcasted_iota(jnp.int32, (rank, 1), 0)
        for k in range(rank):
            low = k // 8 * 8
            pivot_row = work[k : k + 1]
            scale = 1.0 / work[k : k + 1, k : k + 1]
            part = work[low:]
            factor = jnp.where(index[low:] > k, part[:, k : k + 1] * scale, 0.0)
            part = part - factor * pivot_row
            work = part if low == 0 else jnp.concatenate([work[:low], part], axis=0)
        diagonal = jnp.sum(jnp.where(row == col, work[:, :rank], 0.0), axis=1, keepdims=True)
        out_ref[...] = work[:, rank:] / jnp.sqrt(diagonal)

    return pl.pallas_call(
        kernel,
        out_shape=jax.ShapeDtypeStruct((rank, rank), F32),
        cost_estimate=cost(2 * rank * rank * rank * 8, 8 * rank * rank),
        compiler_params=PARAMS,
        name="inverse_factor",
    )(gram)


def finish(place, half, inverse, own, other, gathered, width):
    rank = inverse.shape[0]
    parts = gathered.shape[0]
    across = width // 256
    slab = 2 * LANES

    def kernel(place_ref, half_ref, inverse_ref, own_ref, other_ref, gathered_ref, dec_ref, right_ref):
        across_rows = [
            jnp.concatenate([gathered_ref[i + j] for j in range(across)], axis=1)
            for i in range(0, parts, across)
        ]
        right = nn(inverse_ref[...], jnp.concatenate(across_rows, axis=0), FULL)
        right_ref[...] = right
        odd = half_ref[0] == 1
        even_rows = jnp.where(odd, other_ref[0], own_ref[0])
        odd_rows = jnp.where(odd, own_ref[0], other_ref[0])
        basis = nn(inverse_ref[...], jnp.concatenate([even_rows, odd_rows], axis=1), FULL)
        dec_ref[...] = tn(basis, right, FULL).astype(BF16)

    block = pl.BlockSpec((1, rank, LANES), lambda i, place, half: (place[0], 0, 0))
    return pl.pallas_call(
        kernel,
        grid_spec=pltpu.PrefetchScalarGridSpec(
            num_scalar_prefetch=2,
            grid=(1,),
            in_specs=[
                pl.BlockSpec(inverse.shape, lambda i, place, half: (0, 0)),
                block,
                block,
                pl.BlockSpec(gathered.shape, lambda i, place, half: (0, 0, 0)),
            ],
            out_specs=[
                pl.BlockSpec((slab, width), lambda i, place, half: (0, 0)),
                pl.BlockSpec((rank, width), lambda i, place, half: (0, 0)),
            ],
        ),
        out_shape=(
            jax.ShapeDtypeStruct((slab, width), BF16),
            jax.ShapeDtypeStruct((rank, width), F32),
        ),
        cost_estimate=cost(12 * rank * slab * width, 4 * gathered.size),
        compiler_params=PARAMS,
        name="finish",
    )(place, half, inverse, own, other, gathered)


def exchange(value, axes):
    return lax.all_to_all(value, axes, 0, 0, tiled=True)


def in_hbm(value):
    return pltpu.with_memory_space_constraint(value, pltpu.HBM)


def index_of(axes):
    return lax.axis_index(axes).astype(jnp.int32).reshape(1)


def swapped(value):
    return lax.ppermute(value, "c", [(0, 1), (1, 0)])


def per_device(activations, grads_out, feedback, start_right):
    width = grads_out.shape[1]
    far, near = lax.axis_size("zh"), lax.axis_size("zl")
    outer = lax.axis_size(XY)
    half = index_of("c")
    place = jnp.concatenate([index_of("zh"), index_of("zl"), half])
    feedback = in_hbm(feedback)

    gathered = lax.all_gather(activations, ("zh", "zl", "c"), axis=0)
    columns = [activations] + [
        lax.ppermute(activations, "zl", [((i + j) % near, i) for i in range(near)])
        for j in range(1, near)
    ]
    keep, give, own, other = left_products(
        half, in_hbm(start_right.T), in_hbm(grads_out), feedback, 4
    )
    inner = added_copies(keep, swapped(give), far)
    inner = summed_copies(exchange(inner, "zh"), 1)[0]
    left = add_activations(place, (inner, swapped(inner)), columns, own, swapped(other))

    left = summed_copies(exchange(left, XY), near)
    left = summed_copies(exchange(left, "zl"), far)
    left = summed_copies(exchange(left, "zh"), outer)
    own = exchange(left, XY)
    other = swapped(own)

    right, gram = right_products(half, own, other, in_hbm(gathered), feedback, grads_out, 4, outer)
    inverse = inverse_factor(gram)
    right = summed_copies(exchange(right, XY), outer)
    right = exchange(right, XY)
    decompressed, right = finish(index_of(XY), half, inverse, own, other, right, width)
    return decompressed, right.T


def solution(mesh):
    outer, tp = mesh.shape["outer"], mesh.shape["tp"]
    across = 4 if outer == 16 else 2
    near = 4 if tp == 32 else 2
    names = ("x", "y", "zh", "zl", "c")
    shape = (outer // across, across, tp // (2 * near), near, 2)
    split_mesh = Mesh(mesh.devices.reshape(shape), names)
    z = ("zh", "zl", "c")
    return jax.shard_map(
        per_device,
        mesh=split_mesh,
        in_specs=(P(XY, z), P(XY, z), P(XY, z), P(z, None)),
        out_specs=(P(XY, z), P(z, None)),
        check_vma=False,
    )
```

time: 158 us -> 154 us (0.975)
  between operations: 0.78 us -> 14.2 us
  blocking collectives: 77.2 us -> 69.6 us
  local copies, waits for them, and re-layouts: 6.9 us -> 0.01 us
  starting transfers between devices: 42.8 us -> 38.2 us
    ppermute x5 -> x7, starting transfers between devices: 27.8 us -> 17.5 us  [the longest x3 9.2 us: per_device(): lax.ppermute(activations, 'zl', [((i + j) % near, i) for i in range(near)])]
    all_to_all x5, blocking collectives: 77.2 us -> 69.6 us  [exchange(): return lax.all_to_all(value, axes, 0, 0, tiled=True)]
    unnamed x14 -> x4, local copies, waits for them, and re-layouts: 6.9 us -> 0.01 us
    all_to_all x3 -> x2, starting transfers between devices: 15 us -> 20.7 us  [exchange(): return lax.all_to_all(value, axes, 0, 0, tiled=True)]
    ppermute x5 -> x7, waiting for transfers between devices: 4.09 us -> 2.97 us  [the longest x4 2.96 us: swapped(): return lax.ppermute(value, 'c', [(0, 1), (1, 0)])]
    pallas_call x7 -> x4, Pallas kernels: 9.31 us -> 10.1 us  [the longest x1 4.43 us: right_products(): pl.pallas_call(kernel, in_specs=whole_specs(3) + [pl.BlockSpec(memory_spa...]
    all_to_all x3 -> x2, waiting for transfers between devices: 7.48 us -> 8.21 us  [exchange(): return lax.all_to_all(value, axes, 0, 0, tiled=True)]
  transfers between devices with their start and end apart: 8 -> 10, of which waited for: 4 -> 4; matrix products, arithmetic and copies ran while one was open for 0% -> 0% of each run, Pallas kernels for 7% -> 7%
where the time goes in v3:
time: 154 us; the launch traced here: 152 us
  blocking collectives  69.6 us (45%)
  starting transfers between devices  38.2 us (25%)
  Pallas kernels  18 us (12%)
  between operations  14.2 us (9%)
  waiting for transfers between devices  11.9 us (8%)
    all_to_all x5, blocking collectives, exchange(): return lax.all_to_all(value, axes, 0, 0, tiled=True)  69.6 us
    all_to_all x2, starting transfers between devices, exchange(): return lax.all_to_all(value, axes, 0, 0, tiled=True)  20.7 us
    ppermute x3, starting transfers between devices, per_device(): lax.ppermute(activations, 'zl', [((i + j) % near, i) for i in range(near)])  9.2 us
    ppermute x4, starting transfers between devices, swapped(): return lax.ppermute(value, 'c', [(0, 1), (1, 0)])  8.29 us
    all_to_all x2, waiting for transfers between devices, exchange(): return lax.all_to_all(value, axes, 0, 0, tiled=True)  8.21 us
    pallas_call x1, Pallas kernels, inverse_factor(): pl.pallas_call(kernel, out_shape=jax.ShapeDtypeStruct((rank, rank), F32),...  5.46 us
    pallas_call x1, Pallas kernels, right_products(): pl.pallas_call(kernel, in_specs=whole_specs(3) + [pl.BlockSpec(memory_spa...  4.43 us
    pallas_call x1, Pallas kernels, left_products(): pl.pallas_call(kernel, in_specs=whole_specs(0) + [pl.BlockSpec(memory_spa...  4.23 us
  transfers between devices with their start and end apart: 10, of which 4 were waited for; matrix products, arithmetic and copies ran while one was open for 0% of the time, Pallas kernels for 7%

profile of v3, /device:TPU:6, one launch (start us, length us, event | category | flops | bytes accessed | tf_op | source)
XLA Modules:
  0.0 151.9 jit_solution(13636739850117889537)
XLA Ops:
  7.2 0.0 all-gather.3.cloned.1.call-start
  7.2 0.7 all-gather.3.cloned.1.call-update
  7.9 4.2 %left_products.1 = (f32[32,256]{1,0:T(8,128)S(1)}, f32[32,256]{1,0:T(8,128)S(1)}, f32[16,64,128]{2,1,0:T(8,128)S(1)}, f32[16,64,128]{2,1,0:T(8,128)S(1)}) custom-call(s32[1]{0:T(128)} %bitcast.1.half_ref, f32[64,512]{1,0:T(8,128)} %bitcast.11, bf16[256,512]{1,0:T(8,128)(2,1)} %grads_ref.3, bf16[4096,512]{1,0:T(8,128)(2,1)} %feed_ref.3), custom_call_target="tpu_custom_call" | custom-call | flops 805306368 | bytes 5242880 | tf_op jit(solution)/shard_map/left_products/pallas_call | solution.py:120
  12.1 0.0 copy-start
  12.2 2.1 %collective-permute-start = (f32[32,256]{1,0:T(8,128)S(1)}, f32[32,256]{1,0:T(8,128)S(1)}, u32[]{:S(2)}, u32[]{:S(2)}) collective-permute-start(f32[32,256]{1,0:T(8,128)S(1)} %get-tuple-element.11), channel_id=1, source_target_pairs={{0,1},{1,0},{2,3},{3,2},{4,5},{5,4},{6,7},{7,6},{8,9},{9,8},{10,11... | collective-permute-start | bytes 98312 | tf_op jit(solution)/shard_map/ppermute | solution.py:323
  14.2 2.4 %collective-permute-start.2 = (f32[16,64,128]{2,1,0:T(8,128)S(1)}, f32[16,64,128]{2,1,0:T(8,128)S(1)}, u32[]{:S(2)}, u32[]{:S(2)}) collective-permute-start(f32[16,64,128]{2,1,0:T(8,128)S(1)} %get-tuple-element.13), channel_id=1, source_target_pairs={{0,1},{1,0},{2,3},{3,2},{4,5},{5,4},{6,7},{7,6},{8,9},{9,8},{10,11... | collective-permute-start | bytes 1572872 | tf_op jit(solution)/shard_map/ppermute | solution.py:323
  16.6 0.0 collective-permute-done.two_ref
  16.6 0.7 added_copies.1
  17.3 15.1 %all-to-all-start = ((f32[4,32,256]{2,1,0:T(8,128)}), f32[4,32,256]{2,1,0:T(8,128)S(1)}, u32[]{:S(2)}, u32[]{:S(2)}) async-start(f32[4,32,256]{2,1,0:T(8,128)} %added_copies.1), calls=%async_computation | async-start | bytes 262144 | tf_op jit(solution)/shard_map/all_to_all | solution.py:311
  32.4 3.8 %collective-permute-start.3 = (bf16[256,128]{1,0:T(8,128)(2,1)S(1)}, bf16[256,128]{1,0:T(8,128)(2,1)S(1)}, u32[]{:S(2)}, u32[]{:S(2)}) collective-permute-start(bf16[256,128]{1,0:T(8,128)(2,1)S(1)} %copy-done.1), channel_id=1, source_target_pairs={{2,0},{4,2},{6,4},{0,6},{3,1},{5,3},{7,5},{1,7},{10,8},{12,10},{14... | collective-permute-start | bytes 196616 | tf_op jit(solution)/shard_map/ppermute | solution.py:336
  36.2 2.5 %collective-permute-start.4 = (bf16[256,128]{1,0:T(8,128)(2,1)S(1)}, bf16[256,128]{1,0:T(8,128)(2,1)S(1)}, u32[]{:S(2)}, u32[]{:S(2)}) collective-permute-start(bf16[256,128]{1,0:T(8,128)(2,1)S(1)} %copy-done.1), channel_id=1, source_target_pairs={{4,0},{6,2},{0,4},{2,6},{5,1},{7,3},{1,5},{3,7},{12,8},{14,10},{8,... | collective-permute-start | bytes 196616 | tf_op jit(solution)/shard_map/ppermute | solution.py:336
  38.7 2.9 %collective-permute-start.5 = (bf16[256,128]{1,0:T(8,128)(2,1)S(1)}, bf16[256,128]{1,0:T(8,128)(2,1)S(1)}, u32[]{:S(2)}, u32[]{:S(2)}) collective-permute-start(bf16[256,128]{1,0:T(8,128)(2,1)S(1)} %copy-done.1), channel_id=1, source_target_pairs={{6,0},{0,2},{2,4},{4,6},{7,1},{1,3},{3,5},{5,7},{14,8},{8,10},{10,... | collective-permute-start | bytes 196616 | tf_op jit(solution)/shard_map/ppermute | solution.py:336
  41.6 7.8 %all-to-all-done.shares_ref = f32[4,32,256]{2,1,0:T(8,128)S(1)} async-done(((f32[4,32,256]{2,1,0:T(8,128)}), f32[4,32,256]{2,1,0:T(8,128)S(1)}, u32[]{:S(2)}, u32[]{:S(2)}) %all-to-all-start) | async-done | bytes 131104 | tf_op jit(solution)/shard_map/all_to_all | solution.py:311
  49.5 1.9 %collective-permute-start.1 = (f32[32,256]{1,0:T(8,128)S(1)}, f32[32,256]{1,0:T(8,128)S(1)}, u32[]{:S(2)}, u32[]{:S(2)}) collective-permute-start(f32[32,256]{1,0:T(8,128)S(1)} %bitcast.8), channel_id=1, source_target_pairs={{0,1},{1,0},{2,3},{3,2},{4,5},{5,4},{6,7},{7,6},{8,9},{9,8},{10,11... | collective-permute-start | bytes 98312 | tf_op jit(solution)/shard_map/ppermute | solution.py:323
  51.4 0.1 pad_add_fusion.place_ref
  51.5 0.0 collective-permute-done.3.refs_1_
  51.5 1.1 collective-permute-done.1.inner_other_ref
  52.6 0.0 collective-permute-done.2.other_ref
  52.6 0.8 add_activations.1
  53.3 16.8 %all_to_all.35.shares_ref = f32[16,64,128]{2,1,0:T(8,128)S(1)} all-to-all(f32[16,64,128]{2,1,0:T(8,128)S(1)} %add_activations.1), channel_id=1, replica_groups=mesh['x'=4,'y'=4,'zh'=4,'zl'=4,'c'=2] {'x','y'}, dimensions={0} | all-to-all | bytes 1048576 | tf_op jit(solution)/shard_map/all_to_all | solution.py:311
  70.1 10.3 %all_to_all.36.shares_ref = f32[4,64,128]{2,1,0:T(8,128)S(1)} all-to-all(f32[4,64,128]{2,1,0:T(8,128)S(1)} %summed_copies.6), channel_id=1, replica_groups=mesh['x'=4,'y'=4,'zh'=4,'zl'=4,'c'=2] {'zl'}, dimensions={0} | all-to-all | bytes 262144 | tf_op jit(solution)/shard_map/all_to_all | solution.py:311
  80.5 18.4 %all_to_all.37.shares_ref = f32[4,64,128]{2,1,0:T(8,128)S(1)} all-to-all(f32[4,64,128]{2,1,0:T(8,128)S(1)} %summed_copies.7), channel_id=1, replica_groups=mesh['x'=4,'y'=4,'zh'=4,'zl'=4,'c'=2] {'zh'}, dimensions={0} | all-to-all | bytes 262144 | tf_op jit(solution)/shard_map/all_to_all | solution.py:311
  98.9 12.9 %all_to_all.38.own_ref = f32[16,64,128]{2,1,0:T(8,128)S(1)} all-to-all(f32[16,64,128]{2,1,0:T(8,128)S(1)} %summed_copies.8), channel_id=1, replica_groups=mesh['x'=4,'y'=4,'zh'=4,'zl'=4,'c'=2] {'x','y'}, dimensions={0} | all-to-all | bytes 1048576 | tf_op jit(solution)/shard_map/all_to_all | solution.py:311
  111.9 1.9 %collective-permute-start.6 = (f32[16,64,128]{2,1,0:T(8,128)S(1)}, f32[16,64,128]{2,1,0:T(8,128)S(1)}, u32[]{:S(2)}, u32[]{:S(2)}) collective-permute-start(f32[16,64,128]{2,1,0:T(8,128)S(1)} %all_to_all.38.own_ref), channel_id=1, source_target_pairs={{0,1},{1,0},{2,3},{3,2},{4,5},{5,4},{6,7},{7,6},{8,9},{9,8},{10,11... | collective-permute-start | bytes 1572872 | tf_op jit(solution)/shard_map/ppermute | solution.py:323
  113.8 1.9 %collective-permute-done.6.other_ref = f32[16,64,128]{2,1,0:T(8,128)S(1)} collective-permute-done((f32[16,64,128]{2,1,0:T(8,128)S(1)}, f32[16,64,128]{2,1,0:T(8,128)S(1)}, u32[]{:S(2)}, u32[]{:S(2)}) %collective-permute-start.6) | collective-permute-done | bytes 524320 | tf_op jit(solution)/shard_map/ppermute | solution.py:323
  115.7 4.4 %right_products.1 = (f32[16,8,256]{2,1,0:T(8,128)S(1)}, f32[64,64]{1,0:T(8,128)S(1)}) custom-call(s32[1]{0:T(128)} %bitcast.1.half_ref, f32[16,64,128]{2,1,0:T(8,128)S(1)} %all_to_all.38.own_ref, f32[16,64,128]{2,1,0:T(8,128)S(1)} %collective-permute-done.6.other_ref, bf16[256,512]{1,0:T(8,128)(2,1)S(1)} %copy-done, bf16[32,256,128]{2,1,0:T(8,128)(2,1)} %bitcast.10, ...), custom_call_target="tpu_custom_call" | custom-call | flops 1107296256 | bytes 4194304 | tf_op jit(solution)/shard_map/right_products/pallas_call | solution.py:217
  120.1 11.2 %all_to_all.39.shares_ref = f32[16,8,256]{2,1,0:T(8,128)S(1)} all-to-all(f32[16,8,256]{2,1,0:T(8,128)S(1)} %get-tuple-element.15), channel_id=1, replica_groups=mesh['x'=4,'y'=4,'zh'=4,'zl'=4,'c'=2] {'x','y'}, dimensions={0} | all-to-all | bytes 262144 | tf_op jit(solution)/shard_map/all_to_all | solution.py:311
  131.2 0.7 summed_copies.9
  131.9 5.6 %all-to-all-start.6 = ((f32[16,8,256]{2,1,0:T(8,128)}), f32[16,8,256]{2,1,0:T(8,128)S(1)}, u32[]{:S(2)}, u32[]{:S(2)}) async-start(f32[16,8,256]{2,1,0:T(8,128)} %summed_copies.9), calls=%async_computation.6 | async-start | bytes 262144 | tf_op jit(solution)/shard_map/all_to_all | solution.py:311
  137.5 5.5 %inverse_factor.1.inverse_ref = f32[64,64]{1,0:T(8,128)S(1)} custom-call(f32[64,64]{1,0:T(8,128)S(1)} %get-tuple-element.14.gram_ref), custom_call_target="tpu_custom_call" | custom-call | flops 4194304 | bytes 32768 | tf_op jit(solution)/shard_map/inverse_factor/pallas_call | solution.py:255
  143.0 0.4 all-to-all-done.6.gathered_ref
  143.4 1.7 %finish.1 = (bf16[256,512]{1,0:T(8,128)(2,1)}, f32[64,512]{1,0:T(8,128)}) custom-call(s32[1]{0:T(128)} %bitcast.place_ref, s32[1]{0:T(128)} %bitcast.1.half_ref, f32[64,64]{1,0:T(8,128)S(1)} %inverse_factor.1.inverse_ref, f32[16,64,128]{2,1,0:T(8,128)S(1)} %all_to_all.38.own_ref, f32[16,64,128]{2,1,0:T(8,128)S(1)} %collective-permute-done.6.other_ref, ...), custom_call_target="tpu_custom_call" | custom-call | flops 100663296 | bytes 131072 | tf_op jit(solution)/shard_map/finish/pallas_call | solution.py:284
  (10 shorter events, 0.1 us)
Async XLA Ops:
  7.2 25.2 %copy-start.1 = (bf16[256,128]{1,0:T(8,128)(2,1)S(1)}, bf16[256,128]{1,0:T(8,128)(2,1)}, u32[]{:S(2)}) copy-start(bf16[256,128]{1,0:T(8,128)(2,1)} %refs_0_.1) | copy-start | bytes 196612
  7.2 108.5 %all-gather.3.cloned.1.call-start = ((), (), s32[]{:S(2)}) async-start(), calls=%async_computation.7 | async-start | bytes 2162688 | tf_op jit(solution)/shard_map/all_gather | solution.py:334
  12.1 103.5 %copy-start = (bf16[256,512]{1,0:T(8,128)(2,1)S(1)}, bf16[256,512]{1,0:T(8,128)(2,1)}, u32[]{:S(2)}) copy-start(bf16[256,512]{1,0:T(8,128)(2,1)} %grads_ref.3) | copy-start | bytes 786436
  12.2 4.5 %collective-permute-start = (f32[32,256]{1,0:T(8,128)S(1)}, f32[32,256]{1,0:T(8,128)S(1)}, u32[]{:S(2)}, u32[]{:S(2)}) collective-permute-start(f32[32,256]{1,0:T(8,128)S(1)} %get-tuple-element.11), channel_id=1, source_target_pairs={{0,1},{1,0},{2,3},{3,2},{4,5},{5,4},{6,7},{7,6},{8,9},{9,8},{10,11... | collective-permute-start | bytes 98312 | tf_op jit(solution)/shard_map/ppermute | solution.py:323
  14.2 38.3 %collective-permute-start.2 = (f32[16,64,128]{2,1,0:T(8,128)S(1)}, f32[16,64,128]{2,1,0:T(8,128)S(1)}, u32[]{:S(2)}, u32[]{:S(2)}) collective-permute-start(f32[16,64,128]{2,1,0:T(8,128)S(1)} %get-tuple-element.13), channel_id=1, source_target_pairs={{0,1},{1,0},{2,3},{3,2},{4,5},{5,4},{6,7},{7,6},{8,9},{9,8},{10,11... | collective-permute-start | bytes 1572872 | tf_op jit(solution)/shard_map/ppermute | solution.py:323
  17.3 32.1 %all-to-all-start = ((f32[4,32,256]{2,1,0:T(8,128)}), f32[4,32,256]{2,1,0:T(8,128)S(1)}, u32[]{:S(2)}, u32[]{:S(2)}) async-start(f32[4,32,256]{2,1,0:T(8,128)} %added_copies.1), calls=%async_computation | async-start | bytes 262144 | tf_op jit(solution)/shard_map/all_to_all | solution.py:311
  32.4 19.1 %collective-permute-start.3 = (bf16[256,128]{1,0:T(8,128)(2,1)S(1)}, bf16[256,128]{1,0:T(8,128)(2,1)S(1)}, u32[]{:S(2)}, u32[]{:S(2)}) collective-permute-start(bf16[256,128]{1,0:T(8,128)(2,1)S(1)} %copy-done.1), channel_id=1, source_target_pairs={{2,0},{4,2},{6,4},{0,6},{3,1},{5,3},{7,5},{1,7},{10,8},{12,10},{14... | collective-permute-start | bytes 196616 | tf_op jit(solution)/shard_map/ppermute | solution.py:336
  36.2 15.2 %collective-permute-start.4 = (bf16[256,128]{1,0:T(8,128)(2,1)S(1)}, bf16[256,128]{1,0:T(8,128)(2,1)S(1)}, u32[]{:S(2)}, u32[]{:S(2)}) collective-permute-start(bf16[256,128]{1,0:T(8,128)(2,1)S(1)} %copy-done.1), channel_id=1, source_target_pairs={{4,0},{6,2},{0,4},{2,6},{5,1},{7,3},{1,5},{3,7},{12,8},{14,10},{8,... | collective-permute-start | bytes 196616 | tf_op jit(solution)/shard_map/ppermute | solution.py:336
  38.7 12.8 %collective-permute-start.5 = (bf16[256,128]{1,0:T(8,128)(2,1)S(1)}, bf16[256,128]{1,0:T(8,128)(2,1)S(1)}, u32[]{:S(2)}, u32[]{:S(2)}) collective-permute-start(bf16[256,128]{1,0:T(8,128)(2,1)S(1)} %copy-done.1), channel_id=1, source_target_pairs={{6,0},{0,2},{2,4},{4,6},{7,1},{1,3},{3,5},{5,7},{14,8},{8,10},{10,... | collective-permute-start | bytes 196616 | tf_op jit(solution)/shard_map/ppermute | solution.py:336
  49.5 3.1 %collective-permute-start.1 = (f32[32,256]{1,0:T(8,128)S(1)}, f32[32,256]{1,0:T(8,128)S(1)}, u32[]{:S(2)}, u32[]{:S(2)}) collective-permute-start(f32[32,256]{1,0:T(8,128)S(1)} %bitcast.8), channel_id=1, source_target_pairs={{0,1},{1,0},{2,3},{3,2},{4,5},{5,4},{6,7},{7,6},{8,9},{9,8},{10,11... | collective-permute-start | bytes 98312 | tf_op jit(solution)/shard_map/ppermute | solution.py:323
  111.9 3.8 %collective-permute-start.6 = (f32[16,64,128]{2,1,0:T(8,128)S(1)}, f32[16,64,128]{2,1,0:T(8,128)S(1)}, u32[]{:S(2)}, u32[]{:S(2)}) collective-permute-start(f32[16,64,128]{2,1,0:T(8,128)S(1)} %all_to_all.38.own_ref), channel_id=1, source_target_pairs={{0,1},{1,0},{2,3},{3,2},{4,5},{5,4},{6,7},{7,6},{8,9},{9,8},{10,11... | collective-permute-start | bytes 1572872 | tf_op jit(solution)/shard_map/ppermute | solution.py:323
  131.9 11.4 %all-to-all-start.6 = ((f32[16,8,256]{2,1,0:T(8,128)}), f32[16,8,256]{2,1,0:T(8,128)S(1)}, u32[]{:S(2)}, u32[]{:S(2)}) async-start(f32[16,8,256]{2,1,0:T(8,128)} %summed_copies.9), calls=%async_computation.6 | async-start | bytes 262144 | tf_op jit(solution)/shard_map/all_to_all | solution.py:311
Sparse Core Ops, SparseCore 0:
  10.1 79.4 all-gather.2

commit v4 on v3

--- a/solution.py
+++ b/solution.py
@@ -46,19 +46,30 @@
     return pl.CostEstimate(flops=flops, bytes_accessed=count, transcendentals=0)
 
 
-def kept_and_given(odd, value):
-    half = value.shape[0] // 2
-    first, second = value[:half], value[half:]
-    return jnp.where(odd, second, first), jnp.where(odd, first, second)
-
-
-def joined(odd, own, other):
-    return jnp.concatenate([jnp.where(odd, other, own), jnp.where(odd, own, other)], axis=0)
-
-
 def whole_specs(count):
     scalar = pl.BlockSpec(memory_space=pltpu.SMEM)
     return [scalar] + [pl.BlockSpec(memory_space=pltpu.VMEM)] * count
+
+
+def copied(value, copies):
+    def kernel(value_ref, out_ref, sems):
+        started = [
+            pltpu.make_async_copy(value_ref, out_ref.at[i], sems.at[i]) for i in range(copies)
+        ]
+        for copy in started:
+            copy.start()
+        for copy in started:
+            copy.wait()
+
+    return pl.pallas_call(
+        kernel,
+        in_specs=[pl.BlockSpec(memory_space=pltpu.HBM)],
+        out_shape=jax.ShapeDtypeStruct((copies,) + value.shape, value.dtype),
+        scratch_shapes=[pltpu.SemaphoreType.DMA((copies,))],
+        cost_estimate=cost(0, 2 * value.size * (1 + copies)),
+        compiler_params=PARAMS,
+        name="copied",
+    )(value)
 
 
 def added_copies(one, two, copies):
@@ -73,6 +84,19 @@
         cost_estimate=cost(one.size, 4 * one.size * (2 + copies)),
         compiler_params=PARAMS,
         name="added_copies",
+    )(one, two)
+
+
+def added(one, two):
+    def kernel(one_ref, two_ref, out_ref):
+        out_ref[...] = one_ref[...] + two_ref[...]
+
+    return pl.pallas_call(
+        kernel,
+        out_shape=jax.ShapeDtypeStruct(one.shape, F32),
+        cost_estimate=cost(one.size, 12 * one.size),
+        compiler_params=PARAMS,
+        name="added",
     )(one, two)
 
 
@@ -92,7 +116,7 @@
     pairs = rows // (2 * LANES * chunks)
 
     def kernel(half_ref, start_ref, grads_ref, feed_ref, *refs):
-        keep_ref, give_ref, own_ref, other_ref, held, sems, start, held_grads, few = refs
+        inner_ref, own_ref, other_ref, held, sems, start, held_grads, few = refs
         first = [
             pltpu.make_async_copy(start_ref, start, few.at[0]),
             pltpu.make_async_copy(grads_ref, held_grads, few.at[1]),
@@ -104,7 +128,7 @@
         first[0].wait()
         split = pieces(start[...])
         first[1].wait()
-        keep_ref[...], give_ref[...] = kept_and_given(odd, folded(nt(split, held_grads[...])))
+        inner_ref[...] = folded(nt(split, held_grads[...]))
         for k in range(chunks):
             copies[k].wait()
             part = held[k * (rows // chunks) : (k + 1) * (rows // chunks)]
@@ -115,12 +139,12 @@
                 own_ref[k * pairs + i] = jnp.where(odd, odd_rows, even_rows)
                 other_ref[k * pairs + i] = jnp.where(odd, even_rows, odd_rows)
 
-    small = jax.ShapeDtypeStruct((rank // 2, tokens), F32)
+    small = jax.ShapeDtypeStruct((rank, tokens), F32)
     large = jax.ShapeDtypeStruct((rows // (2 * LANES), rank, LANES), F32)
     return pl.pallas_call(
         kernel,
         in_specs=whole_specs(0) + [pl.BlockSpec(memory_space=pltpu.HBM)] * 3,
-        out_shape=(small, small, large, large),
+        out_shape=(small, large, large),
         scratch_shapes=[
             pltpu.VMEM(feedback.shape, BF16),
             pltpu.SemaphoreType.DMA((chunks,)),
@@ -135,28 +159,30 @@
 
 
 def add_activations(place, inner, columns, own, other):
-    near_size, tokens = len(columns), columns[0].shape[0]
+    far_size, tokens, _ = columns.shape
     blocks, rank, _ = own.shape
 
-    def kernel(place_ref, inner_ref, inner_other_ref, own_ref, other_ref, *refs):
-        column_refs, out_ref = refs[:-1], refs[-1]
+    def kernel(place_ref, columns_ref, own_ref, other_ref, *refs):
+        inner_refs, out_ref = refs[:-1], refs[-1]
         for i in range(blocks):
             out_ref[i] = own_ref[i] + other_ref[i]
-        total = joined(place_ref[2] == 1, inner_ref[...], inner_other_ref[...])
-        across = jnp.concatenate([ref[...] for ref in column_refs], axis=1)
+        total = inner_refs[0][...]
+        for ref in inner_refs[1:]:
+            total = total + ref[...]
+        across = jnp.concatenate([columns_ref[i] for i in range(far_size)], axis=1)
         extra = folded(nn(pieces(total), across))
-        for i in range(near_size):
-            block = place_ref[0] * near_size + lax.rem(place_ref[1] + i, near_size)
+        for i in range(far_size):
+            block = i * (blocks // far_size) + place_ref[0]
             out_ref[block] = out_ref[block] + extra[:, i * LANES : (i + 1) * LANES]
 
     return pl.pallas_call(
         kernel,
-        in_specs=whole_specs(4 + near_size),
+        in_specs=whole_specs(3 + len(inner)),
         out_shape=jax.ShapeDtypeStruct(own.shape, F32),
         cost_estimate=cost(24 * rank * tokens * LANES, 12 * own.size),
         compiler_params=PARAMS,
         name="add_activations",
-    )(place, *inner, own, other, *columns)
+    )(place, columns, own, other, *inner)
 
 
 def summed_copies(shares, copies):
@@ -178,22 +204,34 @@
     )(shares)
 
 
-def right_products(half, own, other, gathered, feedback, grads, chunks, parts):
+def inner_products(near, left, columns):
+    blocks, rank, _ = left.shape
+    far_size, tokens, _ = columns.shape
+
+    def kernel(near_ref, left_ref, columns_ref, out_ref):
+        rows = [left_ref[i * (blocks // far_size) + near_ref[0]] for i in range(far_size)]
+        across = jnp.concatenate([columns_ref[i] for i in range(far_size)], axis=1)
+        out_ref[...] = folded(nt(pieces(jnp.concatenate(rows, axis=1)), across))
+
+    return pl.pallas_call(
+        kernel,
+        in_specs=whole_specs(2),
+        out_shape=jax.ShapeDtypeStruct((rank, tokens), F32),
+        cost_estimate=cost(6 * rank * tokens * far_size * LANES, 2 * columns.size),
+        compiler_params=PARAMS,
+        name="inner_products",
+    )(near, left, columns)
+
+
+def feedback_right(half, own, other, feedback, chunks):
     blocks, rank, _ = own.shape
     rows, width = feedback.shape
-    tokens = grads.shape[0]
     pairs = blocks // chunks
-    split_rows = rank * width // (256 * parts)
-    across = width // 256
-
-    def kernel(
-        half_ref, own_ref, other_ref, grads_ref, act_ref, feed_ref, out_ref, gram_ref, held, sems, act, act_sems
-    ):
-        act_copies = fetched(act_ref, act, act_sems)
+
+    def kernel(half_ref, own_ref, other_ref, feed_ref, out_ref, gram_ref, held, sems):
         copies = fetched(feed_ref, held, sems)
         odd = half_ref[0] == 1
         right = jnp.zeros((rank, width), F32)
-        inner = jnp.zeros((rank, tokens), F32)
         square = jnp.zeros((rank, 3 * rank), F32)
         for k in range(chunks):
             row_blocks = []
@@ -202,35 +240,48 @@
                 row_blocks.append(jnp.where(odd, own_ref[i], other_ref[i]))
             split = pieces(jnp.concatenate(row_blocks, axis=1))
             square = square + folded(nt(split, split))
-            act_copies[k].wait()
-            columns = [act[i] for i in range(2 * k * pairs, 2 * (k + 1) * pairs)]
-            inner = inner + folded(nt(split, jnp.concatenate(columns, axis=1)))
             copies[k].wait()
             part = held[k * (rows // chunks) : (k + 1) * (rows // chunks)]
             right = right + folded(nn(split, part))
-        right = right + folded(nn(pieces(inner), grads_ref[...]))
+        out_ref[...] = right
+        gram_ref[...] = square[:, :rank] + square[:, rank : 2 * rank] + square[:, 2 * rank :]
+
+    return pl.pallas_call(
+        kernel,
+        in_specs=whole_specs(2) + [pl.BlockSpec(memory_space=pltpu.HBM)],
+        out_shape=(
+            jax.ShapeDtypeStruct((rank, width), F32),
+            jax.ShapeDtypeStruct((rank, rank), F32),
+        ),
+        scratch_shapes=[pltpu.VMEM(feedback.shape, BF16), pltpu.SemaphoreType.DMA((chunks,))],
+        cost_estimate=cost(6 * rank * rows * (width + 3 * rank), 2 * feedback.size),
+        compiler_params=PARAMS,
+        name="feedback_right",
+    )(half, own, other, feedback)
+
+
+def add_grads(shares, grads, partial, parts):
+    ways, rank, tokens = shares.shape
+    width = grads.shape[1]
+    split_rows = rank * width // (256 * parts)
+    across = width // 256
+
+    def kernel(shares_ref, grads_ref, partial_ref, out_ref):
+        inner = shares_ref[0]
+        for i in range(1, ways):
+            inner = inner + shares_ref[i]
+        total = partial_ref[...] + folded(nn(pieces(inner), grads_ref[...]))
         for i in range(parts):
             down, over = i // across * split_rows, i % across * 256
-            out_ref[i] = right[down : down + split_rows, over : over + 256]
-        gram_ref[...] = square[:, :rank] + square[:, rank : 2 * rank] + square[:, 2 * rank :]
-
-    return pl.pallas_call(
-        kernel,
-        in_specs=whole_specs(3) + [pl.BlockSpec(memory_space=pltpu.HBM)] * 2,
-        out_shape=(
-            jax.ShapeDtypeStruct((parts, split_rows, 256), F32),
-            jax.ShapeDtypeStruct((rank, rank), F32),
-        ),
-        scratch_shapes=[
-            pltpu.VMEM(feedback.shape, BF16),
-            pltpu.SemaphoreType.DMA((chunks,)),
-            pltpu.VMEM(gathered.shape, BF16),
-            pltpu.SemaphoreType.DMA((chunks,)),
-        ],
-        cost_estimate=cost(6 * rank * rows * (width + 3 * rank), 2 * feedback.size),
-        compiler_params=PARAMS,
-        name="right_products",
-    )(half, own, other, grads, gathered, feedback)
+            out_ref[i] = total[down : down + split_rows, over : over + 256]
+
+    return pl.pallas_call(
+        kernel,
+        out_shape=jax.ShapeDtypeStruct((parts, split_rows, 256), F32),
+        cost_estimate=cost(6 * rank * tokens * width, 4 * shares.size + 2 * grads.size),
+        compiler_params=PARAMS,
+        name="add_grads",
+    )(shares, grads, partial)
 
 
 def inverse_factor(gram):
@@ -328,20 +379,18 @@
     far, near = lax.axis_size("zh"), lax.axis_size("zl")
     outer = lax.axis_size(XY)
     half = index_of("c")
-    place = jnp.concatenate([index_of("zh"), index_of("zl"), half])
     feedback = in_hbm(feedback)
 
-    gathered = lax.all_gather(activations, ("zh", "zl", "c"), axis=0)
-    columns = [activations] + [
-        lax.ppermute(activations, "zl", [((i + j) % near, i) for i in range(near)])
+    columns = exchange(copied(in_hbm(activations), far), "zh")
+    inner, own, other = left_products(
+        half, in_hbm(start_right.T), in_hbm(grads_out), feedback, 4
+    )
+    inner = added(inner, swapped(inner))
+    inner = [inner] + [
+        lax.ppermute(inner, "zl", [((i + j) % near, i) for i in range(near)])
         for j in range(1, near)
     ]
-    keep, give, own, other = left_products(
-        half, in_hbm(start_right.T), in_hbm(grads_out), feedback, 4
-    )
-    inner = added_copies(keep, swapped(give), far)
-    inner = summed_copies(exchange(inner, "zh"), 1)[0]
-    left = add_activations(place, (inner, swapped(inner)), columns, own, swapped(other))
+    left = add_activations(index_of("zl"), inner, columns, own, swapped(other))
 
     left = summed_copies(exchange(left, XY), near)
     left = summed_copies(exchange(left, "zl"), far)
@@ -349,7 +398,10 @@
     own = exchange(left, XY)
     other = swapped(own)
 
-    right, gram = right_products(half, own, other, in_hbm(gathered), feedback, grads_out, 4, outer)
+    inner = inner_products(index_of("zl"), own, columns)
+    inner = exchange(added_copies(inner, swapped(inner), near), "zl")
+    right, gram = feedback_right(half, own, other, feedback, 4)
+    right = add_grads(inner, grads_out, right, outer)
     inverse = inverse_factor(gram)
     right = summed_copies(exchange(right, XY), outer)
     right = exchange(right, XY)

time: 154 us -> 148 us (0.961)
  between operations: 14.2 us -> 0.78 us
  blocking collectives: 69.6 us -> 73.6 us
  starting transfers between devices: 38.2 us -> 41.8 us
    all_to_all x2 -> x3, waiting for transfers between devices: 8.21 us -> 2.59 us  [exchange(): return lax.all_to_all(value, axes, 0, 0, tiled=True)]
    ppermute x3, waiting for transfers between devices: 0.01 us -> 5.01 us  [per_device(): lax.ppermute(inner, 'zl', [((i + j) % near, i) for i in range(near)])]
    all_to_all x5, blocking collectives: 69.6 us -> 73.6 us  [exchange(): return lax.all_to_all(value, axes, 0, 0, tiled=True)]
    all_to_all x2 -> x3, starting transfers between devices: 20.7 us -> 24.4 us  [exchange(): return lax.all_to_all(value, axes, 0, 0, tiled=True)]
    pallas_call x2 -> x6, Pallas kernels: 5.19 us -> 5.66 us  [the longest x1 3.26 us: feedback_right(): pl.pallas_call(kernel, in_specs=whole_specs(2) + [pl.BlockSpec(memory_spa...]
  transfers between devices with their start and end apart: 10 -> 10, of which waited for: 4 -> 7; matrix products, arithmetic and copies ran while one was open for 0% -> 0% of each run, Pallas kernels for 7% -> 9%
where the time goes in v4:
time: 148 us; the launch traced here: 146 us
  blocking collectives  73.6 us (50%)
  starting transfers between devices  41.8 us (28%)
  Pallas kernels  18.5 us (12%)
  waiting for transfers between devices  11.6 us (8%)
    all_to_all x5, blocking collectives, exchange(): return lax.all_to_all(value, axes, 0, 0, tiled=True)  73.6 us
    all_to_all x3, starting transfers between devices, exchange(): return lax.all_to_all(value, axes, 0, 0, tiled=True)  24.4 us
    ppermute x3, starting transfers between devices, per_device(): lax.ppermute(inner, 'zl', [((i + j) % near, i) for i in range(near)])  9.23 us
    ppermute x4, starting transfers between devices, swapped(): return lax.ppermute(value, 'c', [(0, 1), (1, 0)])  8.16 us
    pallas_call x1, Pallas kernels, inverse_factor(): pl.pallas_call(kernel, out_shape=jax.ShapeDtypeStruct((rank, rank), F32),...  5.46 us
    ppermute x3, waiting for transfers between devices, per_device(): lax.ppermute(inner, 'zl', [((i + j) % near, i) for i in range(near)])  5.01 us
    pallas_call x1, Pallas kernels, left_products(): pl.pallas_call(kernel, in_specs=whole_specs(0) + [pl.BlockSpec(memory_spa...  4.22 us
    ppermute x4, waiting for transfers between devices, swapped(): return lax.ppermute(value, 'c', [(0, 1), (1, 0)])  3.98 us
  transfers between devices with their start and end apart: 10, of which 7 were waited for; matrix products, arithmetic and copies ran while one was open for 0% of the time, Pallas kernels for 9%

profile of v4, /device:TPU:6, one launch (start us, length us, event | category | flops | bytes accessed | tf_op | source)
XLA Modules:
  0.0 146.2 jit_solution(10745370902603638140)
XLA Ops:
  0.6 1.7 %copied.1 = bf16[4,256,128]{2,1,0:T(8,128)(2,1)} custom-call(bf16[256,128]{1,0:T(8,128)(2,1)} %value_ref.1), custom_call_target="tpu_custom_call" | custom-call | bytes 327680 | tf_op jit(solution)/shard_map/copied/pallas_call | solution.py:64
  2.4 15.1 %all-to-all-start = ((bf16[4,256,128]{2,1,0:T(8,128)(2,1)}), bf16[4,256,128]{2,1,0:T(8,128)(2,1)S(1)}, u32[]{:S(2)}, u32[]{:S(2)}) async-start(bf16[4,256,128]{2,1,0:T(8,128)(2,1)} %copied.1), calls=%async_computation | async-start | bytes 524288 | tf_op jit(solution)/shard_map/all_to_all | solution.py:362
  17.5 4.2 %left_products.1 = (f32[64,256]{1,0:T(8,128)S(1)}, f32[16,64,128]{2,1,0:T(8,128)S(1)}, f32[16,64,128]{2,1,0:T(8,128)S(1)}) custom-call(s32[1]{0:T(128)} %bitcast.1.half_ref, f32[64,512]{1,0:T(8,128)} %bitcast.5, bf16[256,512]{1,0:T(8,128)(2,1)} %grads_ref.3, bf16[4096,512]{1,0:T(8,128)(2,1)} %feed_ref.3), custom_call_target="tpu_custom_call" | custom-call | flops 805306368 | bytes 5242880 | tf_op jit(solution)/shard_map/left_products/pallas_call | solution.py:144
  21.7 1.9 %collective-permute-start = (f32[16,64,128]{2,1,0:T(8,128)S(1)}, f32[16,64,128]{2,1,0:T(8,128)S(1)}, u32[]{:S(2)}, u32[]{:S(2)}) collective-permute-start(f32[16,64,128]{2,1,0:T(8,128)S(1)} %get-tuple-element.10), channel_id=1, source_target_pairs={{0,1},{1,0},{2,3},{3,2},{4,5},{5,4},{6,7},{7,6},{8,9},{9,8},{10,11... | collective-permute-start | bytes 1572872 | tf_op jit(solution)/shard_map/ppermute | solution.py:374
  23.6 2.4 %collective-permute-start.1 = (f32[64,256]{1,0:T(8,128)S(1)}, f32[64,256]{1,0:T(8,128)S(1)}, u32[]{:S(2)}, u32[]{:S(2)}) collective-permute-start(f32[64,256]{1,0:T(8,128)S(1)} %get-tuple-element.11.one_ref), channel_id=1, source_target_pairs={{0,1},{1,0},{2,3},{3,2},{4,5},{5,4},{6,7},{7,6},{8,9},{9,8},{10,11... | collective-permute-start | bytes 196616 | tf_op jit(solution)/shard_map/ppermute | solution.py:374
  26.0 0.9 collective-permute-done.1.two_ref
  26.9 3.8 %collective-permute-start.2 = (f32[64,256]{1,0:T(8,128)S(1)}, f32[64,256]{1,0:T(8,128)S(1)}, u32[]{:S(2)}, u32[]{:S(2)}) collective-permute-start(f32[64,256]{1,0:T(8,128)S(1)} %added.1.refs_0_), channel_id=1, source_target_pairs={{2,0},{4,2},{6,4},{0,6},{3,1},{5,3},{7,5},{1,7},{10,8},{12,10},{14... | collective-permute-start | bytes 196616 | tf_op jit(solution)/shard_map/ppermute | solution.py:390
  30.8 2.5 %collective-permute-start.3 = (f32[64,256]{1,0:T(8,128)S(1)}, f32[64,256]{1,0:T(8,128)S(1)}, u32[]{:S(2)}, u32[]{:S(2)}) collective-permute-start(f32[64,256]{1,0:T(8,128)S(1)} %added.1.refs_0_), channel_id=1, source_target_pairs={{4,0},{6,2},{0,4},{2,6},{5,1},{7,3},{1,5},{3,7},{12,8},{14,10},{8,... | collective-permute-start | bytes 196616 | tf_op jit(solution)/shard_map/ppermute | solution.py:390
  33.2 2.9 %collective-permute-start.4 = (f32[64,256]{1,0:T(8,128)S(1)}, f32[64,256]{1,0:T(8,128)S(1)}, u32[]{:S(2)}, u32[]{:S(2)}) collective-permute-start(f32[64,256]{1,0:T(8,128)S(1)} %added.1.refs_0_), channel_id=1, source_target_pairs={{6,0},{0,2},{2,4},{4,6},{7,1},{1,3},{3,5},{5,7},{14,8},{8,10},{10,... | collective-permute-start | bytes 196616 | tf_op jit(solution)/shard_map/ppermute | solution.py:390
  36.2 4.0 %collective-permute-done.3.refs_2_ = f32[64,256]{1,0:T(8,128)S(1)} collective-permute-done((f32[64,256]{1,0:T(8,128)S(1)}, f32[64,256]{1,0:T(8,128)S(1)}, u32[]{:S(2)}, u32[]{:S(2)}) %collective-permute-start.3) | collective-permute-done | bytes 65568 | tf_op jit(solution)/shard_map/ppermute | solution.py:390
  40.2 1.0 collective-permute-done.4.refs_3_
  41.2 0.2 add_activations.1
  41.4 15.9 %all_to_all.40.shares_ref = f32[16,64,128]{2,1,0:T(8,128)S(1)} all-to-all(f32[16,64,128]{2,1,0:T(8,128)S(1)} %add_activations.1), channel_id=1, replica_groups=mesh['x'=4,'y'=4,'zh'=4,'zl'=4,'c'=2] {'x','y'}, dimensions={0} | all-to-all | bytes 1048576 | tf_op jit(solution)/shard_map/all_to_all | solution.py:362
  57.3 8.6 %all_to_all.41.shares_ref = f32[4,64,128]{2,1,0:T(8,128)S(1)} all-to-all(f32[4,64,128]{2,1,0:T(8,128)S(1)} %summed_copies.4), channel_id=1, replica_groups=mesh['x'=4,'y'=4,'zh'=4,'zl'=4,'c'=2] {'zl'}, dimensions={0} | all-to-all | bytes 262144 | tf_op jit(solution)/shard_map/all_to_all | solution.py:362
  65.9 24.5 %all_to_all.42.shares_ref = f32[4,64,128]{2,1,0:T(8,128)S(1)} all-to-all(f32[4,64,128]{2,1,0:T(8,128)S(1)} %summed_copies.5), channel_id=1, replica_groups=mesh['x'=4,'y'=4,'zh'=4,'zl'=4,'c'=2] {'zh'}, dimensions={0} | all-to-all | bytes 262144 | tf_op jit(solution)/shard_map/all_to_all | solution.py:362
  90.5 13.5 %all_to_all.43.own_ref.left_ref = f32[16,64,128]{2,1,0:T(8,128)S(1)} all-to-all(f32[16,64,128]{2,1,0:T(8,128)S(1)} %summed_copies.6), channel_id=1, replica_groups=mesh['x'=4,'y'=4,'zh'=4,'zl'=4,'c'=2] {'x','y'}, dimensions={0} | all-to-all | bytes 1048576 | tf_op jit(solution)/shard_map/all_to_all | solution.py:362
  104.0 0.2 inner_products.1.one_ref
  104.3 1.9 %collective-permute-start.6 = (f32[64,256]{1,0:T(8,128)S(1)}, f32[64,256]{1,0:T(8,128)S(1)}, u32[]{:S(2)}, u32[]{:S(2)}) collective-permute-start(f32[64,256]{1,0:T(8,128)S(1)} %inner_products.1.one_ref), channel_id=1, source_target_pairs={{0,1},{1,0},{2,3},{3,2},{4,5},{5,4},{6,7},{7,6},{8,9},{9,8},{10,11... | collective-permute-start | bytes 196616 | tf_op jit(solution)/shard_map/ppermute | solution.py:374
  106.2 1.2 collective-permute-done.6.two_ref
  107.4 0.7 added_copies.1
  108.1 3.7 %all-to-all-start.5 = ((f32[4,64,256]{2,1,0:T(8,128)}), f32[4,64,256]{2,1,0:T(8,128)S(1)}, u32[]{:S(2)}, u32[]{:S(2)}) async-start(f32[4,64,256]{2,1,0:T(8,128)} %added_copies.1), calls=%async_computation.5 | async-start | bytes 524288 | tf_op jit(solution)/shard_map/all_to_all | solution.py:362
  111.8 1.9 %collective-permute-start.5 = (f32[16,64,128]{2,1,0:T(8,128)S(1)}, f32[16,64,128]{2,1,0:T(8,128)S(1)}, u32[]{:S(2)}, u32[]{:S(2)}) collective-permute-start(f32[16,64,128]{2,1,0:T(8,128)S(1)} %all_to_all.43.own_ref.left_ref), channel_id=1, source_target_pairs={{0,1},{1,0},{2,3},{3,2},{4,5},{5,4},{6,7},{7,6},{8,9},{9,8},{10,11... | collective-permute-start | bytes 1572872 | tf_op jit(solution)/shard_map/ppermute | solution.py:374
  113.7 1.9 %collective-permute-done.5.other_ref = f32[16,64,128]{2,1,0:T(8,128)S(1)} collective-permute-done((f32[16,64,128]{2,1,0:T(8,128)S(1)}, f32[16,64,128]{2,1,0:T(8,128)S(1)}, u32[]{:S(2)}, u32[]{:S(2)}) %collective-permute-start.5) | collective-permute-done | bytes 524320 | tf_op jit(solution)/shard_map/ppermute | solution.py:374
  115.6 3.3 %feedback_right.1 = (f32[64,512]{1,0:T(8,128)S(1)}, f32[64,64]{1,0:T(8,128)S(1)}) custom-call(s32[1]{0:T(128)} %bitcast.1.half_ref, f32[16,64,128]{2,1,0:T(8,128)S(1)} %all_to_all.43.own_ref.left_ref, f32[16,64,128]{2,1,0:T(8,128)S(1)} %collective-permute-done.5.other_ref, bf16[4096,512]{1,0:T(8,128)(2,1)} %feed_ref.3), custom_call_target="tpu_custom_call" | custom-call | flops 1107296256 | bytes 4194304 | tf_op jit(solution)/shard_map/feedback_right/pallas_call | solution.py:249
  118.9 2.2 %all-to-all-done.5.shares_ref = f32[4,64,256]{2,1,0:T(8,128)S(1)} async-done(((f32[4,64,256]{2,1,0:T(8,128)}), f32[4,64,256]{2,1,0:T(8,128)S(1)}, u32[]{:S(2)}, u32[]{:S(2)}) %all-to-all-start.5) | async-done | bytes 262176 | tf_op jit(solution)/shard_map/all_to_all | solution.py:362
  121.1 0.2 add_grads.1
  121.3 11.1 %all_to_all.44.shares_ref = f32[16,8,256]{2,1,0:T(8,128)S(1)} all-to-all(f32[16,8,256]{2,1,0:T(8,128)S(1)} %add_grads.1), channel_id=1, replica_groups=mesh['x'=4,'y'=4,'zh'=4,'zl'=4,'c'=2] {'x','y'}, dimensions={0} | all-to-all | bytes 262144 | tf_op jit(solution)/shard_map/all_to_all | solution.py:362
  132.4 0.7 summed_copies.7
  133.1 5.6 %all-to-all-start.7 = ((f32[16,8,256]{2,1,0:T(8,128)}), f32[16,8,256]{2,1,0:T(8,128)S(1)}, u32[]{:S(2)}, u32[]{:S(2)}) async-start(f32[16,8,256]{2,1,0:T(8,128)} %summed_copies.7), calls=%async_computation.7 | async-start | bytes 262144 | tf_op jit(solution)/shard_map/all_to_all | solution.py:362
  138.7 5.5 %inverse_factor.1.inverse_ref = f32[64,64]{1,0:T(8,128)S(1)} custom-call(f32[64,64]{1,0:T(8,128)S(1)} %get-tuple-element.12.gram_ref), custom_call_target="tpu_custom_call" | custom-call | flops 4194304 | bytes 32768 | tf_op jit(solution)/shard_map/inverse_factor/pallas_call | solution.py:306
  144.1 0.4 all-to-all-done.7.gathered_ref
  144.6 1.7 %finish.1 = (bf16[256,512]{1,0:T(8,128)(2,1)}, f32[64,512]{1,0:T(8,128)}) custom-call(s32[1]{0:T(128)} %bitcast.place_ref, s32[1]{0:T(128)} %bitcast.1.half_ref, f32[64,64]{1,0:T(8,128)S(1)} %inverse_factor.1.inverse_ref, f32[16,64,128]{2,1,0:T(8,128)S(1)} %all_to_all.43.own_ref.left_ref, f32[16,64,128]{2,1,0:T(8,128)S(1)} %collective-permute-done.5.other_ref, ...), custom_call_target="tpu_custom_call" | custom-call | flops 100663296 | bytes 131072 | tf_op jit(solution)/shard_map/finish/pallas_call | solution.py:335
  (9 shorter events, 0.1 us)
Async XLA Ops:
  2.4 38.8 %all-to-all-start = ((bf16[4,256,128]{2,1,0:T(8,128)(2,1)}), bf16[4,256,128]{2,1,0:T(8,128)(2,1)S(1)}, u32[]{:S(2)}, u32[]{:S(2)}) async-start(bf16[4,256,128]{2,1,0:T(8,128)(2,1)} %copied.1), calls=%async_computation | async-start | bytes 524288 | tf_op jit(solution)/shard_map/all_to_all | solution.py:362
  21.7 19.5 %collective-permute-start = (f32[16,64,128]{2,1,0:T(8,128)S(1)}, f32[16,64,128]{2,1,0:T(8,128)S(1)}, u32[]{:S(2)}, u32[]{:S(2)}) collective-permute-start(f32[16,64,128]{2,1,0:T(8,128)S(1)} %get-tuple-element.10), channel_id=1, source_target_pairs={{0,1},{1,0},{2,3},{3,2},{4,5},{5,4},{6,7},{7,6},{8,9},{9,8},{10,11... | collective-permute-start | bytes 1572872 | tf_op jit(solution)/shard_map/ppermute | solution.py:374
  23.6 3.3 %collective-permute-start.1 = (f32[64,256]{1,0:T(8,128)S(1)}, f32[64,256]{1,0:T(8,128)S(1)}, u32[]{:S(2)}, u32[]{:S(2)}) collective-permute-start(f32[64,256]{1,0:T(8,128)S(1)} %get-tuple-element.11.one_ref), channel_id=1, source_target_pairs={{0,1},{1,0},{2,3},{3,2},{4,5},{5,4},{6,7},{7,6},{8,9},{9,8},{10,11... | collective-permute-start | bytes 196616 | tf_op jit(solution)/shard_map/ppermute | solution.py:374
  26.9 9.3 %collective-permute-start.2 = (f32[64,256]{1,0:T(8,128)S(1)}, f32[64,256]{1,0:T(8,128)S(1)}, u32[]{:S(2)}, u32[]{:S(2)}) collective-permute-start(f32[64,256]{1,0:T(8,128)S(1)} %added.1.refs_0_), channel_id=1, source_target_pairs={{2,0},{4,2},{6,4},{0,6},{3,1},{5,3},{7,5},{1,7},{10,8},{12,10},{14... | collective-permute-start | bytes 196616 | tf_op jit(solution)/shard_map/ppermute | solution.py:390
  30.8 9.4 %collective-permute-start.3 = (f32[64,256]{1,0:T(8,128)S(1)}, f32[64,256]{1,0:T(8,128)S(1)}, u32[]{:S(2)}, u32[]{:S(2)}) collective-permute-start(f32[64,256]{1,0:T(8,128)S(1)} %added.1.refs_0_), channel_id=1, source_target_pairs={{4,0},{6,2},{0,4},{2,6},{5,1},{7,3},{1,5},{3,7},{12,8},{14,10},{8,... | collective-permute-start | bytes 196616 | tf_op jit(solution)/shard_map/ppermute | solution.py:390
  33.2 8.0 %collective-permute-start.4 = (f32[64,256]{1,0:T(8,128)S(1)}, f32[64,256]{1,0:T(8,128)S(1)}, u32[]{:S(2)}, u32[]{:S(2)}) collective-permute-start(f32[64,256]{1,0:T(8,128)S(1)} %added.1.refs_0_), channel_id=1, source_target_pairs={{6,0},{0,2},{2,4},{4,6},{7,1},{1,3},{3,5},{5,7},{14,8},{8,10},{10,... | collective-permute-start | bytes 196616 | tf_op jit(solution)/shard_map/ppermute | solution.py:390
  90.5 30.6 %copy-start = (bf16[256,512]{1,0:T(8,128)(2,1)S(1)}, bf16[256,512]{1,0:T(8,128)(2,1)}, u32[]{:S(2)}) copy-start(bf16[256,512]{1,0:T(8,128)(2,1)} %grads_ref.3) | copy-start | bytes 786436
  104.3 3.1 %collective-permute-start.6 = (f32[64,256]{1,0:T(8,128)S(1)}, f32[64,256]{1,0:T(8,128)S(1)}, u32[]{:S(2)}, u32[]{:S(2)}) collective-permute-start(f32[64,256]{1,0:T(8,128)S(1)} %inner_products.1.one_ref), channel_id=1, source_target_pairs={{0,1},{1,0},{2,3},{3,2},{4,5},{5,4},{6,7},{7,6},{8,9},{9,8},{10,11... | collective-permute-start | bytes 196616 | tf_op jit(solution)/shard_map/ppermute | solution.py:374
  108.1 12.9 %all-to-all-start.5 = ((f32[4,64,256]{2,1,0:T(8,128)}), f32[4,64,256]{2,1,0:T(8,128)S(1)}, u32[]{:S(2)}, u32[]{:S(2)}) async-start(f32[4,64,256]{2,1,0:T(8,128)} %added_copies.1), calls=%async_computation.5 | async-start | bytes 524288 | tf_op jit(solution)/shard_map/all_to_all | solution.py:362
  111.8 3.8 %collective-permute-start.5 = (f32[16,64,128]{2,1,0:T(8,128)S(1)}, f32[16,64,128]{2,1,0:T(8,128)S(1)}, u32[]{:S(2)}, u32[]{:S(2)}) collective-permute-start(f32[16,64,128]{2,1,0:T(8,128)S(1)} %all_to_all.43.own_ref.left_ref), channel_id=1, source_target_pairs={{0,1},{1,0},{2,3},{3,2},{4,5},{5,4},{6,7},{7,6},{8,9},{9,8},{10,11... | collective-permute-start | bytes 1572872 | tf_op jit(solution)/shard_map/ppermute | solution.py:374
  133.1 11.4 %all-to-all-start.7 = ((f32[16,8,256]{2,1,0:T(8,128)}), f32[16,8,256]{2,1,0:T(8,128)S(1)}, u32[]{:S(2)}, u32[]{:S(2)}) async-start(f32[16,8,256]{2,1,0:T(8,128)} %summed_copies.7), calls=%async_computation.7 | async-start | bytes 262144 | tf_op jit(solution)/shard_map/all_to_all | solution.py:362

commit v5 on v4

--- a/solution.py
+++ b/solution.py
@@ -46,57 +46,28 @@
     return pl.CostEstimate(flops=flops, bytes_accessed=count, transcendentals=0)
 
 
+def joined(odd, own, other):
+    return jnp.concatenate([jnp.where(odd, other, own), jnp.where(odd, own, other)], axis=0)
+
+
 def whole_specs(count):
     scalar = pl.BlockSpec(memory_space=pltpu.SMEM)
     return [scalar] + [pl.BlockSpec(memory_space=pltpu.VMEM)] * count
 
 
-def copied(value, copies):
-    def kernel(value_ref, out_ref, sems):
-        started = [
-            pltpu.make_async_copy(value_ref, out_ref.at[i], sems.at[i]) for i in range(copies)
-        ]
-        for copy in started:
-            copy.start()
-        for copy in started:
-            copy.wait()
-
-    return pl.pallas_call(
-        kernel,
-        in_specs=[pl.BlockSpec(memory_space=pltpu.HBM)],
-        out_shape=jax.ShapeDtypeStruct((copies,) + value.shape, value.dtype),
-        scratch_shapes=[pltpu.SemaphoreType.DMA((copies,))],
-        cost_estimate=cost(0, 2 * value.size * (1 + copies)),
-        compiler_params=PARAMS,
-        name="copied",
-    )(value)
-
-
-def added_copies(one, two, copies):
+def added_tail(one, two):
+    blocks = two.shape[0]
+
     def kernel(one_ref, two_ref, out_ref):
-        total = one_ref[...] + two_ref[...]
-        for i in range(copies):
-            out_ref[i] = total
-
-    return pl.pallas_call(
-        kernel,
-        out_shape=jax.ShapeDtypeStruct((copies,) + one.shape, F32),
-        cost_estimate=cost(one.size, 4 * one.size * (2 + copies)),
-        compiler_params=PARAMS,
-        name="added_copies",
-    )(one, two)
-
-
-def added(one, two):
-    def kernel(one_ref, two_ref, out_ref):
-        out_ref[...] = one_ref[...] + two_ref[...]
+        tail = jnp.concatenate([two_ref[blocks - 2], two_ref[blocks - 1]], axis=1)
+        out_ref[...] = one_ref[...] + tail
 
     return pl.pallas_call(
         kernel,
         out_shape=jax.ShapeDtypeStruct(one.shape, F32),
         cost_estimate=cost(one.size, 12 * one.size),
         compiler_params=PARAMS,
-        name="added",
+        name="added_tail",
     )(one, two)
 
 
@@ -110,16 +81,19 @@
     return copies
 
 
-def left_products(half, start_right, grads, feedback, chunks):
+def left_products(half, start_right, grads, activations, feedback, chunks, copies_wanted):
     rows, width = feedback.shape
     rank, tokens = start_right.shape[0], grads.shape[0]
     pairs = rows // (2 * LANES * chunks)
 
-    def kernel(half_ref, start_ref, grads_ref, feed_ref, *refs):
-        inner_ref, own_ref, other_ref, held, sems, start, held_grads, few = refs
+    def kernel(half_ref, start_ref, grads_ref, act_ref, feed_ref, *refs):
+        inner_ref, own_ref, other_ref, copies_ref, held, sems, start, held_grads, few = refs
         first = [
             pltpu.make_async_copy(start_ref, start, few.at[0]),
             pltpu.make_async_copy(grads_ref, held_grads, few.at[1]),
+        ] + [
+            pltpu.make_async_copy(act_ref, copies_ref.at[i], few.at[2 + i])
+            for i in range(copies_wanted)
         ]
         for copy in first:
             copy.start()
@@ -128,7 +102,10 @@
         first[0].wait()
         split = pieces(start[...])
         first[1].wait()
-        inner_ref[...] = folded(nt(split, held_grads[...]))
+        inner = folded(nt(split, held_grads[...]))
+        inner_ref[...] = inner
+        other_ref[chunks * pairs] = inner[:, :LANES]
+        other_ref[chunks * pairs + 1] = inner[:, LANES:]
         for k in range(chunks):
             copies[k].wait()
             part = held[k * (rows // chunks) : (k + 1) * (rows // chunks)]
@@ -138,24 +115,28 @@
                 odd_rows = result[:, (2 * i + 1) * LANES : (2 * i + 2) * LANES]
                 own_ref[k * pairs + i] = jnp.where(odd, odd_rows, even_rows)
                 other_ref[k * pairs + i] = jnp.where(odd, even_rows, odd_rows)
+        for copy in first[2:]:
+            copy.wait()
 
     small = jax.ShapeDtypeStruct((rank, tokens), F32)
     large = jax.ShapeDtypeStruct((rows // (2 * LANES), rank, LANES), F32)
-    return pl.pallas_call(
-        kernel,
-        in_specs=whole_specs(0) + [pl.BlockSpec(memory_space=pltpu.HBM)] * 3,
-        out_shape=(small, large, large),
+    longer = jax.ShapeDtypeStruct((rows // (2 * LANES) + 2, rank, LANES), F32)
+    repeated = jax.ShapeDtypeStruct((copies_wanted,) + activations.shape, BF16)
+    return pl.pallas_call(
+        kernel,
+        in_specs=whole_specs(0) + [pl.BlockSpec(memory_space=pltpu.HBM)] * 4,
+        out_shape=(small, large, longer, repeated),
         scratch_shapes=[
             pltpu.VMEM(feedback.shape, BF16),
             pltpu.SemaphoreType.DMA((chunks,)),
             pltpu.VMEM(start_right.shape, F32),
             pltpu.VMEM(grads.shape, BF16),
-            pltpu.SemaphoreType.DMA((2,)),
+            pltpu.SemaphoreType.DMA((2 + copies_wanted,)),
         ],
         cost_estimate=cost(6 * rank * width * rows, 2 * feedback.size + 4 * rows * rank),
         compiler_params=PARAMS,
         name="left_products",
-    )(half, start_right, grads, feedback)
+    )(half, start_right, grads, activations, feedback)
 
 
 def add_activations(place, inner, columns, own, other):
@@ -172,7 +153,8 @@
         across = jnp.concatenate([columns_ref[i] for i in range(far_size)], axis=1)
         extra = folded(nn(pieces(total), across))
         for i in range(far_size):
-            block = i * (blocks // far_size) + place_ref[0]
+            group = (i + far_size // 2) % far_size
+            block = group * (blocks // far_size) + place_ref[0]
             out_ref[block] = out_ref[block] + extra[:, i * LANES : (i + 1) * LANES]
 
     return pl.pallas_call(
@@ -209,14 +191,19 @@
     far_size, tokens, _ = columns.shape
 
     def kernel(near_ref, left_ref, columns_ref, out_ref):
-        rows = [left_ref[i * (blocks // far_size) + near_ref[0]] for i in range(far_size)]
+        near_size = blocks // far_size
+        groups = [(i + far_size // 2) % far_size for i in range(far_size)]
+        rows = [left_ref[group * near_size + near_ref[0]] for group in groups]
         across = jnp.concatenate([columns_ref[i] for i in range(far_size)], axis=1)
-        out_ref[...] = folded(nt(pieces(jnp.concatenate(rows, axis=1)), across))
+        result = folded(nt(pieces(jnp.concatenate(rows, axis=1)), across))
+        for i in range(near_size):
+            out_ref[2 * i] = result[: rank // 2]
+            out_ref[2 * i + 1] = result[rank // 2 :]
 
     return pl.pallas_call(
         kernel,
         in_specs=whole_specs(2),
-        out_shape=jax.ShapeDtypeStruct((rank, tokens), F32),
+        out_shape=jax.ShapeDtypeStruct((2 * blocks // far_size, rank // 2, tokens), F32),
         cost_estimate=cost(6 * rank * tokens * far_size * LANES, 2 * columns.size),
         compiler_params=PARAMS,
         name="inner_products",
@@ -260,16 +247,14 @@
     )(half, own, other, feedback)
 
 
-def add_grads(shares, grads, partial, parts):
-    ways, rank, tokens = shares.shape
-    width = grads.shape[1]
+def add_grads(half, inner, inner_other, grads, partial, parts):
+    rank, width = partial.shape
+    tokens = grads.shape[0]
     split_rows = rank * width // (256 * parts)
     across = width // 256
 
-    def kernel(shares_ref, grads_ref, partial_ref, out_ref):
-        inner = shares_ref[0]
-        for i in range(1, ways):
-            inner = inner + shares_ref[i]
+    def kernel(half_ref, inner_ref, inner_other_ref, grads_ref, partial_ref, out_ref):
+        inner = joined(half_ref[0] == 1, inner_ref[...], inner_other_ref[...])
         total = partial_ref[...] + folded(nn(pieces(inner), grads_ref[...]))
         for i in range(parts):
             down, over = i // across * split_rows, i % across * 256
@@ -277,11 +262,12 @@
 
     return pl.pallas_call(
         kernel,
+        in_specs=whole_specs(4),
         out_shape=jax.ShapeDtypeStruct((parts, split_rows, 256), F32),
-        cost_estimate=cost(6 * rank * tokens * width, 4 * shares.size + 2 * grads.size),
+        cost_estimate=cost(6 * rank * tokens * width, 8 * inner.size + 2 * grads.size),
         compiler_params=PARAMS,
         name="add_grads",
-    )(shares, grads, partial)
+    )(half, inner, inner_other, grads, partial)
 
 
 def inverse_factor(gram):
@@ -358,8 +344,10 @@
     )(place, half, inverse, own, other, gathered)
 
 
-def exchange(value, axes):
-    return lax.all_to_all(value, axes, 0, 0, tiled=True)
+def exchange(value, axes, first=0):
+    size = lax.axis_size(axes)
+    order = [(i + first) % size for i in range(size)]
+    return lax.all_to_all(value, axes, 0, 0, axis_index_groups=[order], tiled=True)
 
 
 def in_hbm(value):
@@ -381,27 +369,29 @@
     half = index_of("c")
     feedback = in_hbm(feedback)
 
-    columns = exchange(copied(in_hbm(activations), far), "zh")
-    inner, own, other = left_products(
-        half, in_hbm(start_right.T), in_hbm(grads_out), feedback, 4
+    inner, own, other, columns = left_products(
+        half, in_hbm(start_right.T), in_hbm(grads_out), in_hbm(activations), feedback, 4, far
     )
-    inner = added(inner, swapped(inner))
+    columns = exchange(columns, "zh", far // 2)
+    other = swapped(other)
+    inner = added_tail(inner, other)
     inner = [inner] + [
         lax.ppermute(inner, "zl", [((i + j) % near, i) for i in range(near)])
         for j in range(1, near)
     ]
-    left = add_activations(index_of("zl"), inner, columns, own, swapped(other))
+    left = add_activations(index_of("zl"), inner, columns, own, other)
 
     left = summed_copies(exchange(left, XY), near)
-    left = summed_copies(exchange(left, "zl"), far)
-    left = summed_copies(exchange(left, "zh"), outer)
+    left = summed_copies(exchange(left, "zl", 1), far)
+    left = summed_copies(exchange(left, "zh", far // 2), outer)
     own = exchange(left, XY)
     other = swapped(own)
 
     inner = inner_products(index_of("zl"), own, columns)
-    inner = exchange(added_copies(inner, swapped(inner), near), "zl")
+    inner = summed_copies(exchange(inner, ("zl", "c"), 2), 1)[0]
     right, gram = feedback_right(half, own, other, feedback, 4)
-    right = add_grads(inner, grads_out, right, outer)
+    inner, right = lax.optimization_barrier((inner, right))
+    right = add_grads(half, inner, swapped(inner), grads_out, right, outer)
     inverse = inverse_factor(gram)
     right = summed_copies(exchange(right, XY), outer)
     right = exchange(right, XY)

time: 148 us -> 137 us (0.926)
  blocking collectives: 73.6 us -> 65.1 us
  starting transfers between devices: 41.8 us -> 44 us
  waiting for transfers between devices: 11.6 us -> 9.49 us
  Pallas kernels: 18.5 us -> 16.8 us
    all_to_all x5, blocking collectives: 73.6 us -> 65.1 us  [exchange(): lax.all_to_all(value, axes, 0, 0, axis_index_groups=[order], tiled=True)]
    all_to_all x3, starting transfers between devices: 24.4 us -> 28 us  [exchange(): lax.all_to_all(value, axes, 0, 0, axis_index_groups=[order], tiled=True)]
    pallas_call x4 -> x2, Pallas kernels: 2.66 us -> 0.22 us  [the longest x1 0.21 us: add_grads(): pl.pallas_call(kernel, in_specs=whole_specs(4), out_shape=jax.ShapeDtypeS...]
    ppermute x4 -> x3, starting transfers between devices: 8.16 us -> 5.87 us  [swapped(): return lax.ppermute(value, 'c', [(0, 1), (1, 0)])]
    ppermute x3, waiting for transfers between devices: 5.01 us -> 3.01 us  [per_device(): lax.ppermute(inner, 'zl', [((i + j) % near, i) for i in range(near)])]
    ppermute x4 -> x3, waiting for transfers between devices: 3.98 us -> 4.88 us  [swapped(): return lax.ppermute(value, 'c', [(0, 1), (1, 0)])]
  transfers between devices with their start and end apart: 10 -> 9, of which waited for: 7 -> 7; matrix products, arithmetic and copies ran while one was open for 0% -> 0% of each run, Pallas kernels for 9% -> 6%
where the time goes in v5:
time: 137 us; the launch traced here: 136 us
  blocking collectives  65.1 us (48%)
  starting transfers between devices  44 us (32%)
  Pallas kernels  16.8 us (12%)
  waiting for transfers between devices  9.49 us (7%)
    all_to_all x5, blocking collectives, exchange(): lax.all_to_all(value, axes, 0, 0, axis_index_groups=[order], tiled=True)  65.1 us
    all_to_all x3, starting transfers between devices, exchange(): lax.all_to_all(value, axes, 0, 0, axis_index_groups=[order], tiled=True)  28 us
    ppermute x3, starting transfers between devices, per_device(): lax.ppermute(inner, 'zl', [((i + j) % near, i) for i in range(near)])  10.1 us
    ppermute x3, starting transfers between devices, swapped(): return lax.ppermute(value, 'c', [(0, 1), (1, 0)])  5.87 us
    pallas_call x1, Pallas kernels, inverse_factor(): pl.pallas_call(kernel, out_shape=jax.ShapeDtypeStruct((rank, rank), F32),...  5.46 us
    ppermute x3, waiting for transfers between devices, swapped(): return lax.ppermute(value, 'c', [(0, 1), (1, 0)])  4.88 us
    pallas_call x1, Pallas kernels, left_products(): pl.pallas_call(kernel, in_specs=whole_specs(0) + [pl.BlockSpec(memory_spa...  4.21 us
    pallas_call x1, Pallas kernels, feedback_right(): pl.pallas_call(kernel, in_specs=whole_specs(2) + [pl.BlockSpec(memory_spa...  3.26 us
  transfers between devices with their start and end apart: 9, of which 7 were waited for; matrix products, arithmetic and copies ran while one was open for 0% of the time, Pallas kernels for 6%

profile of v5, /device:TPU:6, one launch (start us, length us, event | category | flops | bytes accessed | tf_op | source)
XLA Modules:
  0.0 136.2 jit_solution(8622920861864806572)
XLA Ops:
  0.6 4.2 %left_products.1 = (f32[64,256]{1,0:T(8,128)S(1)}, f32[16,64,128]{2,1,0:T(8,128)S(1)}, f32[18,64,128]{2,1,0:T(8,128)S(1)}, bf16[4,256,128]{2,1,0:T(8,128)(2,1)}) custom-call(s32[1]{0:T(128)} %bitcast.1.half_ref, f32[64,512]{1,0:T(8,128)} %bitcast.8, bf16[256,512]{1,0:T(8,128)(2,1)} %grads_ref.3, bf16[256,128]{1,0:T(8,128)(2,1)} %act_ref.1, ...), custom_call_target="tpu_custom_call" | custom-call | flops 805306368 | bytes 5242880 | tf_op jit(solution)/shard_map/left_products/pallas_call | solution.py:125
  4.8 17.5 %all-to-all-start = ((bf16[4,256,128]{2,1,0:T(8,128)(2,1)}), bf16[4,256,128]{2,1,0:T(8,128)(2,1)S(1)}, u32[]{:S(2)}, u32[]{:S(2)}) async-start(bf16[4,256,128]{2,1,0:T(8,128)(2,1)} %get-tuple-element.12), calls=%async_computation | async-start | bytes 524288 | tf_op jit(solution)/shard_map/all_to_all | solution.py:350
  22.3 1.9 %collective-permute-start = (f32[18,64,128]{2,1,0:T(8,128)S(1)}, f32[18,64,128]{2,1,0:T(8,128)S(1)}, u32[]{:S(2)}, u32[]{:S(2)}) collective-permute-start(f32[18,64,128]{2,1,0:T(8,128)S(1)} %get-tuple-element.14), channel_id=1, source_target_pairs={{0,1},{1,0},{2,3},{3,2},{4,5},{5,4},{6,7},{7,6},{8,9},{9,8},{10,11... | collective-permute-start | bytes 1769480 | tf_op jit(solution)/shard_map/ppermute | solution.py:362
  24.2 2.0 %collective-permute-done.two_ref.other_ref = f32[18,64,128]{2,1,0:T(8,128)S(1)} collective-permute-done((f32[18,64,128]{2,1,0:T(8,128)S(1)}, f32[18,64,128]{2,1,0:T(8,128)S(1)}, u32[]{:S(2)}, u32[]{:S(2)}) %collective-permute-start) | collective-permute-done | bytes 589856 | tf_op jit(solution)/shard_map/ppermute | solution.py:362
  26.2 2.9 %collective-permute-start.3 = (f32[64,256]{1,0:T(8,128)S(1)}, f32[64,256]{1,0:T(8,128)S(1)}, u32[]{:S(2)}, u32[]{:S(2)}) collective-permute-start(f32[64,256]{1,0:T(8,128)S(1)} %added_tail.1.refs_0_), channel_id=1, source_target_pairs={{6,0},{0,2},{2,4},{4,6},{7,1},{1,3},{3,5},{5,7},{14,8},{8,10},{10,... | collective-permute-start | bytes 196616 | tf_op jit(solution)/shard_map/ppermute | solution.py:379
  29.2 3.4 %collective-permute-start.2 = (f32[64,256]{1,0:T(8,128)S(1)}, f32[64,256]{1,0:T(8,128)S(1)}, u32[]{:S(2)}, u32[]{:S(2)}) collective-permute-start(f32[64,256]{1,0:T(8,128)S(1)} %added_tail.1.refs_0_), channel_id=1, source_target_pairs={{4,0},{6,2},{0,4},{2,6},{5,1},{7,3},{1,5},{3,7},{12,8},{14,10},{8,... | collective-permute-start | bytes 196616 | tf_op jit(solution)/shard_map/ppermute | solution.py:379
  32.5 3.8 %collective-permute-start.1 = (f32[64,256]{1,0:T(8,128)S(1)}, f32[64,256]{1,0:T(8,128)S(1)}, u32[]{:S(2)}, u32[]{:S(2)}) collective-permute-start(f32[64,256]{1,0:T(8,128)S(1)} %added_tail.1.refs_0_), channel_id=1, source_target_pairs={{2,0},{4,2},{6,4},{0,6},{3,1},{5,3},{7,5},{1,7},{10,8},{12,10},{14... | collective-permute-start | bytes 196616 | tf_op jit(solution)/shard_map/ppermute | solution.py:379
  36.4 0.0 collective-permute-done.3.refs_3_
  36.4 2.5 %collective-permute-done.2.refs_2_ = f32[64,256]{1,0:T(8,128)S(1)} collective-permute-done((f32[64,256]{1,0:T(8,128)S(1)}, f32[64,256]{1,0:T(8,128)S(1)}, u32[]{:S(2)}, u32[]{:S(2)}) %collective-permute-start.2) | collective-permute-done | bytes 65568 | tf_op jit(solution)/shard_map/ppermute | solution.py:379
  38.9 0.5 collective-permute-done.1.refs_1_
  39.4 0.0 all-to-all-done.columns_ref
  39.4 0.2 add_activations.1
  39.6 16.1 %all_to_all.40.shares_ref = f32[16,64,128]{2,1,0:T(8,128)S(1)} all-to-all(f32[16,64,128]{2,1,0:T(8,128)S(1)} %add_activations.1), channel_id=1, replica_groups={{0,32,64,96,128,160,192,224,256,288,320,352,384,416,448,480},{1,33,65,9..., dimensions={0} | all-to-all | bytes 1048576 | tf_op jit(solution)/shard_map/all_to_all | solution.py:350
  55.7 8.7 %all_to_all.41.shares_ref = f32[4,64,128]{2,1,0:T(8,128)S(1)} all-to-all(f32[4,64,128]{2,1,0:T(8,128)S(1)} %summed_copies.5), channel_id=1, replica_groups={{2,4,6,0},{3,5,7,1},{10,12,14,8},{11,13,15,9},{18,20,22,16},{19,21,23,1..., dimensions={0} | all-to-all | bytes 262144 | tf_op jit(solution)/shard_map/all_to_all | solution.py:350
  64.5 15.3 %all_to_all.42.shares_ref = f32[4,64,128]{2,1,0:T(8,128)S(1)} all-to-all(f32[4,64,128]{2,1,0:T(8,128)S(1)} %summed_copies.6), channel_id=1, replica_groups={{16,24,0,8},{17,25,1,9},{18,26,2,10},{19,27,3,11},{20,28,4,12},{21,29,5..., dimensions={0} | all-to-all | bytes 262144 | tf_op jit(solution)/shard_map/all_to_all | solution.py:350
  79.9 0.0 copy-start
  79.9 13.8 %all_to_all.43.own_ref.left_ref = f32[16,64,128]{2,1,0:T(8,128)S(1)} all-to-all(f32[16,64,128]{2,1,0:T(8,128)S(1)} %summed_copies.7), channel_id=1, replica_groups={{0,32,64,96,128,160,192,224,256,288,320,352,384,416,448,480},{1,33,65,9..., dimensions={0} | all-to-all | bytes 1048576 | tf_op jit(solution)/shard_map/all_to_all | solution.py:350
  93.7 1.0 inner_products.1
  94.6 5.0 %all-to-all-start.5 = ((f32[8,32,256]{2,1,0:T(8,128)}), f32[8,32,256]{2,1,0:T(8,128)S(1)}, u32[]{:S(2)}, u32[]{:S(2)}) async-start(f32[8,32,256]{2,1,0:T(8,128)} %inner_products.1), calls=%async_computation.5 | async-start | bytes 524288 | tf_op jit(solution)/shard_map/all_to_all | solution.py:350
  99.6 2.0 %collective-permute-start.4 = (f32[16,64,128]{2,1,0:T(8,128)S(1)}, f32[16,64,128]{2,1,0:T(8,128)S(1)}, u32[]{:S(2)}, u32[]{:S(2)}) collective-permute-start(f32[16,64,128]{2,1,0:T(8,128)S(1)} %all_to_all.43.own_ref.left_ref), channel_id=1, source_target_pairs={{0,1},{1,0},{2,3},{3,2},{4,5},{5,4},{6,7},{7,6},{8,9},{9,8},{10,11... | collective-permute-start | bytes 1572872 | tf_op jit(solution)/shard_map/ppermute | solution.py:362
  101.6 1.7 %collective-permute-done.4.other_ref = f32[16,64,128]{2,1,0:T(8,128)S(1)} collective-permute-done((f32[16,64,128]{2,1,0:T(8,128)S(1)}, f32[16,64,128]{2,1,0:T(8,128)S(1)}, u32[]{:S(2)}, u32[]{:S(2)}) %collective-permute-start.4) | collective-permute-done | bytes 524320 | tf_op jit(solution)/shard_map/ppermute | solution.py:362
  103.4 3.3 %feedback_right.1 = (f32[64,512]{1,0:T(8,128)S(1)}, f32[64,64]{1,0:T(8,128)S(1)}) custom-call(s32[1]{0:T(128)} %bitcast.1.half_ref, f32[16,64,128]{2,1,0:T(8,128)S(1)} %all_to_all.43.own_ref.left_ref, f32[16,64,128]{2,1,0:T(8,128)S(1)} %collective-permute-done.4.other_ref, bf16[4096,512]{1,0:T(8,128)(2,1)} %feed_ref.3), custom_call_target="tpu_custom_call" | custom-call | flops 1107296256 | bytes 4194304 | tf_op jit(solution)/shard_map/feedback_right/pallas_call | solution.py:236
  106.7 1.2 all-to-all-done.5.shares_ref
  107.9 1.9 %collective-permute-start.5 = (f32[32,256]{1,0:T(8,128)S(1)}, f32[32,256]{1,0:T(8,128)S(1)}, u32[]{:S(2)}, u32[]{:S(2)}) collective-permute-start(f32[32,256]{1,0:T(8,128)S(1)} %bitcast.6), channel_id=1, source_target_pairs={{0,1},{1,0},{2,3},{3,2},{4,5},{5,4},{6,7},{7,6},{8,9},{9,8},{10,11... | collective-permute-start | bytes 98312 | tf_op jit(solution)/shard_map/ppermute | solution.py:362
  109.8 1.2 collective-permute-done.5.inner_other_ref
  111.0 0.2 add_grads.1
  111.2 11.2 %all_to_all.44.shares_ref = f32[16,8,256]{2,1,0:T(8,128)S(1)} all-to-all(f32[16,8,256]{2,1,0:T(8,128)S(1)} %add_grads.1), channel_id=1, replica_groups={{0,32,64,96,128,160,192,224,256,288,320,352,384,416,448,480},{1,33,65,9..., dimensions={0} | all-to-all | bytes 262144 | tf_op jit(solution)/shard_map/all_to_all | solution.py:350
  122.3 0.7 summed_copies.9
  123.0 5.6 %all-to-all-start.7 = ((f32[16,8,256]{2,1,0:T(8,128)}), f32[16,8,256]{2,1,0:T(8,128)S(1)}, u32[]{:S(2)}, u32[]{:S(2)}) async-start(f32[16,8,256]{2,1,0:T(8,128)} %summed_copies.9), calls=%async_computation.7 | async-start | bytes 262144 | tf_op jit(solution)/shard_map/all_to_all | solution.py:350
  128.6 5.5 %inverse_factor.1.inverse_ref = f32[64,64]{1,0:T(8,128)S(1)} custom-call(f32[64,64]{1,0:T(8,128)S(1)} %get-tuple-element.16.gram_ref), custom_call_target="tpu_custom_call" | custom-call | flops 4194304 | bytes 32768 | tf_op jit(solution)/shard_map/inverse_factor/pallas_call | solution.py:292
  134.1 0.4 all-to-all-done.7.gathered_ref
  134.5 1.7 %finish.1 = (bf16[256,512]{1,0:T(8,128)(2,1)}, f32[64,512]{1,0:T(8,128)}) custom-call(s32[1]{0:T(128)} %bitcast.place_ref, s32[1]{0:T(128)} %bitcast.1.half_ref, f32[64,64]{1,0:T(8,128)S(1)} %inverse_factor.1.inverse_ref, f32[16,64,128]{2,1,0:T(8,128)S(1)} %all_to_all.43.own_ref.left_ref, f32[16,64,128]{2,1,0:T(8,128)S(1)} %collective-permute-done.4.other_ref, ...), custom_call_target="tpu_custom_call" | custom-call | flops 100663296 | bytes 131072 | tf_op jit(solution)/shard_map/finish/pallas_call | solution.py:321
  (6 shorter events, 0.1 us)
Async XLA Ops:
  4.8 34.5 %all-to-all-start = ((bf16[4,256,128]{2,1,0:T(8,128)(2,1)}), bf16[4,256,128]{2,1,0:T(8,128)(2,1)S(1)}, u32[]{:S(2)}, u32[]{:S(2)}) async-start(bf16[4,256,128]{2,1,0:T(8,128)(2,1)} %get-tuple-element.12), calls=%async_computation | async-start | bytes 524288 | tf_op jit(solution)/shard_map/all_to_all | solution.py:350
  22.3 3.9 %collective-permute-start = (f32[18,64,128]{2,1,0:T(8,128)S(1)}, f32[18,64,128]{2,1,0:T(8,128)S(1)}, u32[]{:S(2)}, u32[]{:S(2)}) collective-permute-start(f32[18,64,128]{2,1,0:T(8,128)S(1)} %get-tuple-element.14), channel_id=1, source_target_pairs={{0,1},{1,0},{2,3},{3,2},{4,5},{5,4},{6,7},{7,6},{8,9},{9,8},{10,11... | collective-permute-start | bytes 1769480 | tf_op jit(solution)/shard_map/ppermute | solution.py:362
  26.2 10.2 %collective-permute-start.3 = (f32[64,256]{1,0:T(8,128)S(1)}, f32[64,256]{1,0:T(8,128)S(1)}, u32[]{:S(2)}, u32[]{:S(2)}) collective-permute-start(f32[64,256]{1,0:T(8,128)S(1)} %added_tail.1.refs_0_), channel_id=1, source_target_pairs={{6,0},{0,2},{2,4},{4,6},{7,1},{1,3},{3,5},{5,7},{14,8},{8,10},{10,... | collective-permute-start | bytes 196616 | tf_op jit(solution)/shard_map/ppermute | solution.py:379
  29.2 9.7 %collective-permute-start.2 = (f32[64,256]{1,0:T(8,128)S(1)}, f32[64,256]{1,0:T(8,128)S(1)}, u32[]{:S(2)}, u32[]{:S(2)}) collective-permute-start(f32[64,256]{1,0:T(8,128)S(1)} %added_tail.1.refs_0_), channel_id=1, source_target_pairs={{4,0},{6,2},{0,4},{2,6},{5,1},{7,3},{1,5},{3,7},{12,8},{14,10},{8,... | collective-permute-start | bytes 196616 | tf_op jit(solution)/shard_map/ppermute | solution.py:379
  32.5 6.8 %collective-permute-start.1 = (f32[64,256]{1,0:T(8,128)S(1)}, f32[64,256]{1,0:T(8,128)S(1)}, u32[]{:S(2)}, u32[]{:S(2)}) collective-permute-start(f32[64,256]{1,0:T(8,128)S(1)} %added_tail.1.refs_0_), channel_id=1, source_target_pairs={{2,0},{4,2},{6,4},{0,6},{3,1},{5,3},{7,5},{1,7},{10,8},{12,10},{14... | collective-permute-start | bytes 196616 | tf_op jit(solution)/shard_map/ppermute | solution.py:379
  79.9 31.1 %copy-start = (bf16[256,512]{1,0:T(8,128)(2,1)S(1)}, bf16[256,512]{1,0:T(8,128)(2,1)}, u32[]{:S(2)}) copy-start(bf16[256,512]{1,0:T(8,128)(2,1)} %grads_ref.3) | copy-start | bytes 786436
  94.6 13.2 %all-to-all-start.5 = ((f32[8,32,256]{2,1,0:T(8,128)}), f32[8,32,256]{2,1,0:T(8,128)S(1)}, u32[]{:S(2)}, u32[]{:S(2)}) async-start(f32[8,32,256]{2,1,0:T(8,128)} %inner_products.1), calls=%async_computation.5 | async-start | bytes 524288 | tf_op jit(solution)/shard_map/all_to_all | solution.py:350
  99.6 3.8 %collective-permute-start.4 = (f32[16,64,128]{2,1,0:T(8,128)S(1)}, f32[16,64,128]{2,1,0:T(8,128)S(1)}, u32[]{:S(2)}, u32[]{:S(2)}) collective-permute-start(f32[16,64,128]{2,1,0:T(8,128)S(1)} %all_to_all.43.own_ref.left_ref), channel_id=1, source_target_pairs={{0,1},{1,0},{2,3},{3,2},{4,5},{5,4},{6,7},{7,6},{8,9},{9,8},{10,11... | collective-permute-start | bytes 1572872 | tf_op jit(solution)/shard_map/ppermute | solution.py:362
  107.9 3.1 %collective-permute-start.5 = (f32[32,256]{1,0:T(8,128)S(1)}, f32[32,256]{1,0:T(8,128)S(1)}, u32[]{:S(2)}, u32[]{:S(2)}) collective-permute-start(f32[32,256]{1,0:T(8,128)S(1)} %bitcast.6), channel_id=1, source_target_pairs={{0,1},{1,0},{2,3},{3,2},{4,5},{5,4},{6,7},{7,6},{8,9},{9,8},{10,11... | collective-permute-start | bytes 98312 | tf_op jit(solution)/shard_map/ppermute | solution.py:362
  123.0 11.4 %all-to-all-start.7 = ((f32[16,8,256]{2,1,0:T(8,128)}), f32[16,8,256]{2,1,0:T(8,128)S(1)}, u32[]{:S(2)}, u32[]{:S(2)}) async-start(f32[16,8,256]{2,1,0:T(8,128)} %summed_copies.9), calls=%async_computation.7 | async-start | bytes 262144 | tf_op jit(solution)/shard_map/all_to_all | solution.py:350

commit v6 on v5

--- a/solution.py
+++ b/solution.py
@@ -9,6 +9,7 @@
 F32 = jnp.float32
 BF16 = jnp.bfloat16
 LANES = 128
+FIRST_STEPS = 24
 XY = ("x", "y")
 FAST = dict(preferred_element_type=F32)
 FULL = dict(preferred_element_type=F32, precision=lax.Precision.HIGHEST)
@@ -197,8 +198,8 @@
         across = jnp.concatenate([columns_ref[i] for i in range(far_size)], axis=1)
         result = folded(nt(pieces(jnp.concatenate(rows, axis=1)), across))
         for i in range(near_size):
-            out_ref[2 * i] = result[: rank // 2]
-            out_ref[2 * i + 1] = result[rank // 2 :]
+            out_ref[2 * i] = result[rank // 2 :]
+            out_ref[2 * i + 1] = result[: rank // 2]
 
     return pl.pallas_call(
         kernel,
@@ -270,32 +271,55 @@
     )(half, inner, inner_other, grads, partial)
 
 
-def inverse_factor(gram):
+def eliminated(work, first, last):
+    rank = work.shape[0]
+    index = lax.broadcasted_iota(jnp.int32, (rank, 1), 0)
+    for k in range(first, last):
+        low = k // 8 * 8
+        pivot_row = work[k : k + 1]
+        scale = 1.0 / work[k : k + 1, k : k + 1]
+        part = work[low:]
+        factor = jnp.where(index[low:] > k, part[:, k : k + 1] * scale, 0.0)
+        part = part - factor * pivot_row
+        work = part if low == 0 else jnp.concatenate([work[:low], part], axis=0)
+    return work
+
+
+def first_steps(gram):
     rank = gram.shape[0]
 
     def kernel(gram_ref, out_ref):
         row = lax.broadcasted_iota(jnp.int32, (rank, rank), 0)
         col = lax.broadcasted_iota(jnp.int32, (rank, rank), 1)
         work = jnp.concatenate([gram_ref[...], (row == col).astype(F32)], axis=1)
-        index = lax.broadcasted_iota(jnp.int32, (rank, 1), 0)
-        for k in range(rank):
-            low = k // 8 * 8
-            pivot_row = work[k : k + 1]
-            scale = 1.0 / work[k : k + 1, k : k + 1]
-            part = work[low:]
-            factor = jnp.where(index[low:] > k, part[:, k : k + 1] * scale, 0.0)
-            part = part - factor * pivot_row
-            work = part if low == 0 else jnp.concatenate([work[:low], part], axis=0)
+        out_ref[...] = eliminated(work, 0, FIRST_STEPS)
+
+    return pl.pallas_call(
+        kernel,
+        out_shape=jax.ShapeDtypeStruct((rank, 2 * rank), F32),
+        cost_estimate=cost(8 * rank * rank * rank, 12 * rank * rank),
+        compiler_params=PARAMS,
+        name="first_steps",
+    )(gram)
+
+
+def inverse_factor(work):
+    rank = work.shape[0]
+
+    def kernel(work_ref, out_ref):
+        row = lax.broadcasted_iota(jnp.int32, (rank, rank), 0)
+        col = lax.broadcasted_iota(jnp.int32, (rank, rank), 1)
+        work = eliminated(work_ref[...], FIRST_STEPS, rank)
         diagonal = jnp.sum(jnp.where(row == col, work[:, :rank], 0.0), axis=1, keepdims=True)
         out_ref[...] = work[:, rank:] / jnp.sqrt(diagonal)
 
     return pl.pallas_call(
         kernel,
         out_shape=jax.ShapeDtypeStruct((rank, rank), F32),
-        cost_estimate=cost(2 * rank * rank * rank * 8, 8 * rank * rank),
+        cost_estimate=cost(8 * rank * rank * rank, 12 * rank * rank),
         compiler_params=PARAMS,
         name="inverse_factor",
-    )(gram)
+    )(work)
 
 
 def finish(place, half, inverse, own, other, gathered, width):
@@ -366,6 +390,7 @@
     width = grads_out.shape[1]
     far, near = lax.axis_size("zh"), lax.axis_size("zl")
     outer = lax.axis_size(XY)
+    opposite = lax.axis_size("x") // 2 * lax.axis_size("y") + lax.axis_size("y") // 2
     half = index_of("c")
     feedback = in_hbm(feedback)
 
@@ -381,20 +406,21 @@
     ]
     left = add_activations(index_of("zl"), inner, columns, own, other)
 
-    left = summed_copies(exchange(left, XY), near)
+    left = summed_copies(exchange(left, XY, opposite), near)
     left = summed_copies(exchange(left, "zl", 1), far)
     left = summed_copies(exchange(left, "zh", far // 2), outer)
-    own = exchange(left, XY)
+    own = exchange(left, XY, opposite)
     other = swapped(own)
 
     inner = inner_products(index_of("zl"), own, columns)
-    inner = summed_copies(exchange(inner, ("zl", "c"), 2), 1)[0]
+    inner = summed_copies(exchange(inner, ("zl", "c"), 3), 1)[0]
     right, gram = feedback_right(half, own, other, feedback, 4)
     inner, right = lax.optimization_barrier((inner, right))
     right = add_grads(half, inner, swapped(inner), grads_out, right, outer)
-    inverse = inverse_factor(gram)
-    right = summed_copies(exchange(right, XY), outer)
-    right = exchange(right, XY)
+    right, work = lax.optimization_barrier((exchange(right, XY, opposite), first_steps(gram)))
+    right = summed_copies(right, outer)
+    inverse = inverse_factor(work)
+    right = exchange(right, XY, opposite)
     decompressed, right = finish(index_of(XY), half, inverse, own, other, right, width)
     return decompressed, right.T
 

time: 137 us -> 135 us (0.985)
  blocking collectives: 65.1 us -> 50.9 us
  starting transfers between devices: 44 us -> 51.6 us
  waiting for transfers between devices: 9.49 us -> 13.1 us
    all_to_all x5 -> x4, blocking collectives: 65.1 us -> 50.9 us  [exchange(): lax.all_to_all(value, axes, 0, 0, axis_index_groups=[order], tiled=True)]
    all_to_all x3 -> x4, starting transfers between devices: 28 us -> 35.6 us  [exchange(): lax.all_to_all(value, axes, 0, 0, axis_index_groups=[order], tiled=True)]
    all_to_all x3 -> x4, waiting for transfers between devices: 1.6 us -> 5.24 us  [exchange(): lax.all_to_all(value, axes, 0, 0, axis_index_groups=[order], tiled=True)]
    pallas_call x1, Pallas kernels: 5.46 us -> 3.32 us  [inverse_factor(): pl.pallas_call(kernel, out_shape=jax.ShapeDtypeStruct((rank, rank), F32),...]
    pallas_call x0 -> x1, Pallas kernels: none -> 2.07 us  [first_steps(): pl.pallas_call(kernel, out_shape=jax.ShapeDtypeStruct((rank, 2 * rank), F...]
  transfers between devices with their start and end apart: 9 -> 10, of which waited for: 7 -> 8; matrix products, arithmetic and copies ran while one was open for 0% -> 0% of each run, Pallas kernels for 6% -> 6%
where the time goes in v6:
time: 135 us; the launch traced here: 134 us
  starting transfers between devices  51.6 us (38%)
  blocking collectives  50.9 us (38%)
  Pallas kernels  17.4 us (13%)
  waiting for transfers between devices  13.1 us (10%)
    all_to_all x4, blocking collectives, exchange(): lax.all_to_all(value, axes, 0, 0, axis_index_groups=[order], tiled=True)  50.9 us
    all_to_all x4, starting transfers between devices, exchange(): lax.all_to_all(value, axes, 0, 0, axis_index_groups=[order], tiled=True)  35.6 us
    ppermute x3, starting transfers between devices, per_device(): lax.ppermute(inner, 'zl', [((i + j) % near, i) for i in range(near)])  10.1 us
    ppermute x3, starting transfers between devices, swapped(): return lax.ppermute(value, 'c', [(0, 1), (1, 0)])  5.87 us
    all_to_all x4, waiting for transfers between devices, exchange(): lax.all_to_all(value, axes, 0, 0, axis_index_groups=[order], tiled=True)  5.24 us
    ppermute x3, waiting for transfers between devices, swapped(): return lax.ppermute(value, 'c', [(0, 1), (1, 0)])  4.88 us
    pallas_call x1, Pallas kernels, left_products(): pl.pallas_call(kernel, in_specs=whole_specs(0) + [pl.BlockSpec(memory_spa...  4.21 us
    pallas_call x1, Pallas kernels, inverse_factor(): pl.pallas_call(kernel, out_shape=jax.ShapeDtypeStruct((rank, rank), F32),...  3.32 us
  transfers between devices with their start and end apart: 10, of which 8 were waited for; matrix products, arithmetic and copies ran while one was open for 0% of the time, Pallas kernels for 6%

profile of v6, /device:TPU:6, one launch (start us, length us, event | category | flops | bytes accessed | tf_op | source)
XLA Modules:
  0.0 133.7 jit_solution(3213034292739793311)
XLA Ops:
  0.6 4.2 %left_products.1 = (f32[64,256]{1,0:T(8,128)S(1)}, f32[16,64,128]{2,1,0:T(8,128)S(1)}, f32[18,64,128]{2,1,0:T(8,128)S(1)}, bf16[4,256,128]{2,1,0:T(8,128)(2,1)}) custom-call(s32[1]{0:T(128)} %bitcast.1.half_ref, f32[64,512]{1,0:T(8,128)} %bitcast.8, bf16[256,512]{1,0:T(8,128)(2,1)} %grads_ref.3, bf16[256,128]{1,0:T(8,128)(2,1)} %act_ref.1, ...), custom_call_target="tpu_custom_call" | custom-call | flops 805306368 | bytes 5242880 | tf_op jit(solution)/shard_map/left_products/pallas_call | solution.py:126
  4.8 17.5 %all-to-all-start = ((bf16[4,256,128]{2,1,0:T(8,128)(2,1)}), bf16[4,256,128]{2,1,0:T(8,128)(2,1)S(1)}, u32[]{:S(2)}, u32[]{:S(2)}) async-start(bf16[4,256,128]{2,1,0:T(8,128)(2,1)} %get-tuple-element.14), calls=%async_computation | async-start | bytes 524288 | tf_op jit(solution)/shard_map/all_to_all | solution.py:374
  22.3 1.9 %collective-permute-start = (f32[18,64,128]{2,1,0:T(8,128)S(1)}, f32[18,64,128]{2,1,0:T(8,128)S(1)}, u32[]{:S(2)}, u32[]{:S(2)}) collective-permute-start(f32[18,64,128]{2,1,0:T(8,128)S(1)} %get-tuple-element.16), channel_id=1, source_target_pairs={{0,1},{1,0},{2,3},{3,2},{4,5},{5,4},{6,7},{7,6},{8,9},{9,8},{10,11... | collective-permute-start | bytes 1769480 | tf_op jit(solution)/shard_map/ppermute | solution.py:386
  24.2 2.0 %collective-permute-done.two_ref.other_ref = f32[18,64,128]{2,1,0:T(8,128)S(1)} collective-permute-done((f32[18,64,128]{2,1,0:T(8,128)S(1)}, f32[18,64,128]{2,1,0:T(8,128)S(1)}, u32[]{:S(2)}, u32[]{:S(2)}) %collective-permute-start) | collective-permute-done | bytes 589856 | tf_op jit(solution)/shard_map/ppermute | solution.py:386
  26.2 2.9 %collective-permute-start.3 = (f32[64,256]{1,0:T(8,128)S(1)}, f32[64,256]{1,0:T(8,128)S(1)}, u32[]{:S(2)}, u32[]{:S(2)}) collective-permute-start(f32[64,256]{1,0:T(8,128)S(1)} %added_tail.1.refs_0_), channel_id=1, source_target_pairs={{6,0},{0,2},{2,4},{4,6},{7,1},{1,3},{3,5},{5,7},{14,8},{8,10},{10,... | collective-permute-start | bytes 196616 | tf_op jit(solution)/shard_map/ppermute | solution.py:404
  29.2 3.4 %collective-permute-start.2 = (f32[64,256]{1,0:T(8,128)S(1)}, f32[64,256]{1,0:T(8,128)S(1)}, u32[]{:S(2)}, u32[]{:S(2)}) collective-permute-start(f32[64,256]{1,0:T(8,128)S(1)} %added_tail.1.refs_0_), channel_id=1, source_target_pairs={{4,0},{6,2},{0,4},{2,6},{5,1},{7,3},{1,5},{3,7},{12,8},{14,10},{8,... | collective-permute-start | bytes 196616 | tf_op jit(solution)/shard_map/ppermute | solution.py:404
  32.5 3.8 %collective-permute-start.1 = (f32[64,256]{1,0:T(8,128)S(1)}, f32[64,256]{1,0:T(8,128)S(1)}, u32[]{:S(2)}, u32[]{:S(2)}) collective-permute-start(f32[64,256]{1,0:T(8,128)S(1)} %added_tail.1.refs_0_), channel_id=1, source_target_pairs={{2,0},{4,2},{6,4},{0,6},{3,1},{5,3},{7,5},{1,7},{10,8},{12,10},{14... | collective-permute-start | bytes 196616 | tf_op jit(solution)/shard_map/ppermute | solution.py:404
  36.4 2.5 %collective-permute-done.2.refs_2_ = f32[64,256]{1,0:T(8,128)S(1)} collective-permute-done((f32[64,256]{1,0:T(8,128)S(1)}, f32[64,256]{1,0:T(8,128)S(1)}, u32[]{:S(2)}, u32[]{:S(2)}) %collective-permute-start.2) | collective-permute-done | bytes 65568 | tf_op jit(solution)/shard_map/ppermute | solution.py:404
  38.9 0.5 collective-permute-done.1.refs_1_
  39.4 0.2 add_activations.1
  39.6 13.5 %all_to_all.40.shares_ref = f32[16,64,128]{2,1,0:T(8,128)S(1)} all-to-all(f32[16,64,128]{2,1,0:T(8,128)S(1)} %add_activations.1), channel_id=1, replica_groups={{320,352,384,416,448,480,0,32,64,96,128,160,192,224,256,288},{321,353,3..., dimensions={0} | all-to-all | bytes 1048576 | tf_op jit(solution)/shard_map/all_to_all | solution.py:374
  53.2 8.7 %all_to_all.41.shares_ref = f32[4,64,128]{2,1,0:T(8,128)S(1)} all-to-all(f32[4,64,128]{2,1,0:T(8,128)S(1)} %summed_copies.5), channel_id=1, replica_groups={{2,4,6,0},{3,5,7,1},{10,12,14,8},{11,13,15,9},{18,20,22,16},{19,21,23,1..., dimensions={0} | all-to-all | bytes 262144 | tf_op jit(solution)/shard_map/all_to_all | solution.py:374
  61.9 15.1 %all_to_all.42.shares_ref = f32[4,64,128]{2,1,0:T(8,128)S(1)} all-to-all(f32[4,64,128]{2,1,0:T(8,128)S(1)} %summed_copies.6), channel_id=1, replica_groups={{16,24,0,8},{17,25,1,9},{18,26,2,10},{19,27,3,11},{20,28,4,12},{21,29,5..., dimensions={0} | all-to-all | bytes 262144 | tf_op jit(solution)/shard_map/all_to_all | solution.py:374
  77.1 0.0 copy-start
  77.1 13.5 %all_to_all.43.left_ref.own_ref = f32[16,64,128]{2,1,0:T(8,128)S(1)} all-to-all(f32[16,64,128]{2,1,0:T(8,128)S(1)} %summed_copies.7), channel_id=1, replica_groups={{320,352,384,416,448,480,0,32,64,96,128,160,192,224,256,288},{321,353,3..., dimensions={0} | all-to-all | bytes 1048576 | tf_op jit(solution)/shard_map/all_to_all | solution.py:374
  90.6 1.0 inner_products.1
  91.6 4.5 %all-to-all-start.5 = ((f32[8,32,256]{2,1,0:T(8,128)}), f32[8,32,256]{2,1,0:T(8,128)S(1)}, u32[]{:S(2)}, u32[]{:S(2)}) async-start(f32[8,32,256]{2,1,0:T(8,128)} %inner_products.1), calls=%async_computation.5 | async-start | bytes 524288 | tf_op jit(solution)/shard_map/all_to_all | solution.py:374
  96.1 2.0 %collective-permute-start.4 = (f32[16,64,128]{2,1,0:T(8,128)S(1)}, f32[16,64,128]{2,1,0:T(8,128)S(1)}, u32[]{:S(2)}, u32[]{:S(2)}) collective-permute-start(f32[16,64,128]{2,1,0:T(8,128)S(1)} %all_to_all.43.left_ref.own_ref), channel_id=1, source_target_pairs={{0,1},{1,0},{2,3},{3,2},{4,5},{5,4},{6,7},{7,6},{8,9},{9,8},{10,11... | collective-permute-start | bytes 1572872 | tf_op jit(solution)/shard_map/ppermute | solution.py:386
  98.2 1.7 %collective-permute-done.4.other_ref = f32[16,64,128]{2,1,0:T(8,128)S(1)} collective-permute-done((f32[16,64,128]{2,1,0:T(8,128)S(1)}, f32[16,64,128]{2,1,0:T(8,128)S(1)}, u32[]{:S(2)}, u32[]{:S(2)}) %collective-permute-start.4) | collective-permute-done | bytes 524320 | tf_op jit(solution)/shard_map/ppermute | solution.py:386
  99.9 3.3 %feedback_right.1 = (f32[64,512]{1,0:T(8,128)S(1)}, f32[64,64]{1,0:T(8,128)S(1)}) custom-call(s32[1]{0:T(128)} %bitcast.1.half_ref, f32[16,64,128]{2,1,0:T(8,128)S(1)} %all_to_all.43.left_ref.own_ref, f32[16,64,128]{2,1,0:T(8,128)S(1)} %collective-permute-done.4.other_ref, bf16[4096,512]{1,0:T(8,128)(2,1)} %feed_ref.3), custom_call_target="tpu_custom_call" | custom-call | flops 1107296256 | bytes 4194304 | tf_op jit(solution)/shard_map/feedback_right/pallas_call | solution.py:237
  103.2 1.2 all-to-all-done.5.shares_ref
  104.4 1.9 %collective-permute-start.5 = (f32[32,256]{1,0:T(8,128)S(1)}, f32[32,256]{1,0:T(8,128)S(1)}, u32[]{:S(2)}, u32[]{:S(2)}) collective-permute-start(f32[32,256]{1,0:T(8,128)S(1)} %bitcast.6), channel_id=1, source_target_pairs={{0,1},{1,0},{2,3},{3,2},{4,5},{5,4},{6,7},{7,6},{8,9},{9,8},{10,11... | collective-permute-start | bytes 98312 | tf_op jit(solution)/shard_map/ppermute | solution.py:386
  106.3 1.2 collective-permute-done.5.inner_other_ref
  107.5 0.9 add_grads.1
  108.4 6.9 %all-to-all-start.6 = ((f32[16,8,256]{2,1,0:T(8,128)}), f32[16,8,256]{2,1,0:T(8,128)S(1)}, u32[]{:S(2)}, u32[]{:S(2)}) async-start(f32[16,8,256]{2,1,0:T(8,128)} %add_grads.1), calls=%async_computation.6 | async-start | bytes 262144 | tf_op jit(solution)/shard_map/all_to_all | solution.py:374
  115.3 2.1 %first_steps.1.work_ref = f32[64,128]{1,0:T(8,128)S(1)} custom-call(f32[64,64]{1,0:T(8,128)S(1)} %get-tuple-element.21.gram_ref), custom_call_target="tpu_custom_call" | custom-call | flops 2097152 | bytes 49152 | tf_op jit(solution)/shard_map/first_steps/pallas_call | solution.py:297
  117.4 2.6 %all-to-all-done.6.shares_ref = f32[16,8,256]{2,1,0:T(8,128)S(1)} async-done(((f32[16,8,256]{2,1,0:T(8,128)}), f32[16,8,256]{2,1,0:T(8,128)S(1)}, u32[]{:S(2)}, u32[]{:S(2)}) %all-to-all-start.6) | async-done | bytes 131104 | tf_op jit(solution)/shard_map/all_to_all | solution.py:374
  120.0 0.7 summed_copies.9
  120.7 6.7 %all-to-all-start.7 = ((f32[16,8,256]{2,1,0:T(8,128)}), f32[16,8,256]{2,1,0:T(8,128)S(1)}, u32[]{:S(2)}, u32[]{:S(2)}) async-start(f32[16,8,256]{2,1,0:T(8,128)} %summed_copies.9), calls=%async_computation.7 | async-start | bytes 262144 | tf_op jit(solution)/shard_map/all_to_all | solution.py:374
  127.3 3.3 %inverse_factor.1.inverse_ref = f32[64,64]{1,0:T(8,128)S(1)} custom-call(f32[64,128]{1,0:T(8,128)S(1)} %first_steps.1.work_ref), custom_call_target="tpu_custom_call" | custom-call | flops 2097152 | bytes 49152 | tf_op jit(solution)/shard_map/inverse_factor/pallas_call | solution.py:316
  130.6 1.4 %all-to-all-done.7.gathered_ref = f32[16,8,256]{2,1,0:T(8,128)S(1)} async-done(((f32[16,8,256]{2,1,0:T(8,128)}), f32[16,8,256]{2,1,0:T(8,128)S(1)}, u32[]{:S(2)}, u32[]{:S(2)}) %all-to-all-start.7) | async-done | bytes 131104 | tf_op jit(solution)/shard_map/all_to_all | solution.py:374
  132.0 1.7 %finish.1 = (bf16[256,512]{1,0:T(8,128)(2,1)}, f32[64,512]{1,0:T(8,128)}) custom-call(s32[1]{0:T(128)} %bitcast.place_ref, s32[1]{0:T(128)} %bitcast.1.half_ref, f32[64,64]{1,0:T(8,128)S(1)} %inverse_factor.1.inverse_ref, f32[16,64,128]{2,1,0:T(8,128)S(1)} %all_to_all.43.left_ref.own_ref, f32[16,64,128]{2,1,0:T(8,128)S(1)} %collective-permute-done.4.other_ref, ...), custom_call_target="tpu_custom_call" | custom-call | flops 100663296 | bytes 131072 | tf_op jit(solution)/shard_map/finish/pallas_call | solution.py:345
  (8 shorter events, 0.1 us)
Async XLA Ops:
  4.8 34.5 %all-to-all-start = ((bf16[4,256,128]{2,1,0:T(8,128)(2,1)}), bf16[4,256,128]{2,1,0:T(8,128)(2,1)S(1)}, u32[]{:S(2)}, u32[]{:S(2)}) async-start(bf16[4,256,128]{2,1,0:T(8,128)(2,1)} %get-tuple-element.14), calls=%async_computation | async-start | bytes 524288 | tf_op jit(solution)/shard_map/all_to_all | solution.py:374
  22.3 3.9 %collective-permute-start = (f32[18,64,128]{2,1,0:T(8,128)S(1)}, f32[18,64,128]{2,1,0:T(8,128)S(1)}, u32[]{:S(2)}, u32[]{:S(2)}) collective-permute-start(f32[18,64,128]{2,1,0:T(8,128)S(1)} %get-tuple-element.16), channel_id=1, source_target_pairs={{0,1},{1,0},{2,3},{3,2},{4,5},{5,4},{6,7},{7,6},{8,9},{9,8},{10,11... | collective-permute-start | bytes 1769480 | tf_op jit(solution)/shard_map/ppermute | solution.py:386
  26.2 10.2 %collective-permute-start.3 = (f32[64,256]{1,0:T(8,128)S(1)}, f32[64,256]{1,0:T(8,128)S(1)}, u32[]{:S(2)}, u32[]{:S(2)}) collective-permute-start(f32[64,256]{1,0:T(8,128)S(1)} %added_tail.1.refs_0_), channel_id=1, source_target_pairs={{6,0},{0,2},{2,4},{4,6},{7,1},{1,3},{3,5},{5,7},{14,8},{8,10},{10,... | collective-permute-start | bytes 196616 | tf_op jit(solution)/shard_map/ppermute | solution.py:404
  29.2 9.7 %collective-permute-start.2 = (f32[64,256]{1,0:T(8,128)S(1)}, f32[64,256]{1,0:T(8,128)S(1)}, u32[]{:S(2)}, u32[]{:S(2)}) collective-permute-start(f32[64,256]{1,0:T(8,128)S(1)} %added_tail.1.refs_0_), channel_id=1, source_target_pairs={{4,0},{6,2},{0,4},{2,6},{5,1},{7,3},{1,5},{3,7},{12,8},{14,10},{8,... | collective-permute-start | bytes 196616 | tf_op jit(solution)/shard_map/ppermute | solution.py:404
  32.5 6.8 %collective-permute-start.1 = (f32[64,256]{1,0:T(8,128)S(1)}, f32[64,256]{1,0:T(8,128)S(1)}, u32[]{:S(2)}, u32[]{:S(2)}) collective-permute-start(f32[64,256]{1,0:T(8,128)S(1)} %added_tail.1.refs_0_), channel_id=1, source_target_pairs={{2,0},{4,2},{6,4},{0,6},{3,1},{5,3},{7,5},{1,7},{10,8},{12,10},{14... | collective-permute-start | bytes 196616 | tf_op jit(solution)/shard_map/ppermute | solution.py:404
  77.1 30.4 %copy-start = (bf16[256,512]{1,0:T(8,128)(2,1)S(1)}, bf16[256,512]{1,0:T(8,128)(2,1)}, u32[]{:S(2)}) copy-start(bf16[256,512]{1,0:T(8,128)(2,1)} %grads_ref.3) | copy-start | bytes 786436
  91.6 12.8 %all-to-all-start.5 = ((f32[8,32,256]{2,1,0:T(8,128)}), f32[8,32,256]{2,1,0:T(8,128)S(1)}, u32[]{:S(2)}, u32[]{:S(2)}) async-start(f32[8,32,256]{2,1,0:T(8,128)} %inner_products.1), calls=%async_computation.5 | async-start | bytes 524288 | tf_op jit(solution)/shard_map/all_to_all | solution.py:374
  96.1 3.8 %collective-permute-start.4 = (f32[16,64,128]{2,1,0:T(8,128)S(1)}, f32[16,64,128]{2,1,0:T(8,128)S(1)}, u32[]{:S(2)}, u32[]{:S(2)}) collective-permute-start(f32[16,64,128]{2,1,0:T(8,128)S(1)} %all_to_all.43.left_ref.own_ref), channel_id=1, source_target_pairs={{0,1},{1,0},{2,3},{3,2},{4,5},{5,4},{6,7},{7,6},{8,9},{9,8},{10,11... | collective-permute-start | bytes 1572872 | tf_op jit(solution)/shard_map/ppermute | solution.py:386
  104.4 3.1 %collective-permute-start.5 = (f32[32,256]{1,0:T(8,128)S(1)}, f32[32,256]{1,0:T(8,128)S(1)}, u32[]{:S(2)}, u32[]{:S(2)}) collective-permute-start(f32[32,256]{1,0:T(8,128)S(1)} %bitcast.6), channel_id=1, source_target_pairs={{0,1},{1,0},{2,3},{3,2},{4,5},{5,4},{6,7},{7,6},{8,9},{9,8},{10,11... | collective-permute-start | bytes 98312 | tf_op jit(solution)/shard_map/ppermute | solution.py:386
  108.4 11.6 %all-to-all-start.6 = ((f32[16,8,256]{2,1,0:T(8,128)}), f32[16,8,256]{2,1,0:T(8,128)S(1)}, u32[]{:S(2)}, u32[]{:S(2)}) async-start(f32[16,8,256]{2,1,0:T(8,128)} %add_grads.1), calls=%async_computation.6 | async-start | bytes 262144 | tf_op jit(solution)/shard_map/all_to_all | solution.py:374
  120.7 11.4 %all-to-all-start.7 = ((f32[16,8,256]{2,1,0:T(8,128)}), f32[16,8,256]{2,1,0:T(8,128)S(1)}, u32[]{:S(2)}, u32[]{:S(2)}) async-start(f32[16,8,256]{2,1,0:T(8,128)} %summed_copies.9), calls=%async_computation.7 | async-start | bytes 262144 | tf_op jit(solution)/shard_map/all_to_all | solution.py:374

commit v7 on v6

--- a/solution.py
+++ b/solution.py
@@ -407,13 +407,13 @@
     left = add_activations(index_of("zl"), inner, columns, own, other)
 
     left = summed_copies(exchange(left, XY, opposite), near)
-    left = summed_copies(exchange(left, "zl", 1), far)
+    left = summed_copies(exchange(left, "zl", near // 2), far)
     left = summed_copies(exchange(left, "zh", far // 2), outer)
     own = exchange(left, XY, opposite)
     other = swapped(own)
 
     inner = inner_products(index_of("zl"), own, columns)
-    inner = summed_copies(exchange(inner, ("zl", "c"), 3), 1)[0]
+    inner = summed_copies(exchange(inner, ("zl", "c"), near + 1), 1)[0]
     right, gram = feedback_right(half, own, other, feedback, 4)
     inner, right = lax.optimization_barrier((inner, right))
     right = add_grads(half, inner, swapped(inner), grads_out, right, outer)

time: 135 us -> 133 us (0.985)
  transfers between devices with their start and end apart: 10 -> 10, of which waited for: 8 -> 8; matrix products, arithmetic and copies ran while one was open for 0% -> 0% of each run, Pallas kernels for 6% -> 7%
where the time goes in v7:
time: 133 us; the launch traced here: 132 us
  starting transfers between devices  51.2 us (38%)
  blocking collectives  50.5 us (38%)
  Pallas kernels  17.4 us (13%)
  waiting for transfers between devices  12.2 us (9%)
    all_to_all x4, blocking collectives, exchange(): lax.all_to_all(value, axes, 0, 0, axis_index_groups=[order], tiled=True)  50.5 us
    all_to_all x4, starting transfers between devices, exchange(): lax.all_to_all(value, axes, 0, 0, axis_index_groups=[order], tiled=True)  35.2 us
    ppermute x3, starting transfers between devices, per_device(): lax.ppermute(inner, 'zl', [((i + j) % near, i) for i in range(near)])  10.1 us
    ppermute x3, starting transfers between devices, swapped(): return lax.ppermute(value, 'c', [(0, 1), (1, 0)])  5.87 us
    ppermute x3, waiting for transfers between devices, swapped(): return lax.ppermute(value, 'c', [(0, 1), (1, 0)])  4.88 us
    all_to_all x4, waiting for transfers between devices, exchange(): lax.all_to_all(value, axes, 0, 0, axis_index_groups=[order], tiled=True)  4.26 us
    pallas_call x1, Pallas kernels, left_products(): pl.pallas_call(kernel, in_specs=whole_specs(0) + [pl.BlockSpec(memory_spa...  4.21 us
    pallas_call x1, Pallas kernels, inverse_factor(): pl.pallas_call(kernel, out_shape=jax.ShapeDtypeStruct((rank, rank), F32),...  3.32 us
  transfers between devices with their start and end apart: 10, of which 8 were waited for; matrix products, arithmetic and copies ran while one was open for 0% of the time, Pallas kernels for 7%

profile of v7, /device:TPU:6, one launch (start us, length us, event | category | flops | bytes accessed | tf_op | source)
XLA Modules:
  0.0 132.1 jit_solution(11937221692575993000)
XLA Ops:
  0.6 4.2 %left_products.1 = (f32[64,256]{1,0:T(8,128)S(1)}, f32[16,64,128]{2,1,0:T(8,128)S(1)}, f32[18,64,128]{2,1,0:T(8,128)S(1)}, bf16[4,256,128]{2,1,0:T(8,128)(2,1)}) custom-call(s32[1]{0:T(128)} %bitcast.1.half_ref, f32[64,512]{1,0:T(8,128)} %bitcast.8, bf16[256,512]{1,0:T(8,128)(2,1)} %grads_ref.3, bf16[256,128]{1,0:T(8,128)(2,1)} %act_ref.1, ...), custom_call_target="tpu_custom_call" | custom-call | flops 805306368 | bytes 5242880 | tf_op jit(solution)/shard_map/left_products/pallas_call | solution.py:126
  4.8 17.5 %all-to-all-start = ((bf16[4,256,128]{2,1,0:T(8,128)(2,1)}), bf16[4,256,128]{2,1,0:T(8,128)(2,1)S(1)}, u32[]{:S(2)}, u32[]{:S(2)}) async-start(bf16[4,256,128]{2,1,0:T(8,128)(2,1)} %get-tuple-element.14), calls=%async_computation | async-start | bytes 524288 | tf_op jit(solution)/shard_map/all_to_all | solution.py:374
  22.3 1.9 %collective-permute-start = (f32[18,64,128]{2,1,0:T(8,128)S(1)}, f32[18,64,128]{2,1,0:T(8,128)S(1)}, u32[]{:S(2)}, u32[]{:S(2)}) collective-permute-start(f32[18,64,128]{2,1,0:T(8,128)S(1)} %get-tuple-element.16), channel_id=1, source_target_pairs={{0,1},{1,0},{2,3},{3,2},{4,5},{5,4},{6,7},{7,6},{8,9},{9,8},{10,11... | collective-permute-start | bytes 1769480 | tf_op jit(solution)/shard_map/ppermute | solution.py:386
  24.2 2.0 %collective-permute-done.two_ref.other_ref = f32[18,64,128]{2,1,0:T(8,128)S(1)} collective-permute-done((f32[18,64,128]{2,1,0:T(8,128)S(1)}, f32[18,64,128]{2,1,0:T(8,128)S(1)}, u32[]{:S(2)}, u32[]{:S(2)}) %collective-permute-start) | collective-permute-done | bytes 589856 | tf_op jit(solution)/shard_map/ppermute | solution.py:386
  26.2 2.9 %collective-permute-start.3 = (f32[64,256]{1,0:T(8,128)S(1)}, f32[64,256]{1,0:T(8,128)S(1)}, u32[]{:S(2)}, u32[]{:S(2)}) collective-permute-start(f32[64,256]{1,0:T(8,128)S(1)} %added_tail.1.refs_0_), channel_id=1, source_target_pairs={{6,0},{0,2},{2,4},{4,6},{7,1},{1,3},{3,5},{5,7},{14,8},{8,10},{10,... | collective-permute-start | bytes 196616 | tf_op jit(solution)/shard_map/ppermute | solution.py:404
  29.2 3.4 %collective-permute-start.2 = (f32[64,256]{1,0:T(8,128)S(1)}, f32[64,256]{1,0:T(8,128)S(1)}, u32[]{:S(2)}, u32[]{:S(2)}) collective-permute-start(f32[64,256]{1,0:T(8,128)S(1)} %added_tail.1.refs_0_), channel_id=1, source_target_pairs={{4,0},{6,2},{0,4},{2,6},{5,1},{7,3},{1,5},{3,7},{12,8},{14,10},{8,... | collective-permute-start | bytes 196616 | tf_op jit(solution)/shard_map/ppermute | solution.py:404
  32.5 3.8 %collective-permute-start.1 = (f32[64,256]{1,0:T(8,128)S(1)}, f32[64,256]{1,0:T(8,128)S(1)}, u32[]{:S(2)}, u32[]{:S(2)}) collective-permute-start(f32[64,256]{1,0:T(8,128)S(1)} %added_tail.1.refs_0_), channel_id=1, source_target_pairs={{2,0},{4,2},{6,4},{0,6},{3,1},{5,3},{7,5},{1,7},{10,8},{12,10},{14... | collective-permute-start | bytes 196616 | tf_op jit(solution)/shard_map/ppermute | solution.py:404
  36.4 2.5 %collective-permute-done.2.refs_2_ = f32[64,256]{1,0:T(8,128)S(1)} collective-permute-done((f32[64,256]{1,0:T(8,128)S(1)}, f32[64,256]{1,0:T(8,128)S(1)}, u32[]{:S(2)}, u32[]{:S(2)}) %collective-permute-start.2) | collective-permute-done | bytes 65568 | tf_op jit(solution)/shard_map/ppermute | solution.py:404
  38.9 0.5 collective-permute-done.1.refs_1_
  39.4 0.2 add_activations.1
  39.6 13.5 %all_to_all.40.shares_ref = f32[16,64,128]{2,1,0:T(8,128)S(1)} all-to-all(f32[16,64,128]{2,1,0:T(8,128)S(1)} %add_activations.1), channel_id=1, replica_groups={{320,352,384,416,448,480,0,32,64,96,128,160,192,224,256,288},{321,353,3..., dimensions={0} | all-to-all | bytes 1048576 | tf_op jit(solution)/shard_map/all_to_all | solution.py:374
  53.2 7.8 %all_to_all.41.shares_ref = f32[4,64,128]{2,1,0:T(8,128)S(1)} all-to-all(f32[4,64,128]{2,1,0:T(8,128)S(1)} %summed_copies.5), channel_id=1, replica_groups={{4,6,0,2},{5,7,1,3},{12,14,8,10},{13,15,9,11},{20,22,16,18},{21,23,17,1..., dimensions={0} | all-to-all | bytes 262144 | tf_op jit(solution)/shard_map/all_to_all | solution.py:374
  61.0 16.0 %all_to_all.42.shares_ref = f32[4,64,128]{2,1,0:T(8,128)S(1)} all-to-all(f32[4,64,128]{2,1,0:T(8,128)S(1)} %summed_copies.6), channel_id=1, replica_groups={{16,24,0,8},{17,25,1,9},{18,26,2,10},{19,27,3,11},{20,28,4,12},{21,29,5..., dimensions={0} | all-to-all | bytes 262144 | tf_op jit(solution)/shard_map/all_to_all | solution.py:374
  77.0 0.0 copy-start
  77.0 13.2 %all_to_all.43.left_ref.own_ref = f32[16,64,128]{2,1,0:T(8,128)S(1)} all-to-all(f32[16,64,128]{2,1,0:T(8,128)S(1)} %summed_copies.7), channel_id=1, replica_groups={{320,352,384,416,448,480,0,32,64,96,128,160,192,224,256,288},{321,353,3..., dimensions={0} | all-to-all | bytes 1048576 | tf_op jit(solution)/shard_map/all_to_all | solution.py:374
  90.2 1.0 inner_products.1
  91.2 4.2 %all-to-all-start.5 = ((f32[8,32,256]{2,1,0:T(8,128)}), f32[8,32,256]{2,1,0:T(8,128)S(1)}, u32[]{:S(2)}, u32[]{:S(2)}) async-start(f32[8,32,256]{2,1,0:T(8,128)} %inner_products.1), calls=%async_computation.5 | async-start | bytes 524288 | tf_op jit(solution)/shard_map/all_to_all | solution.py:374
  95.4 2.0 %collective-permute-start.4 = (f32[16,64,128]{2,1,0:T(8,128)S(1)}, f32[16,64,128]{2,1,0:T(8,128)S(1)}, u32[]{:S(2)}, u32[]{:S(2)}) collective-permute-start(f32[16,64,128]{2,1,0:T(8,128)S(1)} %all_to_all.43.left_ref.own_ref), channel_id=1, source_target_pairs={{0,1},{1,0},{2,3},{3,2},{4,5},{5,4},{6,7},{7,6},{8,9},{9,8},{10,11... | collective-permute-start | bytes 1572872 | tf_op jit(solution)/shard_map/ppermute | solution.py:386
  97.5 1.7 %collective-permute-done.4.other_ref = f32[16,64,128]{2,1,0:T(8,128)S(1)} collective-permute-done((f32[16,64,128]{2,1,0:T(8,128)S(1)}, f32[16,64,128]{2,1,0:T(8,128)S(1)}, u32[]{:S(2)}, u32[]{:S(2)}) %collective-permute-start.4) | collective-permute-done | bytes 524320 | tf_op jit(solution)/shard_map/ppermute | solution.py:386
  99.2 3.3 %feedback_right.1 = (f32[64,512]{1,0:T(8,128)S(1)}, f32[64,64]{1,0:T(8,128)S(1)}) custom-call(s32[1]{0:T(128)} %bitcast.1.half_ref, f32[16,64,128]{2,1,0:T(8,128)S(1)} %all_to_all.43.left_ref.own_ref, f32[16,64,128]{2,1,0:T(8,128)S(1)} %collective-permute-done.4.other_ref, bf16[4096,512]{1,0:T(8,128)(2,1)} %feed_ref.3), custom_call_target="tpu_custom_call" | custom-call | flops 1107296256 | bytes 4194304 | tf_op jit(solution)/shard_map/feedback_right/pallas_call | solution.py:237
  102.5 0.2 all-to-all-done.5.shares_ref
  102.7 1.9 %collective-permute-start.5 = (f32[32,256]{1,0:T(8,128)S(1)}, f32[32,256]{1,0:T(8,128)S(1)}, u32[]{:S(2)}, u32[]{:S(2)}) collective-permute-start(f32[32,256]{1,0:T(8,128)S(1)} %bitcast.6), channel_id=1, source_target_pairs={{0,1},{1,0},{2,3},{3,2},{4,5},{5,4},{6,7},{7,6},{8,9},{9,8},{10,11... | collective-permute-start | bytes 98312 | tf_op jit(solution)/shard_map/ppermute | solution.py:386
  104.7 1.2 collective-permute-done.5.inner_other_ref
  105.8 0.9 add_grads.1
  106.7 6.9 %all-to-all-start.6 = ((f32[16,8,256]{2,1,0:T(8,128)}), f32[16,8,256]{2,1,0:T(8,128)S(1)}, u32[]{:S(2)}, u32[]{:S(2)}) async-start(f32[16,8,256]{2,1,0:T(8,128)} %add_grads.1), calls=%async_computation.6 | async-start | bytes 262144 | tf_op jit(solution)/shard_map/all_to_all | solution.py:374
  113.6 2.1 %first_steps.1.work_ref = f32[64,128]{1,0:T(8,128)S(1)} custom-call(f32[64,64]{1,0:T(8,128)S(1)} %get-tuple-element.21.gram_ref), custom_call_target="tpu_custom_call" | custom-call | flops 2097152 | bytes 49152 | tf_op jit(solution)/shard_map/first_steps/pallas_call | solution.py:297
  115.7 2.6 %all-to-all-done.6.shares_ref = f32[16,8,256]{2,1,0:T(8,128)S(1)} async-done(((f32[16,8,256]{2,1,0:T(8,128)}), f32[16,8,256]{2,1,0:T(8,128)S(1)}, u32[]{:S(2)}, u32[]{:S(2)}) %all-to-all-start.6) | async-done | bytes 131104 | tf_op jit(solution)/shard_map/all_to_all | solution.py:374
  118.3 0.7 summed_copies.9
  119.0 6.7 %all-to-all-start.7 = ((f32[16,8,256]{2,1,0:T(8,128)}), f32[16,8,256]{2,1,0:T(8,128)S(1)}, u32[]{:S(2)}, u32[]{:S(2)}) async-start(f32[16,8,256]{2,1,0:T(8,128)} %summed_copies.9), calls=%async_computation.7 | async-start | bytes 262144 | tf_op jit(solution)/shard_map/all_to_all | solution.py:374
  125.7 3.3 %inverse_factor.1.inverse_ref = f32[64,64]{1,0:T(8,128)S(1)} custom-call(f32[64,128]{1,0:T(8,128)S(1)} %first_steps.1.work_ref), custom_call_target="tpu_custom_call" | custom-call | flops 2097152 | bytes 49152 | tf_op jit(solution)/shard_map/inverse_factor/pallas_call | solution.py:316
  129.0 1.4 %all-to-all-done.7.gathered_ref = f32[16,8,256]{2,1,0:T(8,128)S(1)} async-done(((f32[16,8,256]{2,1,0:T(8,128)}), f32[16,8,256]{2,1,0:T(8,128)S(1)}, u32[]{:S(2)}, u32[]{:S(2)}) %all-to-all-start.7) | async-done | bytes 131104 | tf_op jit(solution)/shard_map/all_to_all | solution.py:374
  130.4 1.7 %finish.1 = (bf16[256,512]{1,0:T(8,128)(2,1)}, f32[64,512]{1,0:T(8,128)}) custom-call(s32[1]{0:T(128)} %bitcast.place_ref, s32[1]{0:T(128)} %bitcast.1.half_ref, f32[64,64]{1,0:T(8,128)S(1)} %inverse_factor.1.inverse_ref, f32[16,64,128]{2,1,0:T(8,128)S(1)} %all_to_all.43.left_ref.own_ref, f32[16,64,128]{2,1,0:T(8,128)S(1)} %collective-permute-done.4.other_ref, ...), custom_call_target="tpu_custom_call" | custom-call | flops 100663296 | bytes 131072 | tf_op jit(solution)/shard_map/finish/pallas_call | solution.py:345
  (8 shorter events, 0.1 us)
Async XLA Ops:
  4.8 34.5 %all-to-all-start = ((bf16[4,256,128]{2,1,0:T(8,128)(2,1)}), bf16[4,256,128]{2,1,0:T(8,128)(2,1)S(1)}, u32[]{:S(2)}, u32[]{:S(2)}) async-start(bf16[4,256,128]{2,1,0:T(8,128)(2,1)} %get-tuple-element.14), calls=%async_computation | async-start | bytes 524288 | tf_op jit(solution)/shard_map/all_to_all | solution.py:374
  22.3 3.9 %collective-permute-start = (f32[18,64,128]{2,1,0:T(8,128)S(1)}, f32[18,64,128]{2,1,0:T(8,128)S(1)}, u32[]{:S(2)}, u32[]{:S(2)}) collective-permute-start(f32[18,64,128]{2,1,0:T(8,128)S(1)} %get-tuple-element.16), channel_id=1, source_target_pairs={{0,1},{1,0},{2,3},{3,2},{4,5},{5,4},{6,7},{7,6},{8,9},{9,8},{10,11... | collective-permute-start | bytes 1769480 | tf_op jit(solution)/shard_map/ppermute | solution.py:386
  26.2 10.2 %collective-permute-start.3 = (f32[64,256]{1,0:T(8,128)S(1)}, f32[64,256]{1,0:T(8,128)S(1)}, u32[]{:S(2)}, u32[]{:S(2)}) collective-permute-start(f32[64,256]{1,0:T(8,128)S(1)} %added_tail.1.refs_0_), channel_id=1, source_target_pairs={{6,0},{0,2},{2,4},{4,6},{7,1},{1,3},{3,5},{5,7},{14,8},{8,10},{10,... | collective-permute-start | bytes 196616 | tf_op jit(solution)/shard_map/ppermute | solution.py:404
  29.2 9.7 %collective-permute-start.2 = (f32[64,256]{1,0:T(8,128)S(1)}, f32[64,256]{1,0:T(8,128)S(1)}, u32[]{:S(2)}, u32[]{:S(2)}) collective-permute-start(f32[64,256]{1,0:T(8,128)S(1)} %added_tail.1.refs_0_), channel_id=1, source_target_pairs={{4,0},{6,2},{0,4},{2,6},{5,1},{7,3},{1,5},{3,7},{12,8},{14,10},{8,... | collective-permute-start | bytes 196616 | tf_op jit(solution)/shard_map/ppermute | solution.py:404
  32.5 6.8 %collective-permute-start.1 = (f32[64,256]{1,0:T(8,128)S(1)}, f32[64,256]{1,0:T(8,128)S(1)}, u32[]{:S(2)}, u32[]{:S(2)}) collective-permute-start(f32[64,256]{1,0:T(8,128)S(1)} %added_tail.1.refs_0_), channel_id=1, source_target_pairs={{2,0},{4,2},{6,4},{0,6},{3,1},{5,3},{7,5},{1,7},{10,8},{12,10},{14... | collective-permute-start | bytes 196616 | tf_op jit(solution)/shard_map/ppermute | solution.py:404
  77.0 28.8 %copy-start = (bf16[256,512]{1,0:T(8,128)(2,1)S(1)}, bf16[256,512]{1,0:T(8,128)(2,1)}, u32[]{:S(2)}) copy-start(bf16[256,512]{1,0:T(8,128)(2,1)} %grads_ref.3) | copy-start | bytes 786436
  91.2 11.5 %all-to-all-start.5 = ((f32[8,32,256]{2,1,0:T(8,128)}), f32[8,32,256]{2,1,0:T(8,128)S(1)}, u32[]{:S(2)}, u32[]{:S(2)}) async-start(f32[8,32,256]{2,1,0:T(8,128)} %inner_products.1), calls=%async_computation.5 | async-start | bytes 524288 | tf_op jit(solution)/shard_map/all_to_all | solution.py:374
  95.4 3.8 %collective-permute-start.4 = (f32[16,64,128]{2,1,0:T(8,128)S(1)}, f32[16,64,128]{2,1,0:T(8,128)S(1)}, u32[]{:S(2)}, u32[]{:S(2)}) collective-permute-start(f32[16,64,128]{2,1,0:T(8,128)S(1)} %all_to_all.43.left_ref.own_ref), channel_id=1, source_target_pairs={{0,1},{1,0},{2,3},{3,2},{4,5},{5,4},{6,7},{7,6},{8,9},{9,8},{10,11... | collective-permute-start | bytes 1572872 | tf_op jit(solution)/shard_map/ppermute | solution.py:386
  102.7 3.1 %collective-permute-start.5 = (f32[32,256]{1,0:T(8,128)S(1)}, f32[32,256]{1,0:T(8,128)S(1)}, u32[]{:S(2)}, u32[]{:S(2)}) collective-permute-start(f32[32,256]{1,0:T(8,128)S(1)} %bitcast.6), channel_id=1, source_target_pairs={{0,1},{1,0},{2,3},{3,2},{4,5},{5,4},{6,7},{7,6},{8,9},{9,8},{10,11... | collective-permute-start | bytes 98312 | tf_op jit(solution)/shard_map/ppermute | solution.py:386
  106.7 11.6 %all-to-all-start.6 = ((f32[16,8,256]{2,1,0:T(8,128)}), f32[16,8,256]{2,1,0:T(8,128)S(1)}, u32[]{:S(2)}, u32[]{:S(2)}) async-start(f32[16,8,256]{2,1,0:T(8,128)} %add_grads.1), calls=%async_computation.6 | async-start | bytes 262144 | tf_op jit(solution)/shard_map/all_to_all | solution.py:374
  119.0 11.4 %all-to-all-start.7 = ((f32[16,8,256]{2,1,0:T(8,128)}), f32[16,8,256]{2,1,0:T(8,128)S(1)}, u32[]{:S(2)}, u32[]{:S(2)}) async-start(f32[16,8,256]{2,1,0:T(8,128)} %summed_copies.9), calls=%async_computation.7 | async-start | bytes 262144 | tf_op jit(solution)/shard_map/all_to_all | solution.py:374
